TPU v7x, 256 devices: a whole 4x4x8 slice. The times are simulated.
256 devices in a mesh: dp: 16 (over z, y_hi), tensor: 16 (over x, y_lo, core).
Axes of the slice: x: 4, y: 4 (y_hi: 2, y_lo: 2; y = y_hi * 2 + y_lo), z: 8, core: 2. Of those that a mesh axis runs over, the one named last changes fastest.
Arguments:
- inputs: bfloat16 [48, 2, 128, 4096], P('dp', None, None, 'tensor'), may hold values from -6 to 6
- cotangent: bfloat16 [48, 2, 128, 4096], P('dp', None, None, 'tensor'), may hold values from -6 to 6
- gate_pre: bfloat16 [48, 2, 128, 16384], P('dp', None, None, 'tensor'), may hold values from -6 to 6
- up_out: bfloat16 [48, 2, 128, 16384], P('dp', None, None, 'tensor'), may hold values from -6 to 6
- w_down: bfloat16 [16384, 4096], P('tensor'), may hold values from -0.046875 to 0.046875
- up_in_basis: bfloat16 [4096, 64], replicated, may hold values from -0.09375 to 0.09375
- up_out_basis: bfloat16 [16384, 64], P('tensor'), may hold values from -0.046875 to 0.046875
- down_in_basis: bfloat16 [16384, 64], P('tensor'), may hold values from -0.046875 to 0.046875
- down_out_basis: bfloat16 [4096, 64], replicated, may hold values from -0.09375 to 0.09375
- lengths: int32 [48, 2], P('dp'), may hold values from 32 to 128, as said below
- margins: float32 [48], P('dp'), may hold values from -4 to 4
- curvature: float32 [2, 64, 64], replicated, may hold values from 0.1 to 10
Outputs:
- train_grads: float32 [32, 2, 64, 64], P('dp', None, 'tensor')
- scores: float32 [16, 32], P(None, 'dp')
Inputs may be any that keep to these rules, and one draw needn't show every extreme that they name: `lengths`: each entry counts the live tokens of a sequence; positions from it on are padding and take no part. In every draw some sequence is full and some has 32 live tokens.
All inputs are finite; a program needn't handle non-finite values.
Results may differ from a plain program's by a relative error of at most 0.0043.
Values may be sent and summed in bfloat16 or wider, within the bound.
No kernel may reach another device: no remote copies, remote signals or barrier semaphores. Data moves between devices by JAX's collectives and lax.ppermute only.
A program may use at most 128 MiB of HBM per device.

v0:
```python
import jax
import jax.numpy as jnp
from jax import lax
from jax.sharding import PartitionSpec as P

QUERY_DEV = 1


highest = lax.Precision.HIGHEST
epsilon = 1e-06


def tile_scores(query_part, train_part):
    flat_query = query_part.reshape(query_part.shape[0], -1)
    flat_train = train_part.reshape(train_part.shape[0], -1)
    return lax.dot_general(
        flat_query,
        flat_train,
        (((1,), (1,)), ((), ())),
        precision=highest,
        preferred_element_type=jnp.float32,
    )


def circulate_scores(query_block, weighted):
    return tile_scores(lax.all_gather(query_block, "dp", axis=0, tiled=True), weighted)


def shards(
    inputs,
    cotangent,
    gate_pre,
    up_out,
    w_down,
    up_in_basis,
    up_out_basis,
    down_in_basis,
    down_out_basis,
    lengths,
    margins,
    curvature,
):
    pair_count = inputs.shape[0]
    seq_len = inputs.shape[2]
    local_width = inputs.shape[3]
    hidden_local = gate_pre.shape[3]
    proj_size = up_in_basis.shape[1]
    token_count = pair_count * 2 * seq_len
    flat_inputs = inputs.reshape(token_count, local_width)
    flat_cotangent = cotangent.reshape(token_count, local_width)
    basis_rows = up_in_basis
    input_next = jnp.dot(
        lax.all_gather(flat_inputs, "tensor", axis=1, tiled=True),
        basis_rows,
        preferred_element_type=jnp.float32,
    )
    shard_piece = lax.all_gather(flat_cotangent, "tensor", axis=1, tiled=True)
    basis_rows = down_out_basis
    hidden_next = lax.dot_general(
        shard_piece, w_down, (((1,), (1,)), ((), ())), preferred_element_type=jnp.float32
    )
    proj_next = jnp.dot(shard_piece, basis_rows, preferred_element_type=jnp.float32)
    hidden_next, proj_next = (hidden_next, proj_next)
    input_proj = input_next
    cotangent_proj = proj_next
    gate_value = jax.nn.silu(gate_pre.reshape(token_count, hidden_local).astype(jnp.float32))
    up_grad = (hidden_next * gate_value).astype(jnp.bfloat16)
    activation = (
        gate_value * up_out.reshape(token_count, hidden_local).astype(jnp.float32)
    ).astype(jnp.bfloat16)
    up_proj = jnp.dot(up_grad, up_out_basis, preferred_element_type=jnp.float32)
    act_proj = jnp.dot(activation, down_in_basis, preferred_element_type=jnp.float32)
    positions = jnp.arange(seq_len, dtype=jnp.int32)
    live = (
        (positions[None, None, :] < lengths[:, :, None])
        .astype(jnp.float32)
        .reshape(pair_count * 2, seq_len, 1)
    )
    input_proj = input_proj.reshape(pair_count * 2, seq_len, proj_size) * live
    cotangent_proj = cotangent_proj.reshape(pair_count * 2, seq_len, proj_size) * live
    up_proj = up_proj.reshape(pair_count * 2, seq_len, proj_size)
    act_proj = act_proj.reshape(pair_count * 2, seq_len, proj_size)
    seq_up = jnp.einsum("sti,stj->sij", input_proj, up_proj, precision=highest)
    seq_down = jnp.einsum("sti,stj->sij", act_proj, cotangent_proj, precision=highest)
    seq_grads = jnp.stack([seq_up, seq_down], axis=1).reshape(
        pair_count, 2, 2, proj_size, proj_size
    )
    pair_weight = (1.0 / (1.0 + jnp.exp(margins)))[:, None, None, None]
    partial_grads = pair_weight * (seq_grads[:, 0] - seq_grads[:, 1])
    train_count = pair_count - QUERY_DEV
    row_share = proj_size // lax.axis_size("tensor")
    row_offset = lax.axis_index("tensor") * row_share
    summed = lax.psum(partial_grads, "tensor")
    train_block = summed[:train_count]
    query_block = summed[train_count:]
    weighted = curvature[None] * train_block
    self_terms = jnp.sum(weighted * train_block, axis=(1, 2, 3))
    cross = circulate_scores(query_block, weighted)
    train_out = lax.dynamic_slice_in_dim(train_block, row_offset, row_share, 2)
    scores = cross / jnp.sqrt(self_terms + epsilon)[None, :]
    return (train_out, scores)


def solution(mesh):
    return jax.shard_map(
        shards,
        mesh=mesh,
        in_specs=(
            P("dp", None, None, "tensor"),
            P("dp", None, None, "tensor"),
            P("dp", None, None, "tensor"),
            P("dp", None, None, "tensor"),
            P("tensor", None),
            P(),
            P("tensor", None),
            P("tensor", None),
            P(),
            P("dp", None),
            P("dp"),
            P(),
        ),
        out_specs=(P("dp", None, "tensor", None), P(None, "dp")),
        check_vma=False,
    )
```

profile of v0, /device:TPU:6, one launch (start us, length us, event | category | flops | bytes accessed | tf_op | source)
XLA Modules:
  0.0 322.0 jit_solution(11115425916471424408)
XLA Ops:
  7.2 0.7 all-gather.3.cloned.1.call-update
  8.0 0.7 all-gather.5.cloned.1.call-update
  8.7 0.0 all-reduce.2.cloned.1.call-start
  8.7 0.8 copy.28
  9.5 0.1 lt.23
  9.6 0.7 add_divide_fusion
  10.2 0.1 fusion.23
  10.3 2.9 fusion
  13.2 0.6 fusion.20
  13.8 53.6 %all-gather.3.cloned.1.call-done = bf16[768,4096]{1,0:T(8,128)(2,1)} async-done(((bf16[768,256]{1,0:T(8,128)(2,1)}), bf16[768,4096]{1,0:T(8,128)(2,1)}) %all-gather.3.cloned.1.call-update) | async-done | bytes 6291472 | tf_op jit(solution)/shard_map/all_gather | solution.py:53
  67.4 4.8 %fusion.24 = f32[768,64]{0,1:T(8,128)S(1)} fusion(bf16[768,4096]{1,0:T(8,128)(2,1)} %all-gather.3.cloned.1.call-done, bf16[4096,64]{0,1:T(8,128)(2,1)S(1)} %copy-done), kind=kOutput, calls=%fused_computation.43 | convolution fusion | flops 402653184 | bytes 7012352 | tf_op jit(solution)/shard_map/dot_general | solution.py:52
  72.2 51.9 %all-gather.5.cloned.1.call-done = bf16[768,4096]{1,0:T(8,128)(2,1)} async-done(((bf16[768,256]{1,0:T(8,128)(2,1)}), bf16[768,4096]{1,0:T(8,128)(2,1)}) %all-gather.5.cloned.1.call-update) | async-done | bytes 6291472 | tf_op jit(solution)/shard_map/all_gather | solution.py:57
  124.1 4.8 %fusion.25 = f32[768,64]{0,1:T(8,128)S(1)} fusion(bf16[768,4096]{1,0:T(8,128)(2,1)} %all-gather.5.cloned.1.call-done, bf16[4096,64]{0,1:T(8,128)(2,1)S(1)} %copy-done.2), kind=kOutput, calls=%fused_computation.44 | convolution fusion | flops 402653184 | bytes 7012352 | tf_op jit(solution)/shard_map/dot_general | solution.py:62
  129.0 11.4 %fusion.8 = bf16[768,1024]{1,0:T(8,128)(2,1)S(1)} fusion(bf16[3,2,128,1024]{3,2,1,0:T(8,128)(2,1)S(1)} %copy-done.1, bf16[768,4096]{1,0:T(8,128)(2,1)} %all-gather.5.cloned.1.call-done, bf16[1024,4096]{1,0:T(8,128)(2,1)} %param.16), kind=kOutput, calls=%fused_computation.13 | convolution fusion | flops 6447955968 | bytes 17825792 | tf_op jit(solution)/shard_map/dot_general | solution.py:59
  140.4 0.6 convolution_bitcast_fusion
  141.1 0.4 fusion.12
  141.5 0.4 fusion.17
  142.0 0.8 fusion.16
  142.8 114.4 %all-reduce.2.cloned.1.call-done = f32[3,2,64,64]{3,2,1,0:T(8,128)} async-done(((f32[3,2,64,64]{3,2,1,0:T(8,128)}), f32[3,2,64,64]{3,2,1,0:T(8,128)}) %all-reduce.2.cloned.1.call-update) | async-done | bytes 98320 | tf_op jit(solution)/shard_map/psum | solution.py:93
  257.2 1.0 multiply_reduce_fusion
  258.2 0.8 slice.19
  259.1 53.4 %all_gather.11 = f32[16,2,64,64]{3,2,1,0:T(8,128)S(1)} all-gather(f32[1,2,64,64]{3,2,1,0:T(8,128)S(1)} %slice.19), channel_id=1, replica_groups=mesh['dp'=16,'tensor'=16] {'dp'}, dimensions={0}, use_global_device_ids=true | all-gather | bytes 557056 | tf_op jit(solution)/shard_map/all_gather | solution.py:26
  312.4 0.6 constant_dynamic-slice_fusion
  313.0 2.4 fusion.9
  (20 shorter events, 0.3 us)
Async XLA Ops:
  7.2 60.2 %copy-start = (bf16[4096,64]{0,1:T(8,128)(2,1)S(1)}, bf16[4096,64]{0,1:T(8,128)(2,1)}, u32[]{:S(2)}) copy-start(bf16[4096,64]{0,1:T(8,128)(2,1)} %param.17) | copy-start | bytes 1572868
  7.2 6.0 %copy-start.3 = (bf16[1024,64]{0,1:T(8,128)(2,1)S(1)}, bf16[1024,64]{0,1:T(8,128)(2,1)}, u32[]{:S(2)}) copy-start(bf16[1024,64]{0,1:T(8,128)(2,1)} %param.19) | copy-start | bytes 393220
  7.2 60.2 %all-gather.3.cloned.1.call-start = ((), (), s32[]{:S(2)}) async-start(), calls=%async_computation | async-start | bytes 6684672 | tf_op jit(solution)/shard_map/all_gather | solution.py:53
  7.9 116.2 %all-gather.5.cloned.1.call-start = ((), (), s32[]{:S(2)}) async-start(), calls=%async_computation.1 | async-start | bytes 6684672 | tf_op jit(solution)/shard_map/all_gather | solution.py:57
  8.7 248.5 %all-reduce.2.cloned.1.call-start = ((), (), s32[]{:S(2)}) async-start(), calls=%async_computation.2 | async-start | bytes 393216 | tf_op jit(solution)/shard_map/psum | solution.py:93
  13.8 110.3 %copy-start.2 = (bf16[4096,64]{0,1:T(8,128)(2,1)S(1)}, bf16[4096,64]{0,1:T(8,128)(2,1)}, u32[]{:S(2)}) copy-start(bf16[4096,64]{0,1:T(8,128)(2,1)} %param.20) | copy-start | bytes 1572868
  72.2 56.7 %copy-start.1 = (bf16[3,2,128,1024]{3,2,1,0:T(8,128)(2,1)S(1)}, bf16[3,2,128,1024]{3,2,1,0:T(8,128)(2,1)}, u32[]{:S(2)}) copy-start(bf16[3,2,128,1024]{3,2,1,0:T(8,128)(2,1)} %param.14) | copy-start | bytes 4718596
  129.0 11.4 %copy-start.4 = (bf16[1024,64]{0,1:T(8,128)(2,1)S(1)}, bf16[1024,64]{0,1:T(8,128)(2,1)}, u32[]{:S(2)}) copy-start(bf16[1024,64]{0,1:T(8,128)(2,1)} %param.18) | copy-start | bytes 393220
  140.4 116.8 %copy-start.5 = (f32[2,64,64]{2,1,0:T(8,128)S(1)}, f32[2,64,64]{2,1,0:T(8,128)}, u32[]{:S(2)}) copy-start(f32[2,64,64]{2,1,0:T(8,128)} %param.23) | copy-start | bytes 98308
Sparse Core Ops, SparseCore 0:
  9.8 57.5 all-gather.2
  69.1 54.9 all-gather.4
  142.9 114.2 all-reduce.1
where the time goes:
time: 322 us
  waiting for transfers between devices  221 us (69%)
  blocking collectives  53.4 us (17%)
  matrix products  25.5 us (8%)
  between operations  13.9 us (4%)
  other arithmetic  5.46 us (2%)
    psum x1, waiting for transfers between devices, shards(): summed = lax.psum(partial_grads, 'tensor')  114 us
    all_gather x1, waiting for transfers between devices, shards(): lax.all_gather(flat_inputs, 'tensor', axis=1, tiled=True)  53.6 us
    all_gather x1, blocking collectives, circulate_scores(): lax.all_gather(query_block, 'dp', axis=0, tiled=True)  53.4 us
    all_gather x1, waiting for transfers between devices, shards(): shard_piece = lax.all_gather(flat_cotangent, 'tensor', axis=1, tiled=True)  51.9 us
    dot_general x1, matrix products, shards(): lax.dot_general(shard_piece, w_down, (((1,), (1,)), ((), ())), preferred_...  11.4 us
  transfers between devices with their start and end apart: 3, of which 3 were waited for; matrix products, arithmetic and copies ran while one was open for 3% of the time, Pallas kernels for 0%

commit v1 on v0

v1 whole, which is shorter than its diff:
```python
import jax
import jax.numpy as jnp
from jax import lax
from jax.experimental import pallas as pl
from jax.experimental.pallas import tpu as pltpu
from jax.sharding import PartitionSpec as P

QUERY_DEV = 1
NX, NY, NC = 4, 2, 2
highest = lax.Precision.HIGHEST
epsilon = 1e-06
F32, BF16 = jnp.float32, jnp.bfloat16
VMEM_LIMIT = 56 * 1024 * 1024


def moves(step):
    pairs = []
    for x in range(NX):
        for y in range(NY):
            for c in range(NC):
                tx, ty, tc = step(x, y, c)
                source = (x * NY + y) * NC + c
                target = ((tx % NX) * NY + ty % NY) * NC + tc % NC
                pairs.append((source, target))
    return pairs


X_UP = moves(lambda x, y, c: (x + 1, y, c))
X_DOWN = moves(lambda x, y, c: (x - 1, y, c))
Y_SWAP = moves(lambda x, y, c: (x, y + 1, c))
CORE_SWAP = moves(lambda x, y, c: (x, y, c + 1))


def send(value, pairs):
    return lax.ppermute(value, "tensor", pairs)


def dot_t(a, b):
    return lax.dot_general(a, b, (((1,), (1,)), ((), ())), preferred_element_type=F32)


def columns_of_core(w_down, core):
    rows = w_down.shape[0]
    chips = NX * NY
    width = w_down.shape[1] // (chips * NC)

    def body(core_ref, w_ref, o_ref):
        o_ref[...] = w_ref[...]

    return pl.pallas_call(
        body,
        grid_spec=pltpu.PrefetchScalarGridSpec(
            num_scalar_prefetch=1,
            grid=(chips,),
            in_specs=[pl.BlockSpec((rows, width), lambda i, core_ref: (0, NC * i + core_ref[0]))],
            out_specs=pl.BlockSpec((rows, width), lambda i, core_ref: (0, i)),
        ),
        out_shape=jax.ShapeDtypeStruct((rows, chips * width), w_down.dtype),
        compiler_params=pltpu.CompilerParams(vmem_limit_bytes=VMEM_LIMIT),
        name="columns_of_core",
    )(core[None], w_down)


def stage(blocks, pieces, weights, other_weights, gate, other_gate, bases, row_block, tokens, last=None):
    shards_n = len(pieces)
    width = pieces[0][0].shape[1]
    hidden = gate.shape[1]
    chunk = 512
    steps = hidden // chunk
    basis, other_basis, out_basis = bases
    flat = [piece for shard in pieces for piece in shard]
    counts = [len(shard) for shard in pieces]
    pair_tokens = 256
    pairs = tokens // pair_tokens

    def body(blocks_ref, *refs):
        refs = list(refs)
        cots = []
        for count in counts:
            got = [refs.pop(0) for _ in range(count)]
            cots.append(got)
        own_w = [refs.pop(0) for _ in range(shards_n)]
        other_w = [refs.pop(0) for _ in range(shards_n)]
        out_bases = [refs.pop(0) for _ in range(shards_n)]
        gate_ref, other_gate_ref, basis_ref, other_basis_ref = refs[:4]
        refs = refs[4:]
        if last is not None:
            before_ref, left_ref, grads_ref, sums_ref = refs
        else:
            (sums_ref,) = refs
        step = pl.program_id(0)
        values = [
            got[0][...] if len(got) == 1 else jnp.concatenate([ref[...] for ref in got], axis=0)
            for got in cots
        ]

        @pl.when(step == 0)
        def _():
            first = before_ref[...] if last is not None else jnp.zeros(sums_ref.shape, F32)
            for value, ref in zip(values, out_bases):
                first = first + jnp.dot(value, ref[...], preferred_element_type=F32)
            sums_ref[...] = first

        total = sums_ref[...]
        for w_refs, g_ref, b_ref in ((own_w, gate_ref, basis_ref), (other_w, other_gate_ref, other_basis_ref)):
            grad = dot_t(values[0], w_refs[0][...])
            for value, ref in zip(values[1:], w_refs[1:]):
                grad = grad + dot_t(value, ref[...])
            gate_value = g_ref[...].astype(F32)
            gate_value = gate_value / (1.0 + jnp.exp(-gate_value))
            total = total + jnp.dot((grad * gate_value).astype(BF16), b_ref[...], preferred_element_type=F32)
        sums_ref[...] = total

        if last is not None:

            @pl.when(step == steps - 1)
            def _():
                half = lax.broadcasted_iota(jnp.int32, (64, 128), 1) < 64
                for pair in range(pairs):
                    rows = pl.ds(pair * pair_tokens, pair_tokens)
                    both = lax.dot_general(
                        left_ref[rows, :],
                        sums_ref[rows, :],
                        (((0,), (0,)), ((), ())),
                        precision=highest,
                        preferred_element_type=F32,
                    )
                    grads_ref[pair] = jnp.where(half, both[:64], both[64:])

    def whole(array):
        return pl.BlockSpec(array.shape, lambda i, blocks_ref: (0,) * array.ndim)

    def at(row, s):
        return lambda i, blocks_ref: (i, blocks_ref[row * shards_n + s])

    in_specs = [whole(piece) for piece in flat]
    operands = list(flat)
    for s in range(shards_n):
        in_specs.append(pl.BlockSpec((chunk, width), at(0, s)))
        operands.append(weights)
    for s in range(shards_n):
        in_specs.append(pl.BlockSpec((chunk, width), at(1, s)))
        operands.append(other_weights)
    for s in range(shards_n):
        in_specs.append(
            pl.BlockSpec((width, 128), lambda i, blocks_ref, s=s: (blocks_ref[s], 0))
        )
        operands.append(out_basis)
    for array in (gate, other_gate):
        in_specs.append(pl.BlockSpec((tokens, chunk), lambda i, blocks_ref: (row_block, i)))
        operands.append(array)
    for array in (basis, other_basis):
        in_specs.append(pl.BlockSpec((chunk, 128), lambda i, blocks_ref: (i, 0)))
        operands.append(array)
    sums_spec = pl.BlockSpec((tokens, 128), lambda i, blocks_ref: (0, 0))
    sums_shape = jax.ShapeDtypeStruct((tokens, 128), F32)
    out_specs, out_shape = sums_spec, sums_shape
    scratch = []
    if last is not None:
        before, left = last
        in_specs.append(sums_spec)
        operands.append(before)
        in_specs.append(pl.BlockSpec((tokens, 128), lambda i, blocks_ref: (row_block, 0)))
        operands.append(left)
        out_specs = pl.BlockSpec((pairs, 64, 128), lambda i, blocks_ref: (0, 0, 0))
        out_shape = jax.ShapeDtypeStruct((pairs, 64, 128), F32)
        scratch = [pltpu.VMEM((tokens, 128), F32)]
    flops = 4 * tokens * hidden * (shards_n * width + 128)
    return pl.pallas_call(
        body,
        grid_spec=pltpu.PrefetchScalarGridSpec(
            num_scalar_prefetch=1,
            grid=(steps,),
            in_specs=in_specs,
            out_specs=out_specs,
            scratch_shapes=scratch,
        ),
        out_shape=out_shape,
        compiler_params=pltpu.CompilerParams(vmem_limit_bytes=VMEM_LIMIT),
        cost_estimate=pl.CostEstimate(
            flops=flops,
            bytes_accessed=4 * shards_n * width * hidden + 4 * tokens * hidden,
            transcendentals=2 * tokens * hidden,
        ),
        name="stage_last" if last is not None else "stage_first",
    )(blocks, *operands)


def pack_tokens(value):
    tokens = value.shape[0]
    return value.reshape(16, 2, tokens // 32, 64).transpose(0, 2, 1, 3).reshape(16, tokens // 32, 128)


def unpack_tokens(value):
    rows = value.shape[1]
    return value.reshape(16, rows, 2, 64).transpose(0, 2, 1, 3).reshape(rows * 32, 64)


def shards(
    inputs,
    cotangent,
    gate_pre,
    up_out,
    w_down,
    up_in_basis,
    up_out_basis,
    down_in_basis,
    down_out_basis,
    lengths,
    margins,
    curvature,
):
    pair_count = inputs.shape[0]
    seq_len = inputs.shape[2]
    width = inputs.shape[3]
    hidden = gate_pre.shape[3]
    pair_tokens = 2 * seq_len
    token_count = pair_count * pair_tokens
    train_count = pair_count - QUERY_DEV
    train_tokens = train_count * pair_tokens
    query_tokens = QUERY_DEV * pair_tokens
    dp_size = lax.axis_size("dp")
    tensor_size = lax.axis_size("tensor")
    place = lax.axis_index("tensor")
    x, y, core = place // (NY * NC), (place // NC) % NY, place % NC

    flat_cotangent = cotangent.reshape(token_count, width)
    gate = gate_pre.reshape(token_count, hidden)
    query_own = flat_cotangent[train_tokens:]
    train_own = flat_cotangent[:train_tokens]

    def first_hop(own):
        return send(own, X_UP), send(own, X_DOWN), send(own, Y_SWAP)

    def second_hop(left, across):
        return send(left, X_UP), send(across, X_DOWN), send(left, Y_SWAP)

    query_left, query_right, query_across = first_hop(query_own)
    train_left, train_right, train_across = first_hop(train_own)

    other_gate = send(gate, CORE_SWAP)
    other_weights = send(columns_of_core(w_down, 1 - core), CORE_SWAP)
    padded_basis = jnp.pad(up_out_basis, ((0, 0), (0, 64)))
    other_basis = send(padded_basis, CORE_SWAP)
    padded_out_basis = jnp.pad(down_out_basis, ((0, 0), (64, 0)))
    bases = (padded_basis, other_basis, padded_out_basis)

    rows = lax.dynamic_slice_in_dim(up_in_basis, place * width, width, 0)
    partial_inputs = jnp.dot(inputs.reshape(token_count, width), rows, preferred_element_type=F32)
    pieces = lax.all_to_all(pack_tokens(partial_inputs), "tensor", 0, 0, tiled=True)
    mine = jnp.sum(pieces, axis=0)
    spread = jnp.broadcast_to(mine[None], (tensor_size, *mine.shape))
    input_proj = unpack_tokens(lax.all_to_all(spread, "tensor", 0, 0, tiled=True))

    gate_value = jax.nn.silu(gate.astype(F32))
    activation = (gate_value * up_out.reshape(token_count, hidden).astype(F32)).astype(BF16)
    act_proj = jnp.dot(activation, down_in_basis, preferred_element_type=F32)
    act_proj = act_proj + send(act_proj, CORE_SWAP)

    positions = jnp.arange(seq_len, dtype=jnp.int32)
    live = (positions[None, None, :] < lengths[:, :, None]).astype(F32)
    weight = 1.0 / (1.0 + jnp.exp(margins))
    factor = live * weight[:, None, None] * jnp.array([1.0, -1.0], F32)[None, :, None]
    left_factors = jnp.concatenate([input_proj, act_proj], axis=1) * factor.reshape(token_count, 1)

    chip = x * NY + y
    flipped = 1 - y

    def chip_at(dx, row):
        return ((x + dx) % NX) * NY + row

    near = jnp.stack([chip, chip_at(3, y), chip_at(1, y), chip_at(0, flipped)])
    far = jnp.stack([chip_at(2, y), chip_at(1, flipped), chip_at(3, flipped), chip_at(2, flipped)])
    near_blocks = jnp.concatenate([near * NC + core, near]).astype(jnp.int32)
    far_blocks = jnp.concatenate([far * NC + core, far]).astype(jnp.int32)
    query_block = train_tokens // query_tokens

    query_x2, query_pr, query_pl = second_hop(query_left, query_across)
    train_x2, train_pr, train_pl = second_hop(train_left, train_across)

    query_near = stage(
        near_blocks,
        [(query_own,), (query_left,), (query_right,), (query_across,)],
        w_down, other_weights, gate, other_gate, bases, query_block, query_tokens,
    )
    query_far = send(query_x2, Y_SWAP)
    train_near = stage(
        near_blocks,
        [(train_own,), (train_left,), (train_right,), (train_across,)],
        w_down, other_weights, gate, other_gate, bases, 0, train_tokens,
    )
    middle = train_tokens // 2
    train_far = (send(train_pl[:middle], X_UP), send(train_pr[middle:], X_DOWN))

    query_grads = stage(
        far_blocks,
        [(query_x2,), (query_pr,), (query_pl,), (query_far,)],
        w_down, other_weights, gate, other_gate, bases, query_block, query_tokens,
        (query_near, left_factors),
    )
    row_share = 64 // tensor_size
    query_out = jnp.broadcast_to(
        query_grads.reshape(1, tensor_size, row_share, 128), (dp_size, tensor_size, row_share, 128)
    ).reshape(dp_size * tensor_size, row_share, 128)
    query_parts = lax.all_to_all(query_out, ("dp", "tensor"), 0, 0, tiled=True)

    train_grads = stage(
        far_blocks,
        [(train_x2,), (train_pr,), (train_pl,), train_far],
        w_down, other_weights, gate, other_gate, bases, 0, train_tokens,
        (train_near, left_factors),
    )
    train_out = train_grads.reshape(train_count, tensor_size, row_share, 128).transpose(1, 0, 2, 3)
    train_parts = lax.all_to_all(
        train_out.reshape(tensor_size, train_count * row_share, 128), "tensor", 0, 0, tiled=True
    )
    train_rows = jnp.sum(train_parts, axis=0).reshape(train_count, row_share, 128)
    query_rows = jnp.sum(query_parts.reshape(dp_size, tensor_size, row_share, 128), axis=1)

    own_curvature = lax.dynamic_slice_in_dim(curvature, place * row_share, row_share, 1)
    own_curvature = own_curvature.transpose(1, 0, 2).reshape(row_share, 128)
    weighted = own_curvature[None] * train_rows
    self_part = jnp.sum(weighted * train_rows, axis=(1, 2))
    cross_part = jnp.sum(query_rows[:, None] * weighted[None], axis=(2, 3))
    sums = jnp.concatenate([cross_part.reshape(-1), self_part])
    sums = jnp.pad(sums, (0, 128 - sums.shape[0]))
    all_sums = lax.all_to_all(
        jnp.broadcast_to(sums[None, None], (tensor_size, 1, 128)), "tensor", 0, 0, tiled=True
    )
    sums = jnp.sum(all_sums, axis=(0, 1))
    cross = sums[: dp_size * train_count].reshape(dp_size, train_count)
    self_terms = sums[dp_size * train_count : dp_size * train_count + train_count]
    scores = cross / jnp.sqrt(self_terms + epsilon)[None, :]
    train_block = train_rows.reshape(train_count, row_share, 2, 64).transpose(0, 2, 1, 3)
    return train_block, scores


def solution(mesh):
    return jax.shard_map(
        shards,
        mesh=mesh,
        in_specs=(
            P("dp", None, None, "tensor"),
            P("dp", None, None, "tensor"),
            P("dp", None, None, "tensor"),
            P("dp", None, None, "tensor"),
            P("tensor", None),
            P(),
            P("tensor", None),
            P("tensor", None),
            P(),
            P("dp", None),
            P("dp"),
            P(),
        ),
        out_specs=(P("dp", None, "tensor", None), P(None, "dp")),
        check_vma=False,
    )
```

time: 322 us -> 144 us (0.45)
  the two profiles are of different devices: /device:TPU:6 before, /device:TPU:1 now
where the time goes in v1:
time: 144 us; the launch traced here: 143 us
  starting transfers between devices  55.1 us (38%)
  Pallas kernels  35.7 us (25%)
  waiting for transfers between devices  24.1 us (17%)
  local copies, waits for them, and re-layouts  21.1 us (15%)
  other arithmetic  5.19 us (4%)
    pallas_call x4, Pallas kernels, stage(): pl.pallas_call(body, grid_spec=pltpu.PrefetchScalarGridSpec(num_scalar_pr...  28.8 us
    ppermute x19, starting transfers between devices, send(): return lax.ppermute(value, 'tensor', pairs)  22.4 us
    all_to_all x1, waiting for transfers between devices, shards(): query_parts = lax.all_to_all(query_out, ('dp', 'tensor'), 0, 0, tiled=True)  19.2 us
    all_to_all x1, starting transfers between devices, shards(): query_parts = lax.all_to_all(query_out, ('dp', 'tensor'), 0, 0, tiled=True)  13.2 us
    pallas_call x1, Pallas kernels, columns_of_core(): pl.pallas_call(body, grid_spec=pltpu.PrefetchScalarGridSpec(num_scalar_pr...  6.85 us
    unnamed x55, local copies, waits for them, and re-layouts  6.62 us
    all_to_all x1, starting transfers between devices, shards(): lax.all_to_all(train_out.reshape(tensor_size, train_count * row_share, 12...  5.81 us
    all_to_all x1, starting transfers between devices, shards(): lax.all_to_all(pack_tokens(partial_inputs), 'tensor', 0, 0, tiled=True)  4.91 us
  transfers between devices with their start and end apart: 24, of which 2 were waited for; matrix products, arithmetic and copies ran while one was open for 15% of the time, Pallas kernels for 20%

profile of v1, /device:TPU:1, one launch (start us, length us, event | category | flops | bytes accessed | tf_op | source)
XLA Modules:
  0.0 143.1 jit_solution(16472607660670752214)
XLA Ops:
  0.7 6.9 %columns_of_core.1 = bf16[1024,2048]{1,0:T(8,128)(2,1)} custom-call(s32[1]{0:T(128)} %bitcast.5.core_ref, bf16[1024,4096]{1,0:T(8,128)(2,1)} %refs_7_.7), custom_call_target="tpu_custom_call" | custom-call | tf_op jit(solution)/shard_map/columns_of_core/pallas_call | solution.py:50
  7.5 3.2 %collective-permute-start.7 = (bf16[1024,2048]{1,0:T(8,128)(2,1)}, bf16[1024,2048]{1,0:T(8,128)(2,1)}, u32[]{:S(2)}, u32[]{:S(2)}) collective-permute-start(bf16[1024,2048]{1,0:T(8,128)(2,1)} %columns_of_core.1), channel_id=1, source_target_pairs={{0,1},{1,0},{2,3},{3,2},{4,5},{5,4},{6,7},{7,6},{8,9},{9,8},{10,11... | collective-permute-start | bytes 12582920 | tf_op jit(solution)/shard_map/ppermute | solution.py:35
  15.7 4.9 %all-to-all-start = ((f32[16,24,128]{2,1,0:T(8,128)}), f32[16,24,128]{2,1,0:T(8,128)S(1)}, u32[]{:S(2)}, u32[]{:S(2)}) async-start(f32[16,24,128]{2,1,0:T(8,128)} %reshape.119), calls=%async_computation | async-start | bytes 393216 | tf_op jit(solution)/shard_map/all_to_all | solution.py:250
  20.7 2.4 %fusion.4 = bf16[768,1024]{1,0:T(8,128)(2,1)S(1)} fusion(bf16[3,2,128,1024]{3,2,1,0:T(8,128)(2,1)} %param.16, bf16[3,2,128,1024]{3,2,1,0:T(8,128)(2,1)S(1)} %copy-done.1), kind=kLoop, calls=%fused_computation.6 | loop fusion | flops 6291456 | bytes 4718592 | tf_op jit(solution)/shard_map/convert_element_type | solution.py:256
  24.5 1.4 collective-permute-start.4
  25.9 2.4 %collective-permute-start.3 = (bf16[512,256]{1,0:T(8,128)(2,1)}, bf16[512,256]{1,0:T(8,128)(2,1)}, u32[]{:S(2)}, u32[]{:S(2)}) collective-permute-start(bf16[512,256]{1,0:T(8,128)(2,1)} %collective-permute-done.2.refs_3_), channel_id=1, source_target_pairs={{0,12},{1,13},{2,14},{3,15},{4,0},{5,1},{6,2},{7,3},{8,4},{9,5},{1... | collective-permute-start | bytes 786440 | tf_op jit(solution)/shard_map/ppermute | solution.py:35
  29.4 4.8 %all-to-all-start.1 = ((f32[16,24,128]{2,1,0:T(8,128)}), f32[16,24,128]{2,1,0:T(8,128)}, u32[]{:S(2)}, u32[]{:S(2)}) async-start(f32[16,24,128]{2,1,0:T(8,128)} %broadcast_in_dim.11), calls=%async_computation.1 | async-start | bytes 393216 | tf_op jit(solution)/shard_map/all_to_all | solution.py:253
  34.3 2.7 %collective-permute-start.10 = (bf16[512,256]{1,0:T(8,128)(2,1)}, bf16[512,256]{1,0:T(8,128)(2,1)}, u32[]{:S(2)}, u32[]{:S(2)}) collective-permute-start(bf16[512,256]{1,0:T(8,128)(2,1)} %bitcast.4.refs_0_), channel_id=1, source_target_pairs={{0,12},{1,13},{2,14},{3,15},{4,0},{5,1},{6,2},{7,3},{8,4},{9,5},{1... | collective-permute-start | bytes 786440 | tf_op jit(solution)/shard_map/ppermute | solution.py:35
  38.4 2.4 %copy.78 = bf16[4096,64]{1,0:T(8,128)(2,1)} copy(bf16[4096,64]{0,1:T(8,128)(2,1)} %param.21) | data formatting | bytes 1048576 | tf_op args[8]
  40.7 2.6 %pad.12.refs_12_.refs_13_.refs_14_.refs_15_.refs_16_ = bf16[4096,128]{1,0:T(8,128)(2,1)} pad(bf16[4096,64]{1,0:T(8,128)(2,1)} %copy.78, bf16[]{:T(256)} %constant.85.clone.1), padding=0_0x64_0 | pad | bytes 1572866 | tf_op jit(solution)/shard_map/jit(_pad)/pad | solution.py:245
  49.2 1.5 %collective-permute-start.14 = (bf16[256,256]{1,0:T(8,128)(2,1)}, bf16[256,256]{1,0:T(8,128)(2,1)S(1)}, u32[]{:S(2)}, u32[]{:S(2)}) collective-permute-start(bf16[256,256]{1,0:T(8,128)(2,1)} %bitcast.52), channel_id=1, source_target_pairs={{0,2},{1,3},{2,0},{3,1},{4,6},{5,7},{6,4},{7,5},{8,10},{9,11},{10,... | collective-permute-start | bytes 393224 | tf_op jit(solution)/shard_map/ppermute | solution.py:35
  52.0 1.5 %collective-permute-start.6 = (bf16[256,256]{1,0:T(8,128)(2,1)S(1)}, bf16[256,256]{1,0:T(8,128)(2,1)S(1)}, u32[]{:S(2)}, u32[]{:S(2)}) collective-permute-start(bf16[256,256]{1,0:T(8,128)(2,1)S(1)} %slice.41), channel_id=1, source_target_pairs={{0,12},{1,13},{2,14},{3,15},{4,0},{5,1},{6,2},{7,3},{8,4},{9,5},{1... | collective-permute-start | bytes 393224 | tf_op jit(solution)/shard_map/ppermute | solution.py:35
  53.5 7.9 %stage_first.2.refs_21_ = f32[512,128]{1,0:T(8,128)} custom-call(s32[8]{0:T(128)} %concatenate.15.blocks_ref, bf16[512,256]{1,0:T(8,128)(2,1)} %bitcast.4.refs_0_, bf16[512,256]{1,0:T(8,128)(2,1)} %collective-permute-done.refs_1_, bf16[512,256]{1,0:T(8,128)(2,1)} %collective-permute-done.10.refs_2_, bf16[512,256]{1,0:T(8,128)(2,1)} %collective-permute-done.2.refs_3_, ...), custom_call_target="tpu_custom_call" | custom-call | flops 2415919104 | bytes 6291456 | tf_op jit(solution)/shard_map/stage_first/pallas_call | solution.py:169
  61.5 1.4 collective-permute-start.18
  63.2 1.4 collective-permute-start.15
  66.5 8.5 %stage_last.2 = f32[2,64,128]{2,1,0:T(8,128)} custom-call(s32[8]{0:T(128)} %concatenate.14.blocks_ref, bf16[512,256]{1,0:T(8,128)(2,1)} %copy-done.9, bf16[512,256]{1,0:T(8,128)(2,1)} %collective-permute-done.3.refs_1_, bf16[512,256]{1,0:T(8,128)(2,1)} %copy-done.4, bf16[256,256]{1,0:T(8,128)(2,1)} %copy-done.16, bf16[256,256]{1,0:T(8,128)(2,1)} %copy-done.19, ...), custom_call_target="tpu_custom_call" | custom-call | flops 2415919104 | bytes 6291456 | tf_op jit(solution)/shard_map/stage_last/pallas_call | solution.py:169
  76.5 5.8 %all-to-all-start.2 = ((f32[16,8,128]{2,1,0:T(8,128)}), f32[16,8,128]{2,1,0:T(8,128)S(1)}, u32[]{:S(2)}, u32[]{:S(2)}) async-start(f32[16,8,128]{2,1,0:T(8,128)} %copy.87), calls=%async_computation.2 | async-start | bytes 131072 | tf_op jit(solution)/shard_map/all_to_all | solution.py:314
  83.0 6.0 %stage_first.3.refs_20_ = f32[256,128]{1,0:T(8,128)} custom-call(s32[8]{0:T(128)} %concatenate.15.blocks_ref, bf16[256,256]{1,0:T(8,128)(2,1)} %bitcast.53, bf16[256,256]{1,0:T(8,128)(2,1)} %copy-done.10, bf16[256,256]{1,0:T(8,128)(2,1)} %copy-done.17, bf16[256,256]{1,0:T(8,128)(2,1)} %copy-done.13, bf16[1024,4096]{1,0:T(8,128)(2,1)} %refs_7_.7, ...), custom_call_target="tpu_custom_call" | custom-call | flops 1207959552 | bytes 5242880 | tf_op jit(solution)/shard_map/stage_first/pallas_call | solution.py:169
  90.4 6.4 %stage_last.3 = f32[1,64,128]{2,1,0:T(8,128)} custom-call(s32[8]{0:T(128)} %concatenate.14.blocks_ref, bf16[256,256]{1,0:T(8,128)(2,1)} %copy-done.12, bf16[256,256]{1,0:T(8,128)(2,1)} %copy-done.15, bf16[256,256]{1,0:T(8,128)(2,1)} %copy-done.14, bf16[256,256]{1,0:T(8,128)(2,1)} %copy-done.18, bf16[1024,4096]{1,0:T(8,128)(2,1)} %refs_7_.7, ...), custom_call_target="tpu_custom_call" | custom-call | flops 1207959552 | bytes 5242880 | tf_op jit(solution)/shard_map/stage_last/pallas_call | solution.py:169
  96.8 1.7 %broadcast_in_dim.13 = f32[16,16,4,128]{3,2,1,0:T(4,128)} broadcast(f32[16,4,128]{2,1,0:T(4,128)} %bitcast.58), dimensions={1,2,3} | broadcast | bytes 557056 | tf_op jit(solution)/shard_map/broadcast_in_dim | solution.py:302
  98.5 13.2 %all-to-all-start.3 = ((f32[256,4,128]{2,1,0:T(4,128)}), f32[256,4,128]{2,1,0:T(4,128)S(1)}, u32[]{:S(2)}, u32[]{:S(2)}) async-start(f32[256,4,128]{2,1,0:T(4,128)} %bitcast.24), calls=%async_computation.3 | async-start | bytes 1048576 | tf_op jit(solution)/shard_map/all_to_all | solution.py:305
  112.6 19.2 %all-to-all-done.3 = f32[256,4,128]{2,1,0:T(4,128)S(1)} async-done(((f32[256,4,128]{2,1,0:T(4,128)}), f32[256,4,128]{2,1,0:T(4,128)S(1)}, u32[]{:S(2)}, u32[]{:S(2)}) %all-to-all-start.3) | async-done | bytes 524320 | tf_op jit(solution)/shard_map/all_to_all | solution.py:305
  132.8 4.0 %all-to-all-start.4 = ((f32[16,1,128]{2,1,0:T(1,128)}), f32[16,1,128]{2,1,0:T(1,128)S(1)}, u32[]{:S(2)}, u32[]{:S(2)}) async-start(f32[16,1,128]{2,1,0:T(1,128)} %broadcast_in_dim.14), calls=%async_computation.4 | async-start | bytes 16384 | tf_op jit(solution)/shard_map/all_to_all | solution.py:327
  137.5 4.8 %all-to-all-done.4 = f32[16,1,128]{2,1,0:T(1,128)S(1)} async-done(((f32[16,1,128]{2,1,0:T(1,128)}), f32[16,1,128]{2,1,0:T(1,128)S(1)}, u32[]{:S(2)}, u32[]{:S(2)}) %all-to-all-start.4) | async-done | bytes 8224 | tf_op jit(solution)/shard_map/all_to_all | solution.py:327
  (129 shorter events, 25.1 us)
Async XLA Ops:
  7.5 44.5 %collective-permute-start.7 = (bf16[1024,2048]{1,0:T(8,128)(2,1)}, bf16[1024,2048]{1,0:T(8,128)(2,1)}, u32[]{:S(2)}, u32[]{:S(2)}) collective-permute-start(bf16[1024,2048]{1,0:T(8,128)(2,1)} %columns_of_core.1), channel_id=1, source_target_pairs={{0,1},{1,0},{2,3},{3,2},{4,5},{5,4},{6,7},{7,6},{8,9},{9,8},{10,11... | collective-permute-start | bytes 12582920 | tf_op jit(solution)/shard_map/ppermute | solution.py:35
  11.5 13.0 %collective-permute-start = (bf16[512,256]{1,0:T(8,128)(2,1)}, bf16[512,256]{1,0:T(8,128)(2,1)}, u32[]{:S(2)}, u32[]{:S(2)}) collective-permute-start(bf16[512,256]{1,0:T(8,128)(2,1)} %bitcast.4.refs_0_), channel_id=1, source_target_pairs={{0,4},{1,5},{2,6},{3,7},{4,8},{5,9},{6,10},{7,11},{8,12},{9,13},{1... | collective-permute-start | bytes 786440 | tf_op jit(solution)/shard_map/ppermute | solution.py:35
  11.5 14.4 %collective-permute-start.2 = (bf16[512,256]{1,0:T(8,128)(2,1)}, bf16[512,256]{1,0:T(8,128)(2,1)}, u32[]{:S(2)}, u32[]{:S(2)}) collective-permute-start(bf16[512,256]{1,0:T(8,128)(2,1)} %bitcast.4.refs_0_), channel_id=1, source_target_pairs={{0,2},{1,3},{2,0},{3,1},{4,6},{5,7},{6,4},{7,5},{8,10},{9,11},{10,... | collective-permute-start | bytes 786440 | tf_op jit(solution)/shard_map/ppermute | solution.py:35
  12.3 38.5 %collective-permute-start.8 = (bf16[768,1024]{1,0:T(8,128)(2,1)S(1)}, bf16[768,1024]{1,0:T(8,128)(2,1)}, u32[]{:S(2)}, u32[]{:S(2)}) collective-permute-start(bf16[768,1024]{1,0:T(8,128)(2,1)S(1)} %bitcast.47), channel_id=1, source_target_pairs={{0,1},{1,0},{2,3},{3,2},{4,5},{5,4},{6,7},{7,6},{8,9},{9,8},{10,11... | collective-permute-start | bytes 4718600 | tf_op jit(solution)/shard_map/ppermute | solution.py:35
  12.9 10.9 %collective-permute-start.12 = (bf16[256,256]{1,0:T(8,128)(2,1)S(1)}, bf16[256,256]{1,0:T(8,128)(2,1)S(1)}, u32[]{:S(2)}, u32[]{:S(2)}) collective-permute-start(bf16[256,256]{1,0:T(8,128)(2,1)S(1)} %bitcast.51), channel_id=1, source_target_pairs={{0,4},{1,5},{2,6},{3,7},{4,8},{5,9},{6,10},{7,11},{8,12},{9,13},{1... | collective-permute-start | bytes 393224 | tf_op jit(solution)/shard_map/ppermute | solution.py:35
  15.7 12.9 %all-to-all-start = ((f32[16,24,128]{2,1,0:T(8,128)}), f32[16,24,128]{2,1,0:T(8,128)S(1)}, u32[]{:S(2)}, u32[]{:S(2)}) async-start(f32[16,24,128]{2,1,0:T(8,128)} %reshape.119), calls=%async_computation | async-start | bytes 393216 | tf_op jit(solution)/shard_map/all_to_all | solution.py:250
  23.8 10.5 %collective-permute-start.11 = (f32[768,64]{1,0:T(8,128)S(1)}, f32[768,64]{1,0:T(8,128)}, u32[]{:S(2)}, u32[]{:S(2)}) collective-permute-start(f32[768,64]{1,0:T(8,128)S(1)} %fusion.11), channel_id=1, source_target_pairs={{0,1},{1,0},{2,3},{3,2},{4,5},{5,4},{6,7},{7,6},{8,9},{9,8},{10,11... | collective-permute-start | bytes 589832 | tf_op jit(solution)/shard_map/ppermute | solution.py:35
  24.5 12.5 %collective-permute-start.4 = (bf16[512,256]{1,0:T(8,128)(2,1)}, bf16[512,256]{1,0:T(8,128)(2,1)S(1)}, u32[]{:S(2)}, u32[]{:S(2)}) collective-permute-start(bf16[512,256]{1,0:T(8,128)(2,1)} %collective-permute-done.refs_1_), channel_id=1, source_target_pairs={{0,2},{1,3},{2,0},{3,1},{4,6},{5,7},{6,4},{7,5},{8,10},{9,11},{10,... | collective-permute-start | bytes 786440 | tf_op jit(solution)/shard_map/ppermute | solution.py:35
  25.9 20.3 %collective-permute-start.3 = (bf16[512,256]{1,0:T(8,128)(2,1)}, bf16[512,256]{1,0:T(8,128)(2,1)}, u32[]{:S(2)}, u32[]{:S(2)}) collective-permute-start(bf16[512,256]{1,0:T(8,128)(2,1)} %collective-permute-done.2.refs_3_), channel_id=1, source_target_pairs={{0,12},{1,13},{2,14},{3,15},{4,0},{5,1},{6,2},{7,3},{8,4},{9,5},{1... | collective-permute-start | bytes 786440 | tf_op jit(solution)/shard_map/ppermute | solution.py:35
  29.4 15.5 %all-to-all-start.1 = ((f32[16,24,128]{2,1,0:T(8,128)}), f32[16,24,128]{2,1,0:T(8,128)}, u32[]{:S(2)}, u32[]{:S(2)}) async-start(f32[16,24,128]{2,1,0:T(8,128)} %broadcast_in_dim.11), calls=%async_computation.1 | async-start | bytes 393216 | tf_op jit(solution)/shard_map/all_to_all | solution.py:253
  34.3 16.3 %collective-permute-start.10 = (bf16[512,256]{1,0:T(8,128)(2,1)}, bf16[512,256]{1,0:T(8,128)(2,1)}, u32[]{:S(2)}, u32[]{:S(2)}) collective-permute-start(bf16[512,256]{1,0:T(8,128)(2,1)} %bitcast.4.refs_0_), channel_id=1, source_target_pairs={{0,12},{1,13},{2,14},{3,15},{4,0},{5,1},{6,2},{7,3},{8,4},{9,5},{1... | collective-permute-start | bytes 786440 | tf_op jit(solution)/shard_map/ppermute | solution.py:35
  37.0 12.1 %collective-permute-start.9 = (bf16[1024,128]{1,0:T(8,128)(2,1)S(1)}, bf16[1024,128]{1,0:T(8,128)(2,1)S(1)}, u32[]{:S(2)}, u32[]{:S(2)}) collective-permute-start(bf16[1024,128]{1,0:T(8,128)(2,1)S(1)} %pad.13.refs_18_.refs_19_), channel_id=1, source_target_pairs={{0,1},{1,0},{2,3},{3,2},{4,5},{5,4},{6,7},{7,6},{8,9},{9,8},{10,11... | collective-permute-start | bytes 786440 | tf_op jit(solution)/shard_map/ppermute | solution.py:35
  46.2 17.1 %collective-permute-start.1 = (bf16[512,256]{1,0:T(8,128)(2,1)}, bf16[512,256]{1,0:T(8,128)(2,1)S(1)}, u32[]{:S(2)}, u32[]{:S(2)}) collective-permute-start(bf16[512,256]{1,0:T(8,128)(2,1)} %collective-permute-done.refs_1_), channel_id=1, source_target_pairs={{0,4},{1,5},{2,6},{3,7},{4,8},{5,9},{6,10},{7,11},{8,12},{9,13},{1... | collective-permute-start | bytes 786440 | tf_op jit(solution)/shard_map/ppermute | solution.py:35
  49.2 12.3 %collective-permute-start.14 = (bf16[256,256]{1,0:T(8,128)(2,1)}, bf16[256,256]{1,0:T(8,128)(2,1)S(1)}, u32[]{:S(2)}, u32[]{:S(2)}) collective-permute-start(bf16[256,256]{1,0:T(8,128)(2,1)} %bitcast.52), channel_id=1, source_target_pairs={{0,2},{1,3},{2,0},{3,1},{4,6},{5,7},{6,4},{7,5},{8,10},{9,11},{10,... | collective-permute-start | bytes 393224 | tf_op jit(solution)/shard_map/ppermute | solution.py:35
  50.6 12.3 %collective-permute-start.13 = (bf16[256,256]{1,0:T(8,128)(2,1)}, bf16[256,256]{1,0:T(8,128)(2,1)S(1)}, u32[]{:S(2)}, u32[]{:S(2)}) collective-permute-start(bf16[256,256]{1,0:T(8,128)(2,1)} %copy-done.10), channel_id=1, source_target_pairs={{0,4},{1,5},{2,6},{3,7},{4,8},{5,9},{6,10},{7,11},{8,12},{9,13},{1... | collective-permute-start | bytes 393224 | tf_op jit(solution)/shard_map/ppermute | solution.py:35
  50.8 13.8 %collective-permute-start.5 = (bf16[256,256]{1,0:T(8,128)(2,1)S(1)}, bf16[256,256]{1,0:T(8,128)(2,1)S(1)}, u32[]{:S(2)}, u32[]{:S(2)}) collective-permute-start(bf16[256,256]{1,0:T(8,128)(2,1)S(1)} %slice.40), channel_id=1, source_target_pairs={{0,4},{1,5},{2,6},{3,7},{4,8},{5,9},{6,10},{7,11},{8,12},{9,13},{1... | collective-permute-start | bytes 393224 | tf_op jit(solution)/shard_map/ppermute | solution.py:35
  52.0 13.8 %collective-permute-start.6 = (bf16[256,256]{1,0:T(8,128)(2,1)S(1)}, bf16[256,256]{1,0:T(8,128)(2,1)S(1)}, u32[]{:S(2)}, u32[]{:S(2)}) collective-permute-start(bf16[256,256]{1,0:T(8,128)(2,1)S(1)} %slice.41), channel_id=1, source_target_pairs={{0,12},{1,13},{2,14},{3,15},{4,0},{5,1},{6,2},{7,3},{8,4},{9,5},{1... | collective-permute-start | bytes 393224 | tf_op jit(solution)/shard_map/ppermute | solution.py:35
  61.5 20.8 %collective-permute-start.18 = (bf16[256,256]{1,0:T(8,128)(2,1)S(1)}, bf16[256,256]{1,0:T(8,128)(2,1)S(1)}, u32[]{:S(2)}, u32[]{:S(2)}) collective-permute-start(bf16[256,256]{1,0:T(8,128)(2,1)S(1)} %bitcast.54), channel_id=1, source_target_pairs={{0,12},{1,13},{2,14},{3,15},{4,0},{5,1},{6,2},{7,3},{8,4},{9,5},{1... | collective-permute-start | bytes 393224 | tf_op jit(solution)/shard_map/ppermute | solution.py:35
  62.9 26.1 %collective-permute-start.16 = (bf16[256,256]{1,0:T(8,128)(2,1)S(1)}, bf16[256,256]{1,0:T(8,128)(2,1)S(1)}, u32[]{:S(2)}, u32[]{:S(2)}) collective-permute-start(bf16[256,256]{1,0:T(8,128)(2,1)S(1)} %copy-done.11), channel_id=1, source_target_pairs={{0,2},{1,3},{2,0},{3,1},{4,6},{5,7},{6,4},{7,5},{8,10},{9,11},{10,... | collective-permute-start | bytes 393224 | tf_op jit(solution)/shard_map/ppermute | solution.py:35
  63.2 25.8 %collective-permute-start.15 = (bf16[256,256]{1,0:T(8,128)(2,1)S(1)}, bf16[256,256]{1,0:T(8,128)(2,1)S(1)}, u32[]{:S(2)}, u32[]{:S(2)}) collective-permute-start(bf16[256,256]{1,0:T(8,128)(2,1)S(1)} %collective-permute-done.14.refs_3_), channel_id=1, source_target_pairs={{0,12},{1,13},{2,14},{3,15},{4,0},{5,1},{6,2},{7,3},{8,4},{9,5},{1... | collective-permute-start | bytes 393224 | tf_op jit(solution)/shard_map/ppermute | solution.py:35
  64.6 24.4 %collective-permute-start.17 = (bf16[256,256]{1,0:T(8,128)(2,1)S(1)}, bf16[256,256]{1,0:T(8,128)(2,1)S(1)}, u32[]{:S(2)}, u32[]{:S(2)}) collective-permute-start(bf16[256,256]{1,0:T(8,128)(2,1)S(1)} %collective-permute-done.13.refs_0_), channel_id=1, source_target_pairs={{0,2},{1,3},{2,0},{3,1},{4,6},{5,7},{6,4},{7,5},{8,10},{9,11},{10,... | collective-permute-start | bytes 393224 | tf_op jit(solution)/shard_map/ppermute | solution.py:35
  76.5 20.3 %all-to-all-start.2 = ((f32[16,8,128]{2,1,0:T(8,128)}), f32[16,8,128]{2,1,0:T(8,128)S(1)}, u32[]{:S(2)}, u32[]{:S(2)}) async-start(f32[16,8,128]{2,1,0:T(8,128)} %copy.87), calls=%async_computation.2 | async-start | bytes 131072 | tf_op jit(solution)/shard_map/all_to_all | solution.py:314
  98.5 33.4 %all-to-all-start.3 = ((f32[256,4,128]{2,1,0:T(4,128)}), f32[256,4,128]{2,1,0:T(4,128)S(1)}, u32[]{:S(2)}, u32[]{:S(2)}) async-start(f32[256,4,128]{2,1,0:T(4,128)} %bitcast.24), calls=%async_computation.3 | async-start | bytes 1048576 | tf_op jit(solution)/shard_map/all_to_all | solution.py:305
  132.8 9.5 %all-to-all-start.4 = ((f32[16,1,128]{2,1,0:T(1,128)}), f32[16,1,128]{2,1,0:T(1,128)S(1)}, u32[]{:S(2)}, u32[]{:S(2)}) async-start(f32[16,1,128]{2,1,0:T(1,128)} %broadcast_in_dim.14), calls=%async_computation.4 | async-start | bytes 16384 | tf_op jit(solution)/shard_map/all_to_all | solution.py:327
  (25 other events, 177.2 us)

commit v2 on v0

v2 whole, which is shorter than its diff:
```python
import jax
import jax.numpy as jnp
from jax import lax
from jax.experimental import pallas as pl
from jax.experimental.pallas import tpu as pltpu
from jax.sharding import PartitionSpec as P

QUERY_DEV = 1
NX, NY, NC = 4, 2, 2
CHIPS = NX * NY
PROJ = 64
LANES = 128
highest = lax.Precision.HIGHEST
epsilon = 1e-06
F32, BF16 = jnp.float32, jnp.bfloat16
VMEM_LIMIT = 24 * 1024 * 1024


def moves(step):
    pairs = []
    for x in range(NX):
        for y in range(NY):
            for c in range(NC):
                tx, ty, tc = step(x, y, c)
                source = (x * NY + y) * NC + c
                target = ((tx % NX) * NY + ty % NY) * NC + tc % NC
                pairs.append((source, target))
    return pairs


X_UP = moves(lambda x, y, c: (x + 1, y, c))
X_DOWN = moves(lambda x, y, c: (x - 1, y, c))
Y_SWAP = moves(lambda x, y, c: (x, y + 1, c))
CORE_SWAP = moves(lambda x, y, c: (x, y, c + 1))
Y_OR_X = moves(lambda x, y, c: (x + c, y + 1 - c, c))

VMEM = pl.BlockSpec(memory_space=pltpu.VMEM)
ANY = pl.BlockSpec(memory_space=pl.ANY)
SMEM = pl.BlockSpec(memory_space=pltpu.SMEM)
PARAMS = pltpu.CompilerParams(vmem_limit_bytes=VMEM_LIMIT)


def send(value, pairs):
    return lax.ppermute(value, "tensor", pairs)


def dot_rows(a, b, precision=None):
    return lax.dot_general(a, b, (((0,), (0,)), ((), ())), precision=precision, preferred_element_type=F32)


def dot_t(a, b, precision=None):
    return lax.dot_general(a, b, (((1,), (1,)), ((), ())), precision=precision, preferred_element_type=F32)


def in_hbm(array):
    return pltpu.with_memory_space_constraint(array, pltpu.HBM)


def in_vmem(array):
    return pltpu.with_memory_space_constraint(array, pltpu.VMEM)


def first(place, flat, inputs, in_basis_t):
    tokens, width = flat.shape

    def body(place_ref, ref, in_ref, basis_ref, own_ref, proj_ref):
        own_ref[...] = ref[...].T
        proj_ref[...] = dot_t(basis_ref[...], in_ref[...])

    def whole(shape):
        return pl.BlockSpec(shape, lambda i, place_ref: (0, 0))

    return pl.pallas_call(
        body,
        grid_spec=pltpu.PrefetchScalarGridSpec(
            num_scalar_prefetch=1,
            grid=(1,),
            in_specs=[
                whole((tokens, width)),
                whole((tokens, width)),
                pl.BlockSpec((PROJ, width), lambda i, place_ref: (0, place_ref[0])),
            ],
            out_specs=(whole((width, tokens)), whole((PROJ, tokens))),
        ),
        out_shape=(
            jax.ShapeDtypeStruct((width, tokens), BF16),
            jax.ShapeDtypeStruct((PROJ, tokens), F32),
        ),
        compiler_params=PARAMS,
        name="first",
    )(place, in_hbm(flat), in_hbm(inputs), in_hbm(in_basis_t))


def prepare(gate, up_out, down_in_basis_t):
    tokens, hidden = gate.shape
    block = 128

    def body(gate_ref, up_ref, down_ref, g_ref, act_ref):
        raw = gate_ref[...]
        value = raw.astype(F32)
        value = value / (1.0 + jnp.exp(-value))
        activation = (value * up_ref[...].astype(F32)).astype(BF16)
        act_ref[...] = dot_t(down_ref[...], activation)
        g_ref[...] = raw.T

    return pl.pallas_call(
        body,
        grid=(tokens // block,),
        in_specs=[
            pl.BlockSpec((block, hidden), lambda i: (i, 0)),
            pl.BlockSpec((block, hidden), lambda i: (i, 0)),
            pl.BlockSpec((PROJ, hidden), lambda i: (0, 0)),
        ],
        out_specs=(
            pl.BlockSpec((hidden, block), lambda i: (0, i)),
            pl.BlockSpec((PROJ, block), lambda i: (0, i)),
        ),
        out_shape=(
            jax.ShapeDtypeStruct((hidden, tokens), BF16),
            jax.ShapeDtypeStruct((PROJ, tokens), F32),
        ),
        compiler_params=PARAMS,
        name="prepare",
    )(in_hbm(gate), in_hbm(up_out), in_hbm(down_in_basis_t))


def spread_inputs(core, proj, other_proj, copies, after):
    half = proj.shape[1] // 2

    def body(core_ref, proj_ref, other_ref, *refs):
        o_ref = refs[-1]
        start = pl.multiple_of(core_ref[0] * half, half)
        both = (proj_ref[:, pl.ds(start, half)] + other_ref[:, pl.ds(start, half)]).astype(BF16)
        for i in range(copies):
            o_ref[i] = both

    return pl.pallas_call(
        body,
        in_specs=[SMEM, VMEM, VMEM] + [ANY] * len(after),
        out_specs=VMEM,
        out_shape=jax.ShapeDtypeStruct((copies, PROJ, half), BF16),
        compiler_params=PARAMS,
        name="spread_inputs",
    )(core, proj, other_proj, *[in_hbm(array) for array in after])


def left_factors(lengths, weights, parts, act, seq_len):
    tokens = act.shape[1]
    half = tokens // 2
    sequences = tokens // seq_len

    def body(lengths_ref, weights_ref, parts_ref, act_ref, o_ref):
        lane = lax.broadcasted_iota(jnp.int32, (1, seq_len), 1)
        for c in range(NC):
            proj = parts_ref[c].astype(F32)
            for chip in range(1, CHIPS):
                proj = proj + parts_ref[chip * NC + c].astype(F32)
            o_ref[:PROJ, c * half : (c + 1) * half] = proj
        o_ref[PROJ:, :] = act_ref[...]
        for s in range(sequences):
            columns = slice(s * seq_len, (s + 1) * seq_len)
            sign = 1.0 if s % 2 == 0 else -1.0
            factor = jnp.where(lane < lengths_ref[s // 2, s % 2], weights_ref[s // 2] * sign, 0.0)
            o_ref[:, columns] = o_ref[:, columns] * factor

    return pl.pallas_call(
        body,
        in_specs=[SMEM, SMEM, VMEM, VMEM],
        out_specs=VMEM,
        out_shape=jax.ShapeDtypeStruct((2 * PROJ, tokens), F32),
        compiler_params=PARAMS,
        name="left_factors",
    )(lengths, weights, parts, act)


def stage(core, chips, mine, twins, weights, gate_t, basis_t, out_basis_t, after=(), last=None):
    width, tokens = mine[0].shape
    hidden = gate_t.shape[0]
    count = len(mine)
    depth = NC * count * width
    chunk, block = 512, 256
    steps = hidden // chunk
    pieces = [piece for pair in zip(mine, twins) for piece in pair]

    def body(core_ref, chips_ref, *refs):
        refs = list(refs)
        piece_refs = [refs.pop(0) for _ in pieces]
        w_hbm, g_hbm, b_ref, out_basis_ref = [refs.pop(0) for _ in range(4)]
        if last is not None:
            before_ref, left_ref = refs.pop(0), refs.pop(0)
        refs = refs[len(after) :]
        o_ref, cat, w_ref, g_ref, sem, w_sem, g_sem = refs[:7]
        sums = o_ref if last is None else refs[7]
        copies = []
        for i, ref in enumerate(piece_refs):
            side = core_ref[0] if i % NC == 0 else 1 - core_ref[0]
            row = pl.multiple_of((i // NC * NC + side) * width, width)
            copies.append(pltpu.make_async_copy(ref, cat.at[pl.ds(row, width)], sem.at[i]))
        weight_copies = []
        for step in range(steps):
            span = pl.ds(step * chunk, chunk)
            group = []
            for i in range(count):
                columns = pl.ds(pl.multiple_of(chips_ref[i] * NC * width, NC * width), NC * width)
                target = w_ref.at[span, pl.ds(i * NC * width, NC * width)]
                group.append(pltpu.make_async_copy(w_hbm.at[span, columns], target, w_sem.at[step, i]))
            group.append(pltpu.make_async_copy(g_hbm.at[span], g_ref.at[span], g_sem.at[step]))
            weight_copies.append(group)
        for copy in copies + weight_copies[0]:
            copy.start()
        for group in weight_copies[1:]:
            for copy in group:
                copy.start()
        out_basis = jnp.concatenate(
            [
                out_basis_ref[:, pl.ds(pl.multiple_of(chips_ref[i] * NC * width, NC * width), NC * width)]
                for i in range(count)
            ],
            axis=1,
        )
        if last is not None:
            sums[...] = before_ref[...]
        else:
            sums[...] = jnp.zeros_like(sums)
        for copy in copies:
            copy.wait()
        sums[PROJ:, :] += jnp.dot(out_basis, cat[...], preferred_element_type=F32)
        for step in range(steps):
            for copy in weight_copies[step]:
                copy.wait()
            h = step * chunk
            for t in range(0, tokens, block):
                span = slice(t, t + block)
                grad = jnp.dot(w_ref[h : h + chunk, :], cat[:, span], preferred_element_type=F32)
                gate = g_ref[h : h + chunk, span].astype(F32)
                gate = gate / (1.0 + jnp.exp(-gate))
                sums[:PROJ, span] += jnp.dot(
                    b_ref[:, h : h + chunk], (grad * gate).astype(BF16), preferred_element_type=F32
                )
        if last is not None:
            pair_tokens, devices = last[2:]
            share = PROJ // devices
            half = lax.broadcasted_iota(jnp.int32, (PROJ, LANES), 1) < PROJ
            for pair in range(tokens // pair_tokens):
                span = slice(pair * pair_tokens, (pair + 1) * pair_tokens)
                both = dot_t(left_ref[:, span], sums[:, span], highest)
                grads = jnp.where(half, both[:PROJ], both[PROJ:])
                for k in range(devices):
                    o_ref[k, pair] = grads[k * share : (k + 1) * share, :]

    operands = [core, chips, *[in_hbm(piece) for piece in pieces], in_hbm(weights), in_hbm(gate_t)]
    operands += [basis_t, out_basis_t]
    in_specs = [SMEM, SMEM] + [ANY] * (len(pieces) + 2) + [VMEM] * 2
    scratch = [
        pltpu.VMEM((depth, tokens), BF16),
        pltpu.VMEM((hidden, depth), BF16),
        pltpu.VMEM((hidden, tokens), BF16),
        pltpu.SemaphoreType.DMA((len(pieces),)),
        pltpu.SemaphoreType.DMA((steps, count)),
        pltpu.SemaphoreType.DMA((steps,)),
    ]
    shape = (2 * PROJ, tokens)
    if last is not None:
        operands += last[:2]
        in_specs += [VMEM, VMEM]
        scratch.append(pltpu.VMEM(shape, F32))
        shape = (last[3], tokens // last[2], PROJ // last[3], LANES)
    operands += [in_hbm(array) for array in after]
    in_specs += [ANY] * len(after)
    return pl.pallas_call(
        body,
        in_specs=in_specs,
        out_specs=VMEM,
        out_shape=jax.ShapeDtypeStruct(shape, F32),
        scratch_shapes=scratch,
        compiler_params=PARAMS,
        cost_estimate=pl.CostEstimate(
            flops=2 * tokens * hidden * (depth + LANES),
            bytes_accessed=2 * depth * tokens,
            transcendentals=2 * tokens * hidden,
        ),
        name="stage_last" if last is not None else "stage_first",
    )(*operands)


def shards(
    inputs,
    cotangent,
    gate_pre,
    up_out,
    w_down,
    up_in_basis,
    up_out_basis,
    down_in_basis,
    down_out_basis,
    lengths,
    margins,
    curvature,
):
    pair_count = inputs.shape[0]
    seq_len = inputs.shape[2]
    width = inputs.shape[3]
    hidden = gate_pre.shape[3]
    token_count = pair_count * 2 * seq_len
    train_count = pair_count - QUERY_DEV
    dp_size = lax.axis_size("dp")
    tensor_size = lax.axis_size("tensor")
    row_share = PROJ // tensor_size
    place = lax.axis_index("tensor")
    x, y, core = place // (NY * NC), (place // NC) % NY, place % NC

    own, proj = first(
        place[None],
        cotangent.reshape(token_count, width),
        inputs.reshape(token_count, width),
        up_in_basis.T,
    )
    other_proj = send(proj, CORE_SWAP)
    left_own, right_own, across = send(own, X_UP), send(own, X_DOWN), send(own, Y_SWAP)
    near = [own, left_own, right_own, across]
    gate_t, act = prepare(
        gate_pre.reshape(token_count, hidden),
        up_out.reshape(token_count, hidden),
        down_in_basis.T,
    )
    left_own, across, gate_t = lax.optimization_barrier((left_own, across, gate_t))
    x2, pr, pl_ = send(left_own, X_UP), send(across, X_DOWN), send(left_own, Y_SWAP)
    spread = spread_inputs(core[None], proj, other_proj, tensor_size, (left_own, right_own, across, gate_t))
    third, spread = lax.optimization_barrier((jnp.where(core == 0, x2, pl_), spread))
    parts = lax.all_to_all(spread, "tensor", 0, 0, tiled=True)
    last_hop = send(third, Y_OR_X)
    far = [x2, pr, pl_, last_hop]
    near_twins = [send(piece, CORE_SWAP) for piece in near]
    far_twins = [send(piece, CORE_SWAP) for piece in far]

    def chip_at(dx, row):
        return ((x + dx) % NX) * NY + row

    near_chips = [chip_at(0, y), chip_at(3, y), chip_at(1, y), chip_at(0, 1 - y)]
    far_chips = [chip_at(2, y), chip_at(1, 1 - y), chip_at(3, 1 - y), chip_at(2, 1 - y)]
    chips = jnp.stack(near_chips + far_chips).astype(jnp.int32)
    pair_weights = 1.0 / (1.0 + jnp.exp(margins))
    left = left_factors(lengths, pair_weights, parts, act, seq_len)
    shared = (w_down, gate_t, up_out_basis.T, down_out_basis.T)
    near_sums = stage(core[None], chips[:4], near, near_twins, *shared, after=(x2, pr, pl_))
    grads = stage(
        core[None], chips[4:], far, far_twins, *shared,
        last=(near_sums, left, 2 * seq_len, tensor_size),
    )
    grad_parts = lax.all_to_all(grads, "tensor", 0, 0, tiled=True)
    rows = jnp.sum(grad_parts, axis=0)
    train_rows, query_rows = rows[:train_count], rows[train_count:]
    query_all = lax.all_to_all(
        jnp.broadcast_to(query_rows, (dp_size, row_share, LANES)), "dp", 0, 0, tiled=True
    )

    own_curvature = lax.dynamic_slice_in_dim(curvature, place * row_share, row_share, 1)
    own_curvature = own_curvature.transpose(1, 0, 2).reshape(row_share, LANES)
    weighted = own_curvature[None] * train_rows
    self_part = jnp.sum(weighted * train_rows, axis=(1, 2))
    cross_part = jnp.sum(query_all[:, None] * weighted[None], axis=(2, 3))
    sums = jnp.concatenate([cross_part.reshape(-1), self_part])
    sums = jnp.pad(sums, (0, LANES - sums.shape[0]))
    all_sums = lax.all_to_all(
        jnp.broadcast_to(sums[None, None], (tensor_size, 1, LANES)), "tensor", 0, 0, tiled=True
    )
    sums = jnp.sum(all_sums, axis=(0, 1))
    cross = sums[: dp_size * train_count].reshape(dp_size, train_count)
    self_terms = sums[dp_size * train_count : dp_size * train_count + train_count]
    scores = cross / jnp.sqrt(self_terms + epsilon)[None, :]
    train_block = train_rows.reshape(train_count, row_share, 2, PROJ).transpose(0, 2, 1, 3)
    return train_block, scores


def solution(mesh):
    return jax.shard_map(
        shards,
        mesh=mesh,
        in_specs=(
            P("dp", None, None, "tensor"),
            P("dp", None, None, "tensor"),
            P("dp", None, None, "tensor"),
            P("dp", None, None, "tensor"),
            P("tensor", None),
            P(),
            P("tensor", None),
            P("tensor", None),
            P(),
            P("dp", None),
            P("dp"),
            P(),
        ),
        out_specs=(P("dp", None, "tensor", None), P(None, "dp")),
        check_vma=False,
    )
```

time: 322 us -> 105 us (0.33)
  the two profiles are of different devices: /device:TPU:6 before, /device:TPU:1 now
where the time goes in v2:
time: 105 us
  starting transfers between devices  43.7 us (42%)
  Pallas kernels  31.2 us (30%)
  waiting for transfers between devices  22.6 us (22%)
  local copies, waits for them, and re-layouts  5.07 us (5%)
  other arithmetic  1.45 us (1%)
    pallas_call x2, Pallas kernels, stage(): pl.pallas_call(body, in_specs=in_specs, out_specs=VMEM, out_shape=jax.Sha...  23.4 us
    ppermute x16, starting transfers between devices, send(): return lax.ppermute(value, 'tensor', pairs)  17.1 us
    all_to_all x1, starting transfers between devices, shards(): lax.all_to_all(jnp.broadcast_to(query_rows, (dp_size, row_share, LANES)),...  10.6 us
    all_to_all x1, waiting for transfers between devices, shards(): lax.all_to_all(jnp.broadcast_to(query_rows, (dp_size, row_share, LANES)),...  9.02 us
    all_to_all x1, waiting for transfers between devices, shards(): grad_parts = lax.all_to_all(grads, 'tensor', 0, 0, tiled=True)  5.79 us
    all_to_all x1, starting transfers between devices, shards(): parts = lax.all_to_all(spread, 'tensor', 0, 0, tiled=True)  5.59 us
    all_to_all x1, starting transfers between devices, shards(): grad_parts = lax.all_to_all(grads, 'tensor', 0, 0, tiled=True)  5.27 us
    all_to_all x1, starting transfers between devices, shards(): lax.all_to_all(jnp.broadcast_to(sums[None, None], (tensor_size, 1, LANES)...  5.19 us
  transfers between devices with their start and end apart: 20, of which 6 were waited for; matrix products, arithmetic and copies ran while one was open for 2% of the time, Pallas kernels for 17%

profile of v2, /device:TPU:1, one launch (start us, length us, event | category | flops | bytes accessed | tf_op | source)
XLA Modules:
  0.0 104.9 jit_solution(2565710152676949392)
XLA Ops:
  0.6 1.4 %first.1 = (bf16[256,768]{1,0:T(8,128)(2,1)S(1)}, f32[64,768]{1,0:T(8,128)S(1)}) custom-call(s32[1]{0:T(128)} %bitcast.5.place_ref, bf16[768,256]{1,0:T(8,128)(2,1)} %bitcast.32, bf16[768,256]{1,0:T(8,128)(2,1)} %bitcast.33, bf16[64,4096]{1,0:T(8,128)(2,1)} %bitcast.31), custom_call_target="tpu_custom_call" | custom-call | tf_op jit(solution)/shard_map/first/pallas_call | solution.py:73
  2.1 2.1 %collective-permute-start = (bf16[256,768]{1,0:T(8,128)(2,1)S(1)}, bf16[256,768]{1,0:T(8,128)(2,1)S(1)}, u32[]{:S(2)}, u32[]{:S(2)}) collective-permute-start(bf16[256,768]{1,0:T(8,128)(2,1)S(1)} %get-tuple-element.11.refs_0_), channel_id=1, source_target_pairs={{0,4},{1,5},{2,6},{3,7},{4,8},{5,9},{6,10},{7,11},{8,12},{9,13},{1... | collective-permute-start | bytes 1179656 | tf_op jit(solution)/shard_map/ppermute | solution.py:44
  4.2 1.3 %collective-permute-start.1 = (bf16[256,768]{1,0:T(8,128)(2,1)S(1)}, bf16[256,768]{1,0:T(8,128)(2,1)}, u32[]{:S(2)}, u32[]{:S(2)}) collective-permute-start(bf16[256,768]{1,0:T(8,128)(2,1)S(1)} %get-tuple-element.11.refs_0_), channel_id=1, source_target_pairs={{0,2},{1,3},{2,0},{3,1},{4,6},{5,7},{6,4},{7,5},{8,10},{9,11},{10,... | collective-permute-start | bytes 1179656 | tf_op jit(solution)/shard_map/ppermute | solution.py:44
  5.5 1.5 %collective-permute-start.9 = (bf16[256,768]{1,0:T(8,128)(2,1)S(1)}, bf16[256,768]{1,0:T(8,128)(2,1)S(1)}, u32[]{:S(2)}, u32[]{:S(2)}) collective-permute-start(bf16[256,768]{1,0:T(8,128)(2,1)S(1)} %get-tuple-element.11.refs_0_), channel_id=1, source_target_pairs={{0,12},{1,13},{2,14},{3,15},{4,0},{5,1},{6,2},{7,3},{8,4},{9,5},{1... | collective-permute-start | bytes 1179656 | tf_op jit(solution)/shard_map/ppermute | solution.py:44
  6.9 4.6 %prepare.1 = (bf16[1024,768]{1,0:T(8,128)(2,1)S(1)}, f32[64,768]{1,0:T(8,128)S(1)}) custom-call(bf16[768,1024]{1,0:T(8,128)(2,1)} %bitcast.29, bf16[768,1024]{1,0:T(8,128)(2,1)} %bitcast.30, bf16[64,1024]{1,0:T(8,128)(2,1)} %bitcast.34), custom_call_target="tpu_custom_call" | custom-call | tf_op jit(solution)/shard_map/prepare/pallas_call | solution.py:106
  11.6 1.2 %copy-done.1 = bf16[1024,768]{1,0:T(8,128)(2,1)} copy-done((bf16[1024,768]{1,0:T(8,128)(2,1)}, bf16[1024,768]{1,0:T(8,128)(2,1)S(1)}, u32[]{:S(2)}) %copy-start.1) | copy-done | bytes 1572888
  12.8 0.8 collective-permute-done.1.refs_2_.refs_6_
  13.6 1.6 %collective-permute-start.2 = (bf16[256,768]{1,0:T(8,128)(2,1)S(1)}, bf16[256,768]{1,0:T(8,128)(2,1)S(1)}, u32[]{:S(2)}, u32[]{:S(2)}) collective-permute-start(bf16[256,768]{1,0:T(8,128)(2,1)S(1)} %collective-permute-done.refs_0_.refs_2_), channel_id=1, source_target_pairs={{0,4},{1,5},{2,6},{3,7},{4,8},{5,9},{6,10},{7,11},{8,12},{9,13},{1... | collective-permute-start | bytes 1179656 | tf_op jit(solution)/shard_map/ppermute | solution.py:44
  15.2 1.3 %collective-permute-start.6 = (bf16[256,768]{1,0:T(8,128)(2,1)S(1)}, bf16[256,768]{1,0:T(8,128)(2,1)S(1)}, u32[]{:S(2)}, u32[]{:S(2)}) collective-permute-start(bf16[256,768]{1,0:T(8,128)(2,1)S(1)} %collective-permute-done.refs_0_.refs_2_), channel_id=1, source_target_pairs={{0,2},{1,3},{2,0},{3,1},{4,6},{5,7},{6,4},{7,5},{8,10},{9,11},{10,... | collective-permute-start | bytes 1179656 | tf_op jit(solution)/shard_map/ppermute | solution.py:44
  16.5 2.4 %collective-permute-start.8 = (f32[64,768]{1,0:T(8,128)S(1)}, f32[64,768]{1,0:T(8,128)S(1)}, u32[]{:S(2)}, u32[]{:S(2)}) collective-permute-start(f32[64,768]{1,0:T(8,128)S(1)} %get-tuple-element.15.proj_ref), channel_id=1, source_target_pairs={{0,1},{1,0},{2,3},{3,2},{4,5},{5,4},{6,7},{7,6},{8,9},{9,8},{10,11... | collective-permute-start | bytes 589832 | tf_op jit(solution)/shard_map/ppermute | solution.py:44
  18.9 1.3 %collective-permute-done.8.other_ref = f32[64,768]{1,0:T(8,128)S(1)} collective-permute-done((f32[64,768]{1,0:T(8,128)S(1)}, f32[64,768]{1,0:T(8,128)S(1)}, u32[]{:S(2)}, u32[]{:S(2)}) %collective-permute-start.8) | collective-permute-done | bytes 196640 | tf_op jit(solution)/shard_map/ppermute | solution.py:44
  20.2 1.5 %collective-permute-start.4 = (bf16[256,768]{1,0:T(8,128)(2,1)}, bf16[256,768]{1,0:T(8,128)(2,1)}, u32[]{:S(2)}, u32[]{:S(2)}) collective-permute-start(bf16[256,768]{1,0:T(8,128)(2,1)} %collective-permute-done.1.refs_2_.refs_6_), channel_id=1, source_target_pairs={{0,12},{1,13},{2,14},{3,15},{4,0},{5,1},{6,2},{7,3},{8,4},{9,5},{1... | collective-permute-start | bytes 1179656 | tf_op jit(solution)/shard_map/ppermute | solution.py:44
  22.4 1.0 spread_inputs.1
  23.4 2.9 %collective-permute-start.14 = (bf16[256,768]{1,0:T(8,128)(2,1)}, bf16[256,768]{1,0:T(8,128)(2,1)}, u32[]{:S(2)}, u32[]{:S(2)}) collective-permute-start(bf16[256,768]{1,0:T(8,128)(2,1)} %copy-done.8), channel_id=1, source_target_pairs={{0,1},{1,0},{2,3},{3,2},{4,5},{5,4},{6,7},{7,6},{8,9},{9,8},{10,11... | collective-permute-start | bytes 1179656 | tf_op jit(solution)/shard_map/ppermute | solution.py:44
  26.3 0.9 broadcast_select_fusion
  27.7 5.6 %all-to-all-start = ((bf16[16,64,384]{2,1,0:T(8,128)(2,1)}), bf16[16,64,384]{2,1,0:T(8,128)(2,1)S(1)}, u32[]{:S(2)}, u32[]{:S(2)}) async-start(bf16[16,64,384]{2,1,0:T(8,128)(2,1)} %spread_inputs.1), calls=%async_computation | async-start | bytes 1572864 | tf_op jit(solution)/shard_map/all_to_all | solution.py:330
  36.5 11.2 %stage_first.1.refs_12_ = f32[128,768]{1,0:T(8,128)S(1)} custom-call(s32[1]{0:T(128)} %bitcast.core_ref, s32[4]{0:T(128)S(1)} %pad_add_fusion.1.chips_ref, bf16[256,768]{1,0:T(8,128)(2,1)} %copy-done.4, bf16[256,768]{1,0:T(8,128)(2,1)} %collective-permute-done.12.refs_1_, bf16[256,768]{1,0:T(8,128)(2,1)} %copy-done.7, ...), custom_call_target="tpu_custom_call" | custom-call | flops 3422552064 | bytes 3145728 | tf_op jit(solution)/shard_map/stage_first/pallas_call | solution.py:270
  48.5 12.3 %stage_last.1 = f32[16,3,4,128]{3,2,1,0:T(4,128)} custom-call(s32[1]{0:T(128)} %bitcast.core_ref, s32[4]{0:T(128)S(1)} %pad_add_fusion.chips_ref, bf16[256,768]{1,0:T(8,128)(2,1)} %copy-done.5, bf16[256,768]{1,0:T(8,128)(2,1)} %collective-permute-done.3.refs_1_, bf16[256,768]{1,0:T(8,128)(2,1)} %collective-permute-done.4.refs_13_.refs_2_, ...), custom_call_target="tpu_custom_call" | custom-call | flops 3422552064 | bytes 3145728 | tf_op jit(solution)/shard_map/stage_last/pallas_call | solution.py:270
  60.7 5.3 %all-to-all-start.1 = ((f32[16,3,4,128]{3,2,1,0:T(4,128)}), f32[16,3,4,128]{3,2,1,0:T(4,128)S(1)}, u32[]{:S(2)}, u32[]{:S(2)}) async-start(f32[16,3,4,128]{3,2,1,0:T(4,128)} %stage_last.1), calls=%async_computation.1 | async-start | bytes 196608 | tf_op jit(solution)/shard_map/all_to_all | solution.py:350
  66.1 5.8 %all-to-all-done.1 = f32[16,3,4,128]{3,2,1,0:T(4,128)S(1)} async-done(((f32[16,3,4,128]{3,2,1,0:T(4,128)}), f32[16,3,4,128]{3,2,1,0:T(4,128)S(1)}, u32[]{:S(2)}, u32[]{:S(2)}) %all-to-all-start.1) | async-done | bytes 98336 | tf_op jit(solution)/shard_map/all_to_all | solution.py:350
  72.6 10.6 %all-to-all-start.2 = ((f32[16,4,128]{2,1,0:T(4,128)}), f32[16,4,128]{2,1,0:T(4,128)S(1)}, u32[]{:S(2)}, u32[]{:S(2)}) async-start(f32[16,4,128]{2,1,0:T(4,128)} %broadcast_in_dim.13), calls=%async_computation.2 | async-start | bytes 65536 | tf_op jit(solution)/shard_map/all_to_all | solution.py:353
  83.3 9.0 %all-to-all-done.2 = f32[16,4,128]{2,1,0:T(4,128)S(1)} async-done(((f32[16,4,128]{2,1,0:T(4,128)}), f32[16,4,128]{2,1,0:T(4,128)S(1)}, u32[]{:S(2)}, u32[]{:S(2)}) %all-to-all-start.2) | async-done | bytes 32800 | tf_op jit(solution)/shard_map/all_to_all | solution.py:353
  93.3 5.2 %all-to-all-start.3 = ((f32[16,1,128]{2,1,0:T(1,128)}), f32[16,1,128]{2,1,0:T(1,128)S(1)}, u32[]{:S(2)}, u32[]{:S(2)}) async-start(f32[16,1,128]{2,1,0:T(1,128)} %broadcast_in_dim.28), calls=%async_computation.3 | async-start | bytes 16384 | tf_op jit(solution)/shard_map/all_to_all | solution.py:364
  99.2 4.8 %all-to-all-done.3 = f32[16,1,128]{2,1,0:T(1,128)S(1)} async-done(((f32[16,1,128]{2,1,0:T(1,128)}), f32[16,1,128]{2,1,0:T(1,128)S(1)}, u32[]{:S(2)}, u32[]{:S(2)}) %all-to-all-start.3) | async-done | bytes 8224 | tf_op jit(solution)/shard_map/all_to_all | solution.py:364
  (71 shorter events, 8.5 us)
Async XLA Ops:
  0.6 65.4 %copy-start = (f32[2,64,64]{2,1,0:T(8,128)S(1)}, f32[2,64,64]{2,1,0:T(8,128)}, u32[]{:S(2)}) copy-start(f32[2,64,64]{2,1,0:T(8,128)} %param.23) | copy-start | bytes 98308
  2.1 16.8 %copy-start.4 = (bf16[256,768]{1,0:T(8,128)(2,1)}, bf16[256,768]{1,0:T(8,128)(2,1)S(1)}, u32[]{:S(2)}) copy-start(bf16[256,768]{1,0:T(8,128)(2,1)S(1)} %get-tuple-element.11.refs_0_) | copy-start | bytes 1179652
  2.1 10.7 %collective-permute-start = (bf16[256,768]{1,0:T(8,128)(2,1)S(1)}, bf16[256,768]{1,0:T(8,128)(2,1)S(1)}, u32[]{:S(2)}, u32[]{:S(2)}) collective-permute-start(bf16[256,768]{1,0:T(8,128)(2,1)S(1)} %get-tuple-element.11.refs_0_), channel_id=1, source_target_pairs={{0,4},{1,5},{2,6},{3,7},{4,8},{5,9},{6,10},{7,11},{8,12},{9,13},{1... | collective-permute-start | bytes 1179656 | tf_op jit(solution)/shard_map/ppermute | solution.py:44
  4.2 9.4 %collective-permute-start.1 = (bf16[256,768]{1,0:T(8,128)(2,1)S(1)}, bf16[256,768]{1,0:T(8,128)(2,1)}, u32[]{:S(2)}, u32[]{:S(2)}) collective-permute-start(bf16[256,768]{1,0:T(8,128)(2,1)S(1)} %get-tuple-element.11.refs_0_), channel_id=1, source_target_pairs={{0,2},{1,3},{2,0},{3,1},{4,6},{5,7},{6,4},{7,5},{8,10},{9,11},{10,... | collective-permute-start | bytes 1179656 | tf_op jit(solution)/shard_map/ppermute | solution.py:44
  5.5 16.2 %collective-permute-start.9 = (bf16[256,768]{1,0:T(8,128)(2,1)S(1)}, bf16[256,768]{1,0:T(8,128)(2,1)S(1)}, u32[]{:S(2)}, u32[]{:S(2)}) collective-permute-start(bf16[256,768]{1,0:T(8,128)(2,1)S(1)} %get-tuple-element.11.refs_0_), channel_id=1, source_target_pairs={{0,12},{1,13},{2,14},{3,15},{4,0},{5,1},{6,2},{7,3},{8,4},{9,5},{1... | collective-permute-start | bytes 1179656 | tf_op jit(solution)/shard_map/ppermute | solution.py:44
  13.6 9.8 %collective-permute-start.2 = (bf16[256,768]{1,0:T(8,128)(2,1)S(1)}, bf16[256,768]{1,0:T(8,128)(2,1)S(1)}, u32[]{:S(2)}, u32[]{:S(2)}) collective-permute-start(bf16[256,768]{1,0:T(8,128)(2,1)S(1)} %collective-permute-done.refs_0_.refs_2_), channel_id=1, source_target_pairs={{0,4},{1,5},{2,6},{3,7},{4,8},{5,9},{6,10},{7,11},{8,12},{9,13},{1... | collective-permute-start | bytes 1179656 | tf_op jit(solution)/shard_map/ppermute | solution.py:44
  15.2 11.2 %collective-permute-start.6 = (bf16[256,768]{1,0:T(8,128)(2,1)S(1)}, bf16[256,768]{1,0:T(8,128)(2,1)S(1)}, u32[]{:S(2)}, u32[]{:S(2)}) collective-permute-start(bf16[256,768]{1,0:T(8,128)(2,1)S(1)} %collective-permute-done.refs_0_.refs_2_), channel_id=1, source_target_pairs={{0,2},{1,3},{2,0},{3,1},{4,6},{5,7},{6,4},{7,5},{8,10},{9,11},{10,... | collective-permute-start | bytes 1179656 | tf_op jit(solution)/shard_map/ppermute | solution.py:44
  16.5 3.7 %collective-permute-start.8 = (f32[64,768]{1,0:T(8,128)S(1)}, f32[64,768]{1,0:T(8,128)S(1)}, u32[]{:S(2)}, u32[]{:S(2)}) collective-permute-start(f32[64,768]{1,0:T(8,128)S(1)} %get-tuple-element.15.proj_ref), channel_id=1, source_target_pairs={{0,1},{1,0},{2,3},{3,2},{4,5},{5,4},{6,7},{7,6},{8,9},{9,8},{10,11... | collective-permute-start | bytes 589832 | tf_op jit(solution)/shard_map/ppermute | solution.py:44
  18.9 14.4 %collective-permute-start.12 = (bf16[256,768]{1,0:T(8,128)(2,1)S(1)}, bf16[256,768]{1,0:T(8,128)(2,1)}, u32[]{:S(2)}, u32[]{:S(2)}) collective-permute-start(bf16[256,768]{1,0:T(8,128)(2,1)S(1)} %get-tuple-element.11.refs_0_), channel_id=1, source_target_pairs={{0,1},{1,0},{2,3},{3,2},{4,5},{5,4},{6,7},{7,6},{8,9},{9,8},{10,11... | collective-permute-start | bytes 1179656 | tf_op jit(solution)/shard_map/ppermute | solution.py:44
  20.2 13.4 %collective-permute-start.4 = (bf16[256,768]{1,0:T(8,128)(2,1)}, bf16[256,768]{1,0:T(8,128)(2,1)}, u32[]{:S(2)}, u32[]{:S(2)}) collective-permute-start(bf16[256,768]{1,0:T(8,128)(2,1)} %collective-permute-done.1.refs_2_.refs_6_), channel_id=1, source_target_pairs={{0,12},{1,13},{2,14},{3,15},{4,0},{5,1},{6,2},{7,3},{8,4},{9,5},{1... | collective-permute-start | bytes 1179656 | tf_op jit(solution)/shard_map/ppermute | solution.py:44
  21.6 12.4 %collective-permute-start.13 = (bf16[256,768]{1,0:T(8,128)(2,1)S(1)}, bf16[256,768]{1,0:T(8,128)(2,1)}, u32[]{:S(2)}, u32[]{:S(2)}) collective-permute-start(bf16[256,768]{1,0:T(8,128)(2,1)S(1)} %collective-permute-done.refs_0_.refs_2_), channel_id=1, source_target_pairs={{0,1},{1,0},{2,3},{3,2},{4,5},{5,4},{6,7},{7,6},{8,9},{9,8},{10,11... | collective-permute-start | bytes 1179656 | tf_op jit(solution)/shard_map/ppermute | solution.py:44
  23.4 13.1 %copy-start.2 = (bf16[4096,64]{0,1:T(8,128)(2,1)S(1)}, bf16[4096,64]{0,1:T(8,128)(2,1)}, u32[]{:S(2)}) copy-start(bf16[4096,64]{0,1:T(8,128)(2,1)} %param.20) | copy-start | bytes 1572868
  23.4 13.1 %copy-start.3 = (bf16[1024,64]{0,1:T(8,128)(2,1)S(1)}, bf16[1024,64]{0,1:T(8,128)(2,1)}, u32[]{:S(2)}) copy-start(bf16[1024,64]{0,1:T(8,128)(2,1)} %param.18) | copy-start | bytes 393220
  23.4 10.8 %collective-permute-start.14 = (bf16[256,768]{1,0:T(8,128)(2,1)}, bf16[256,768]{1,0:T(8,128)(2,1)}, u32[]{:S(2)}, u32[]{:S(2)}) collective-permute-start(bf16[256,768]{1,0:T(8,128)(2,1)} %copy-done.8), channel_id=1, source_target_pairs={{0,1},{1,0},{2,3},{3,2},{4,5},{5,4},{6,7},{7,6},{8,9},{9,8},{10,11... | collective-permute-start | bytes 1179656 | tf_op jit(solution)/shard_map/ppermute | solution.py:44
  27.2 8.2 %collective-permute-start.10 = (bf16[256,768]{1,0:T(8,128)(2,1)}, bf16[256,768]{1,0:T(8,128)(2,1)}, u32[]{:S(2)}, u32[]{:S(2)}) collective-permute-start(bf16[256,768]{1,0:T(8,128)(2,1)} %broadcast_select_fusion), channel_id=1, source_target_pairs={{0,2},{1,5},{2,0},{3,7},{4,6},{5,9},{6,4},{7,11},{8,10},{9,13},{10... | collective-permute-start | bytes 1179656 | tf_op jit(solution)/shard_map/ppermute | solution.py:44
  27.7 20.1 %all-to-all-start = ((bf16[16,64,384]{2,1,0:T(8,128)(2,1)}), bf16[16,64,384]{2,1,0:T(8,128)(2,1)S(1)}, u32[]{:S(2)}, u32[]{:S(2)}) async-start(bf16[16,64,384]{2,1,0:T(8,128)(2,1)} %spread_inputs.1), calls=%async_computation | async-start | bytes 1572864 | tf_op jit(solution)/shard_map/all_to_all | solution.py:330
  33.3 2.5 %collective-permute-start.15 = (bf16[256,768]{1,0:T(8,128)(2,1)}, bf16[256,768]{1,0:T(8,128)(2,1)S(1)}, u32[]{:S(2)}, u32[]{:S(2)}) collective-permute-start(bf16[256,768]{1,0:T(8,128)(2,1)} %collective-permute-done.1.refs_2_.refs_6_), channel_id=1, source_target_pairs={{0,1},{1,0},{2,3},{3,2},{4,5},{5,4},{6,7},{7,6},{8,9},{9,8},{10,11... | collective-permute-start | bytes 1179656 | tf_op jit(solution)/shard_map/ppermute | solution.py:44
  33.6 14.9 %collective-permute-start.3 = (bf16[256,768]{1,0:T(8,128)(2,1)S(1)}, bf16[256,768]{1,0:T(8,128)(2,1)}, u32[]{:S(2)}, u32[]{:S(2)}) collective-permute-start(bf16[256,768]{1,0:T(8,128)(2,1)S(1)} %collective-permute-done.2.refs_12_.refs_0_), channel_id=1, source_target_pairs={{0,1},{1,0},{2,3},{3,2},{4,5},{5,4},{6,7},{7,6},{8,9},{9,8},{10,11... | collective-permute-start | bytes 1179656 | tf_op jit(solution)/shard_map/ppermute | solution.py:44
  34.1 14.4 %collective-permute-start.7 = (bf16[256,768]{1,0:T(8,128)(2,1)S(1)}, bf16[256,768]{1,0:T(8,128)(2,1)}, u32[]{:S(2)}, u32[]{:S(2)}) collective-permute-start(bf16[256,768]{1,0:T(8,128)(2,1)S(1)} %collective-permute-done.6.refs_14_.refs_4_), channel_id=1, source_target_pairs={{0,1},{1,0},{2,3},{3,2},{4,5},{5,4},{6,7},{7,6},{8,9},{9,8},{10,11... | collective-permute-start | bytes 1179656 | tf_op jit(solution)/shard_map/ppermute | solution.py:44
  34.2 14.3 %collective-permute-start.5 = (bf16[256,768]{1,0:T(8,128)(2,1)}, bf16[256,768]{1,0:T(8,128)(2,1)}, u32[]{:S(2)}, u32[]{:S(2)}) collective-permute-start(bf16[256,768]{1,0:T(8,128)(2,1)} %collective-permute-done.4.refs_13_.refs_2_), channel_id=1, source_target_pairs={{0,1},{1,0},{2,3},{3,2},{4,5},{5,4},{6,7},{7,6},{8,9},{9,8},{10,11... | collective-permute-start | bytes 1179656 | tf_op jit(solution)/shard_map/ppermute | solution.py:44
  35.4 13.1 %collective-permute-start.11 = (bf16[256,768]{1,0:T(8,128)(2,1)}, bf16[256,768]{1,0:T(8,128)(2,1)}, u32[]{:S(2)}, u32[]{:S(2)}) collective-permute-start(bf16[256,768]{1,0:T(8,128)(2,1)} %collective-permute-done.10.refs_6_), channel_id=1, source_target_pairs={{0,1},{1,0},{2,3},{3,2},{4,5},{5,4},{6,7},{7,6},{8,9},{9,8},{10,11... | collective-permute-start | bytes 1179656 | tf_op jit(solution)/shard_map/ppermute | solution.py:44
  60.7 11.2 %all-to-all-start.1 = ((f32[16,3,4,128]{3,2,1,0:T(4,128)}), f32[16,3,4,128]{3,2,1,0:T(4,128)S(1)}, u32[]{:S(2)}, u32[]{:S(2)}) async-start(f32[16,3,4,128]{3,2,1,0:T(4,128)} %stage_last.1), calls=%async_computation.1 | async-start | bytes 196608 | tf_op jit(solution)/shard_map/all_to_all | solution.py:350
  72.6 19.8 %all-to-all-start.2 = ((f32[16,4,128]{2,1,0:T(4,128)}), f32[16,4,128]{2,1,0:T(4,128)S(1)}, u32[]{:S(2)}, u32[]{:S(2)}) async-start(f32[16,4,128]{2,1,0:T(4,128)} %broadcast_in_dim.13), calls=%async_computation.2 | async-start | bytes 65536 | tf_op jit(solution)/shard_map/all_to_all | solution.py:353
  93.3 10.7 %all-to-all-start.3 = ((f32[16,1,128]{2,1,0:T(1,128)}), f32[16,1,128]{2,1,0:T(1,128)S(1)}, u32[]{:S(2)}, u32[]{:S(2)}) async-start(f32[16,1,128]{2,1,0:T(1,128)} %broadcast_in_dim.28), calls=%async_computation.3 | async-start | bytes 16384 | tf_op jit(solution)/shard_map/all_to_all | solution.py:364
  (8 other events, 49.4 us)

commit v3 on v0

v3 whole, which is shorter than its diff:
```python
import jax
import jax.numpy as jnp
from jax import lax
from jax.experimental import pallas as pl
from jax.experimental.pallas import tpu as pltpu
from jax.sharding import PartitionSpec as P

QUERY_DEV = 1
NX, NY, NC = 4, 2, 2
CHIPS = NX * NY
PROJ = 64
LANES = 128
highest = lax.Precision.HIGHEST
epsilon = 1e-06
F32, BF16 = jnp.float32, jnp.bfloat16
VMEM_LIMIT = 24 * 1024 * 1024


def moves(step):
    pairs = []
    for x in range(NX):
        for y in range(NY):
            for c in range(NC):
                tx, ty, tc = step(x, y, c)
                source = (x * NY + y) * NC + c
                target = ((tx % NX) * NY + ty % NY) * NC + tc % NC
                pairs.append((source, target))
    return pairs


X_UP = moves(lambda x, y, c: (x + 1, y, c))
X_DOWN = moves(lambda x, y, c: (x - 1, y, c))
Y_SWAP = moves(lambda x, y, c: (x, y + 1, c))
CORE_SWAP = moves(lambda x, y, c: (x, y, c + 1))
Y_OR_X = moves(lambda x, y, c: (x + c, y + 1 - c, c))

VMEM = pl.BlockSpec(memory_space=pltpu.VMEM)
ANY = pl.BlockSpec(memory_space=pl.ANY)
SMEM = pl.BlockSpec(memory_space=pltpu.SMEM)
PARAMS = pltpu.CompilerParams(vmem_limit_bytes=VMEM_LIMIT)


def send(value, pairs):
    return lax.ppermute(value, "tensor", pairs)


def dot_rows(a, b, precision=None):
    return lax.dot_general(a, b, (((0,), (0,)), ((), ())), precision=precision, preferred_element_type=F32)


def dot_t(a, b, precision=None):
    return lax.dot_general(a, b, (((1,), (1,)), ((), ())), precision=precision, preferred_element_type=F32)


def in_hbm(array):
    return pltpu.with_memory_space_constraint(array, pltpu.HBM)


def in_vmem(array):
    return pltpu.with_memory_space_constraint(array, pltpu.VMEM)


def first(place, flat, inputs, in_basis_t):
    tokens, width = flat.shape

    def body(place_ref, ref, in_ref, basis_ref, own_ref):
        own_ref[:width, :] = ref[...].T
        own_ref[width:, :] = dot_t(basis_ref[...], in_ref[...]).astype(BF16)

    def whole(shape):
        return pl.BlockSpec(shape, lambda i, place_ref: (0, 0))

    shape = (width + PROJ, tokens)
    return pl.pallas_call(
        body,
        grid_spec=pltpu.PrefetchScalarGridSpec(
            num_scalar_prefetch=1,
            grid=(1,),
            in_specs=[
                whole((tokens, width)),
                whole((tokens, width)),
                pl.BlockSpec((PROJ, width), lambda i, place_ref: (0, place_ref[0])),
            ],
            out_specs=whole(shape),
        ),
        out_shape=jax.ShapeDtypeStruct(shape, BF16),
        compiler_params=PARAMS,
        name="first",
    )(place, in_hbm(flat), in_hbm(inputs), in_hbm(in_basis_t))


def prepare(gate, up_out, down_in_basis_t):
    tokens, hidden = gate.shape
    block = tokens // 2

    def body(gate_ref, up_ref, down_ref, g_ref, act_ref):
        raw = gate_ref[...]
        value = raw.astype(F32)
        value = value / (1.0 + jnp.exp(-value))
        activation = (value * up_ref[...].astype(F32)).astype(BF16)
        act_ref[...] = dot_t(down_ref[...], activation)
        g_ref[...] = raw.T

    return pl.pallas_call(
        body,
        grid=(tokens // block,),
        in_specs=[
            pl.BlockSpec((block, hidden), lambda i: (i, 0)),
            pl.BlockSpec((block, hidden), lambda i: (i, 0)),
            pl.BlockSpec((PROJ, hidden), lambda i: (0, 0)),
        ],
        out_specs=(
            pl.BlockSpec((hidden, block), lambda i: (0, i)),
            pl.BlockSpec((PROJ, block), lambda i: (0, i)),
        ),
        out_shape=(
            pltpu.VMEM((hidden, tokens), BF16),
            jax.ShapeDtypeStruct((PROJ, tokens), F32),
        ),
        compiler_params=PARAMS,
        name="prepare",
    )(in_hbm(gate), in_hbm(up_out), in_hbm(down_in_basis_t))


class Stage:
    chunk = 256
    block = 256

    def __init__(self, count, width, hidden, tokens):
        self.count, self.width, self.hidden, self.tokens = count, width, hidden, tokens
        self.steps, self.blocks = hidden // self.chunk, tokens // self.block
        self.depth = NC * count * width
        self.weights_shape = (PROJ + hidden, self.depth)

    def scratch(self):
        pieces = NC * self.count
        return [
            pltpu.VMEM((self.depth, self.tokens), BF16),
            pltpu.VMEM((pieces * PROJ, self.tokens), BF16),
            pltpu.VMEM((self.hidden, self.tokens), BF16),
            pltpu.SemaphoreType.DMA((self.blocks + 1, pieces)),
        ]

    def feature_copies(self, core, refs, cat, proj, sem):
        groups = [[] for _ in range(self.blocks + 1)]
        width, block = self.width, self.block
        for i, ref in enumerate(refs):
            side = core if i % NC == 0 else 1 - core
            row = pl.multiple_of((i // NC * NC + side) * width, width)
            for t in range(self.blocks):
                span = pl.ds(t * block, block)
                target = cat.at[pl.ds(row, width), span]
                groups[t].append(pltpu.make_async_copy(ref.at[pl.ds(0, width), span], target, sem.at[t, i]))
            target = proj.at[pl.ds(i * PROJ, PROJ)]
            source = ref.at[pl.ds(width, PROJ)]
            groups[-1].append(pltpu.make_async_copy(source, target, sem.at[self.blocks, i]))
        return groups

    def weight_copies(self, chips_ref, first_chip, w_hbm, out_hbm, w_ref, sem):
        wide = NC * self.width
        groups = [[] for _ in range(self.steps)]
        for i in range(self.count):
            source = pl.ds(pl.multiple_of(chips_ref[first_chip + i] * wide, wide), wide)
            target = pl.ds(i * wide, wide)
            groups[0].append(
                pltpu.make_async_copy(
                    out_hbm.at[:, source], w_ref.at[pl.ds(0, PROJ), target], sem.at[self.steps, i]
                )
            )
            for step in range(self.steps):
                rows = pl.ds(step * self.chunk, self.chunk)
                to_rows = pl.ds(PROJ + step * self.chunk, self.chunk)
                groups[step].append(
                    pltpu.make_async_copy(w_hbm.at[rows, source], w_ref.at[to_rows, target], sem.at[step, i])
                )
        return groups

    def weight_semaphores(self):
        return pltpu.SemaphoreType.DMA((self.steps + 1, self.count))

    def span(self, t):
        return slice(t * self.block, (t + 1) * self.block)

    def dots(self, step, t, w_ref, g_ref, cat, scaled):
        h, span = step * self.chunk, self.span(t)
        skip = PROJ if step == 0 else 0
        rows = slice(PROJ + h - skip, PROJ + h + self.chunk)
        grad = jnp.dot(w_ref[rows, :], cat[:, span], preferred_element_type=F32)
        gate = g_ref[h : h + self.chunk, span].astype(F32)
        gate = gate / (1.0 + jnp.exp(-gate))
        scaled[h : h + self.chunk, span] = (grad[skip:] * gate).astype(BF16)
        return grad[:skip]

    def projections(self, proj):
        total = proj[:PROJ, :].astype(F32)
        for i in range(1, NC * self.count):
            total = total + proj[i * PROJ : (i + 1) * PROJ, :].astype(F32)
        return total

    def cost(self):
        return pl.CostEstimate(
            flops=2 * self.tokens * self.hidden * (self.depth + LANES),
            bytes_accessed=2 * self.depth * (self.tokens + self.hidden),
            transcendentals=2 * self.tokens * self.hidden,
        )


def start(copies):
    for copy in copies:
        copy.start()


def wait(copies):
    for copy in copies:
        copy.wait()


def middle_stage(core, chips, first_chip, pieces, weights, gates, basis_t, out_basis_t, before=None, next_chips=0):
    count = len(pieces) // NC
    height, tokens = pieces[0].shape
    hidden = gates.shape[0]
    plan = Stage(count, height - PROJ, hidden, tokens)
    follow = Stage(next_chips, height - PROJ, hidden, tokens)

    def body(core_ref, chips_ref, *refs):
        refs = list(refs)
        piece_refs = [refs.pop(0) for _ in pieces]
        w_hbm, out_hbm, g_ref, b_ref = [refs.pop(0) for _ in range(4)]
        before_ref = refs.pop(0) if before is not None else None
        sums = refs.pop(0)
        next_ref = refs.pop(0) if next_chips else None
        cat, proj, scaled, sem, w_ref, w_sem = refs[:6]
        features = plan.feature_copies(core_ref[0], piece_refs, cat, proj, sem)
        columns = plan.weight_copies(chips_ref, first_chip, w_hbm, out_hbm, w_ref, w_sem)
        more = []
        if next_chips:
            more = follow.weight_copies(chips_ref, first_chip + count, w_hbm, out_hbm, next_ref, refs[6])
        groups = [(features[i] if i < plan.blocks else []) + columns[i] for i in range(plan.steps)]
        start(groups[0])
        start(groups[1])
        for i in range(plan.steps):
            wait(groups[i])
            if i + 2 < plan.steps:
                start(groups[i + 2])
            elif i + 2 == plan.steps:
                start(features[-1])
                for group in more:
                    start(group)
            for step in range(i + 1):
                for t in range(min(i + 1, plan.blocks)):
                    if step == i or t == i:
                        down = plan.dots(step, t, w_ref, g_ref, cat, scaled)
                        if step == 0:
                            rows = slice(PROJ, 2 * PROJ)
                            if before_ref is not None:
                                down = down + before_ref[rows, plan.span(t)]
                            sums[rows, plan.span(t)] = down
        for t in range(plan.blocks):
            span = plan.span(t)
            up = jnp.dot(b_ref[...], scaled[:, span], preferred_element_type=F32)
            if before_ref is not None:
                up = up + before_ref[:PROJ, span]
            sums[:PROJ, span] = up
        wait(features[-1])
        total = plan.projections(proj)
        if before_ref is not None:
            total = total + before_ref[2 * PROJ :, :]
        sums[2 * PROJ :, :] = total
        for group in more:
            wait(group)

    operands = [core, chips, *[in_hbm(piece) for piece in pieces], in_hbm(weights), in_hbm(out_basis_t)]
    operands += [in_vmem(gates), basis_t]
    in_specs = [SMEM, SMEM] + [ANY] * (len(pieces) + 2) + [VMEM, VMEM]
    scratch = plan.scratch() + [pltpu.VMEM(plan.weights_shape, BF16), plan.weight_semaphores()]
    out_specs, out_shape = [VMEM], [jax.ShapeDtypeStruct((3 * PROJ, tokens), F32)]
    if before is not None:
        operands.append(before)
        in_specs.append(VMEM)
    if next_chips:
        out_specs.append(VMEM)
        out_shape.append(pltpu.VMEM(follow.weights_shape, BF16))
        scratch.append(follow.weight_semaphores())
    return pl.pallas_call(
        body,
        in_specs=in_specs,
        out_specs=out_specs,
        out_shape=out_shape,
        scratch_shapes=scratch,
        compiler_params=PARAMS,
        cost_estimate=plan.cost(),
        name="middle_stage",
    )(*operands)


def last_stage(core, lengths, pair_weights, pieces, near, weights, gates, basis_t, act, seq_len, devices):
    count = len(pieces) // NC
    height, tokens = pieces[0].shape
    hidden = gates.shape[0]
    plan = Stage(count, height - PROJ, hidden, tokens)
    pair_tokens = 2 * seq_len
    pairs = tokens // pair_tokens
    share = PROJ // devices

    def body(core_ref, lengths_ref, pair_ref, *refs):
        piece_refs, refs = refs[: len(pieces)], refs[len(pieces) :]
        near_ref, w_ref, g_ref, b_ref, act_ref, o_ref, cat, proj, scaled, sem, left, sums = refs
        features = plan.feature_copies(core_ref[0], piece_refs, cat, proj, sem)
        start(features[0])
        start(features[1])
        for t in range(plan.blocks):
            wait(features[t])
            if t + 2 <= plan.blocks:
                start(features[t + 2])
            span = plan.span(t)
            for step in range(plan.steps):
                down = plan.dots(step, t, w_ref, g_ref, cat, scaled)
                if step == 0:
                    sums[PROJ:, span] = down + near_ref[PROJ : 2 * PROJ, span]
            up = jnp.dot(b_ref[...], scaled[:, span], preferred_element_type=F32)
            sums[:PROJ, span] = up + near_ref[:PROJ, span]
        wait(features[-1])
        left[:PROJ, :] = plan.projections(proj) + near_ref[2 * PROJ :, :]
        left[PROJ:, :] = act_ref[...]
        lane = lax.broadcasted_iota(jnp.int32, (1, seq_len), 1)
        for s in range(tokens // seq_len):
            columns = slice(s * seq_len, (s + 1) * seq_len)
            sign = 1.0 if s % 2 == 0 else -1.0
            factor = jnp.where(lane < lengths_ref[s // 2, s % 2], pair_ref[s // 2] * sign, 0.0)
            left[:, columns] = left[:, columns] * factor
        half = lax.broadcasted_iota(jnp.int32, (PROJ, LANES), 1) < PROJ
        for pair in range(pairs):
            span = slice(pair * pair_tokens, (pair + 1) * pair_tokens)
            both = dot_t(left[:, span], sums[:, span], highest)
            grads = jnp.where(half, both[:PROJ], both[PROJ:])
            grads = grads.astype(BF16).reshape(devices, share, LANES)
            for c in range(NC):
                mine = jnp.concatenate([grads[k] for k in range(c, devices, NC)], axis=0)
                for k in range(c, devices, NC):
                    o_ref[k, pair * PROJ // NC : (pair + 1) * PROJ // NC, :] = mine

    return pl.pallas_call(
        body,
        in_specs=[SMEM, SMEM, SMEM] + [ANY] * len(pieces) + [VMEM] * 5,
        out_specs=VMEM,
        out_shape=jax.ShapeDtypeStruct((devices, pairs * PROJ // NC, LANES), BF16),
        scratch_shapes=plan.scratch()
        + [pltpu.VMEM((2 * PROJ, tokens), F32), pltpu.VMEM((2 * PROJ, tokens), F32)],
        compiler_params=PARAMS,
        cost_estimate=plan.cost(),
        name="last_stage",
    )(
        core, lengths, pair_weights, *[in_hbm(piece) for piece in pieces],
        near, in_vmem(weights), in_vmem(gates), basis_t, act,
    )


def shards(
    inputs,
    cotangent,
    gate_pre,
    up_out,
    w_down,
    up_in_basis,
    up_out_basis,
    down_in_basis,
    down_out_basis,
    lengths,
    margins,
    curvature,
):
    pair_count = inputs.shape[0]
    seq_len = inputs.shape[2]
    width = inputs.shape[3]
    hidden = gate_pre.shape[3]
    token_count = pair_count * 2 * seq_len
    train_count = pair_count - QUERY_DEV
    dp_size = lax.axis_size("dp")
    tensor_size = lax.axis_size("tensor")
    row_share = PROJ // tensor_size
    place = lax.axis_index("tensor")
    x, y, core = place // (NY * NC), (place // NC) % NY, place % NC

    own = first(
        place[None],
        cotangent.reshape(token_count, width),
        inputs.reshape(token_count, width),
        up_in_basis.T,
    )
    gates, act = prepare(
        gate_pre.reshape(token_count, hidden),
        up_out.reshape(token_count, hidden),
        down_in_basis.T,
    )
    pair_weights = 1.0 / (1.0 + jnp.exp(margins))

    def chip_at(dx, row):
        return ((x + dx) % NX) * NY + row

    flip = 1 - y
    near_chips = [chip_at(0, y), chip_at(3, y), chip_at(1, y), chip_at(0, flip)]
    far_chips = [chip_at(2, y), chip_at(1, flip), chip_at(3, flip), chip_at(2, flip)]
    chips = jnp.stack(near_chips + far_chips).astype(jnp.int32)
    bases = (up_out_basis.T, down_out_basis.T)

    def with_twins(pieces):
        return [shard for piece in pieces for shard in (piece, send(piece, CORE_SWAP))]

    near = (send(own, X_UP), send(own, X_DOWN), send(own, Y_SWAP))
    (sums,) = middle_stage(core[None], chips, 0, with_twins([own]), w_down, gates, *bases)
    left_own, first_sums = lax.optimization_barrier((near[0], sums))
    right_own, across, sums = lax.optimization_barrier((*near[1:], first_sums))
    near = (left_own, right_own, across)
    x2, pr, pl_ = send(left_own, X_UP), send(across, X_DOWN), send(left_own, Y_SWAP)
    (sums,) = middle_stage(core[None], chips, 1, with_twins(near), w_down, gates, *bases, before=sums)
    third, far, sums = lax.optimization_barrier((jnp.where(core == 0, x2, pl_), (x2, pr, pl_), sums))
    last_hop = send(third, Y_OR_X)
    sums, last_weights = middle_stage(
        core[None], chips, 4, with_twins(far), w_down, gates, *bases, before=sums, next_chips=1
    )
    last_hop, sums = lax.optimization_barrier((last_hop, sums))
    grads = last_stage(
        core[None], lengths, pair_weights, with_twins([last_hop]),
        sums, last_weights, gates, up_out_basis.T, act, seq_len, tensor_size,
    )
    grad_parts = lax.all_to_all(grads, "tensor", 0, 0, tiled=True)
    half_rows = PROJ // NC
    rows = jnp.sum(grad_parts.astype(F32), axis=0).reshape(pair_count, half_rows, LANES)
    train_rows, query_rows = rows[:train_count], rows[train_count:]
    query_all = lax.all_to_all(
        jnp.broadcast_to(query_rows.astype(BF16), (dp_size, half_rows, LANES)), "dp", 0, 0, tiled=True
    )

    own_curvature = lax.dynamic_index_in_dim(
        curvature.reshape(2, tensor_size // NC, NC, row_share, PROJ), core, 2, keepdims=False
    )
    own_curvature = own_curvature.transpose(1, 2, 0, 3).reshape(half_rows, LANES)
    weighted = own_curvature[None] * train_rows
    self_part = jnp.sum(weighted * train_rows, axis=(1, 2))
    cross_part = jnp.sum(query_all.astype(F32)[:, None] * weighted[None], axis=(2, 3))
    sums = jnp.concatenate([cross_part, self_part[None]], axis=0)
    sums = sums + send(sums, CORE_SWAP)
    scores = sums[:dp_size] / jnp.sqrt(sums[dp_size:] + epsilon)
    train_own = lax.dynamic_slice_in_dim(train_rows, place // NC * row_share, row_share, 1)
    train_block = train_own.reshape(train_count, row_share, 2, PROJ).transpose(0, 2, 1, 3)
    return train_block, scores


def solution(mesh):
    return jax.shard_map(
        shards,
        mesh=mesh,
        in_specs=(
            P("dp", None, None, "tensor"),
            P("dp", None, None, "tensor"),
            P("dp", None, None, "tensor"),
            P("dp", None, None, "tensor"),
            P("tensor", None),
            P(),
            P("tensor", None),
            P("tensor", None),
            P(),
            P("dp", None),
            P("dp"),
            P(),
        ),
        out_specs=(P("dp", None, "tensor", None), P(None, "dp")),
        check_vma=False,
    )
```

time: 322 us -> 95.4 us (0.30)
  the two profiles are of different devices: /device:TPU:6 before, /device:TPU:1 now
where the time goes in v3:
time: 95.4 us; the launch traced here: 95 us
  waiting for transfers between devices  31.7 us (33%)
  starting transfers between devices  28.2 us (30%)
  Pallas kernels  27.5 us (29%)
  local copies, waits for them, and re-layouts  5.23 us (5%)
  other arithmetic  1.51 us (2%)
    pallas_call x3, Pallas kernels, middle_stage(): pl.pallas_call(body, in_specs=in_specs, out_specs=out_specs, out_shape=ou...  18 us
    ppermute x16, waiting for transfers between devices, send(): return lax.ppermute(value, 'tensor', pairs)  13.8 us
    ppermute x16, starting transfers between devices, send(): return lax.ppermute(value, 'tensor', pairs)  13.4 us
    all_to_all x1, waiting for transfers between devices, shards(): lax.all_to_all(jnp.broadcast_to(query_rows.astype(BF16), (dp_size, half_r...  9.47 us
    all_to_all x1, starting transfers between devices, shards(): lax.all_to_all(jnp.broadcast_to(query_rows.astype(BF16), (dp_size, half_r...  9.18 us
    all_to_all x1, waiting for transfers between devices, shards(): grad_parts = lax.all_to_all(grads, 'tensor', 0, 0, tiled=True)  8.43 us
    all_to_all x1, starting transfers between devices, shards(): grad_parts = lax.all_to_all(grads, 'tensor', 0, 0, tiled=True)  5.63 us
    pallas_call x1, Pallas kernels, last_stage(): pl.pallas_call(body, in_specs=[SMEM, SMEM, SMEM] + [ANY] * len(pieces) +...  5.05 us
  transfers between devices with their start and end apart: 18, of which 11 were waited for; matrix products, arithmetic and copies ran while one was open for 2% of the time, Pallas kernels for 22%

profile of v3, /device:TPU:1, one launch (start us, length us, event | category | flops | bytes accessed | tf_op | source)
XLA Modules:
  0.0 95.0 jit_solution(18266724563760675302)
XLA Ops:
  0.7 1.4 %first.1.refs_0_ = bf16[320,768]{1,0:T(8,128)(2,1)S(1)} custom-call(s32[1]{0:T(128)} %bitcast.1.place_ref, bf16[768,256]{1,0:T(8,128)(2,1)} %bitcast.40, bf16[768,256]{1,0:T(8,128)(2,1)} %bitcast.41, bf16[64,4096]{1,0:T(8,128)(2,1)} %bitcast.39), custom_call_target="tpu_custom_call" | custom-call | tf_op jit(solution)/shard_map/first/pallas_call | solution.py:74
  2.1 3.3 %collective-permute-start.1 = (bf16[320,768]{1,0:T(8,128)(2,1)S(1)}, bf16[320,768]{1,0:T(8,128)(2,1)S(1)}, u32[]{:S(2)}, u32[]{:S(2)}) collective-permute-start(bf16[320,768]{1,0:T(8,128)(2,1)S(1)} %first.1.refs_0_), channel_id=1, source_target_pairs={{0,1},{1,0},{2,3},{3,2},{4,5},{5,4},{6,7},{7,6},{8,9},{9,8},{10,11... | collective-permute-start | bytes 1474568 | tf_op jit(solution)/shard_map/ppermute | solution.py:44
  5.4 2.7 %collective-permute-start.4 = (bf16[320,768]{1,0:T(8,128)(2,1)S(1)}, bf16[320,768]{1,0:T(8,128)(2,1)}, u32[]{:S(2)}, u32[]{:S(2)}) collective-permute-start(bf16[320,768]{1,0:T(8,128)(2,1)S(1)} %first.1.refs_0_), channel_id=1, source_target_pairs={{0,12},{1,13},{2,14},{3,15},{4,0},{5,1},{6,2},{7,3},{8,4},{9,5},{1... | collective-permute-start | bytes 1474568 | tf_op jit(solution)/shard_map/ppermute | solution.py:44
  8.1 3.0 %prepare.1 = (bf16[1024,768]{1,0:T(8,128)(2,1)S(1)}, f32[64,768]{1,0:T(8,128)S(1)}) custom-call(bf16[768,1024]{1,0:T(8,128)(2,1)} %bitcast.37, bf16[768,1024]{1,0:T(8,128)(2,1)} %bitcast.38, bf16[64,1024]{1,0:T(8,128)(2,1)} %bitcast.44), custom_call_target="tpu_custom_call" | custom-call | tf_op jit(solution)/shard_map/prepare/pallas_call | solution.py:104
  11.9 0.8 copy-done.11
  12.7 4.1 %middle_stage.3.refs_10_ = f32[192,768]{1,0:T(8,128)S(1)} custom-call(s32[1]{0:T(128)} %bitcast.core_ref, s32[8]{0:T(128)S(1)} %stack.35.chips_ref, bf16[320,768]{1,0:T(8,128)(2,1)} %copy-done.2, bf16[320,768]{1,0:T(8,128)(2,1)} %copy-done.11, bf16[1024,4096]{1,0:T(8,128)(2,1)} %refs_6_.3, bf16[64,4096]{1,0:T(8,128)(2,1)} %bitcast.34, ...), custom_call_target="tpu_custom_call" | custom-call | flops 1006632960 | bytes 1835008 | tf_op jit(solution)/shard_map/middle_stage/pallas_call | solution.py:284
  16.8 2.7 %collective-permute-done.refs_0_ = bf16[320,768]{1,0:T(8,128)(2,1)} collective-permute-done((bf16[320,768]{1,0:T(8,128)(2,1)S(1)}, bf16[320,768]{1,0:T(8,128)(2,1)}, u32[]{:S(2)}, u32[]{:S(2)}) %collective-permute-start) | collective-permute-done | bytes 491552 | tf_op jit(solution)/shard_map/ppermute | solution.py:44
  19.5 0.8 collective-permute-done.5.refs_4_
  20.3 1.5 %collective-permute-start.8 = (bf16[320,768]{1,0:T(8,128)(2,1)}, bf16[320,768]{1,0:T(8,128)(2,1)}, u32[]{:S(2)}, u32[]{:S(2)}) collective-permute-start(bf16[320,768]{1,0:T(8,128)(2,1)} %collective-permute-done.4.refs_2_), channel_id=1, source_target_pairs={{0,1},{1,0},{2,3},{3,2},{4,5},{5,4},{6,7},{7,6},{8,9},{9,8},{10,11... | collective-permute-start | bytes 1474568 | tf_op jit(solution)/shard_map/ppermute | solution.py:44
  22.4 1.3 %collective-permute-done.8.refs_3_ = bf16[320,768]{1,0:T(8,128)(2,1)} collective-permute-done((bf16[320,768]{1,0:T(8,128)(2,1)}, bf16[320,768]{1,0:T(8,128)(2,1)}, u32[]{:S(2)}, u32[]{:S(2)}) %collective-permute-start.8) | collective-permute-done | bytes 491552 | tf_op jit(solution)/shard_map/ppermute | solution.py:44
  23.7 1.4 %collective-permute-start.6 = (bf16[320,768]{1,0:T(8,128)(2,1)}, bf16[320,768]{1,0:T(8,128)(2,1)S(1)}, u32[]{:S(2)}, u32[]{:S(2)}) collective-permute-start(bf16[320,768]{1,0:T(8,128)(2,1)} %collective-permute-done.5.refs_4_), channel_id=1, source_target_pairs={{0,12},{1,13},{2,14},{3,15},{4,0},{5,1},{6,2},{7,3},{8,4},{9,5},{1... | collective-permute-start | bytes 1474568 | tf_op jit(solution)/shard_map/ppermute | solution.py:44
  25.1 6.9 %middle_stage.4.refs_10_ = f32[192,768]{1,0:T(8,128)S(1)} custom-call(s32[1]{0:T(128)} %bitcast.core_ref, s32[8]{0:T(128)S(1)} %stack.35.chips_ref, bf16[320,768]{1,0:T(8,128)(2,1)} %collective-permute-done.refs_0_, bf16[320,768]{1,0:T(8,128)(2,1)} %collective-permute-done.7.refs_1_, bf16[320,768]{1,0:T(8,128)(2,1)} %collective-permute-done.4.refs_2_, ...), custom_call_target="tpu_custom_call" | custom-call | flops 2617245696 | bytes 5505024 | tf_op jit(solution)/shard_map/middle_stage/pallas_call | solution.py:284
  32.0 4.6 %collective-permute-done.2.refs_0_ = bf16[320,768]{1,0:T(8,128)(2,1)S(1)} collective-permute-done((bf16[320,768]{1,0:T(8,128)(2,1)}, bf16[320,768]{1,0:T(8,128)(2,1)S(1)}, u32[]{:S(2)}, u32[]{:S(2)}) %collective-permute-start.2) | collective-permute-done | bytes 491552 | tf_op jit(solution)/shard_map/ppermute | solution.py:44
  36.7 0.9 collective-permute-start.11
  38.1 1.0 %collective-permute-done.11.refs_1_ = bf16[320,768]{1,0:T(8,128)(2,1)S(1)} collective-permute-done((bf16[320,768]{1,0:T(8,128)(2,1)S(1)}, bf16[320,768]{1,0:T(8,128)(2,1)S(1)}, u32[]{:S(2)}, u32[]{:S(2)}) %collective-permute-start.11) | collective-permute-done | bytes 491552 | tf_op jit(solution)/shard_map/ppermute | solution.py:44
  41.4 7.0 %middle_stage.5 = (f32[192,768]{1,0:T(8,128)S(1)}, bf16[1088,512]{1,0:T(8,128)(2,1)S(1)}) custom-call(s32[1]{0:T(128)} %bitcast.core_ref, s32[8]{0:T(128)S(1)} %stack.35.chips_ref, bf16[320,768]{1,0:T(8,128)(2,1)} %copy-done.5, bf16[320,768]{1,0:T(8,128)(2,1)} %copy-done.8, bf16[320,768]{1,0:T(8,128)(2,1)} %copy-done.7, bf16[320,768]{1,0:T(8,128)(2,1)} %copy-done.9, ...), custom_call_target="tpu_custom_call" | custom-call | flops 2617245696 | bytes 5505024 | tf_op jit(solution)/shard_map/middle_stage/pallas_call | solution.py:284
  48.9 1.7 %collective-permute-done.14.refs_1_ = bf16[320,768]{1,0:T(8,128)(2,1)} collective-permute-done((bf16[320,768]{1,0:T(8,128)(2,1)}, bf16[320,768]{1,0:T(8,128)(2,1)}, u32[]{:S(2)}, u32[]{:S(2)}) %collective-permute-start.14) | collective-permute-done | bytes 491552 | tf_op jit(solution)/shard_map/ppermute | solution.py:44
  50.7 0.9 copy-done.4
  51.6 5.0 %last_stage.1 = bf16[16,96,128]{2,1,0:T(8,128)(2,1)} custom-call(s32[1]{0:T(128)} %bitcast.core_ref, s32[3,2]{1,0:T(4,128)S(1)} %copy.29.lengths_ref, f32[3]{0:T(128)S(1)} %add_divide_fusion.pair_ref, bf16[320,768]{1,0:T(8,128)(2,1)} %collective-permute-done.10.refs_0_, bf16[320,768]{1,0:T(8,128)(2,1)} %collective-permute-done.14.refs_1_, ...), custom_call_target="tpu_custom_call" | custom-call | flops 1006632960 | bytes 1835008 | tf_op jit(solution)/shard_map/last_stage/pallas_call | solution.py:342
  56.6 5.6 %all-to-all-start = ((bf16[16,96,128]{2,1,0:T(8,128)(2,1)}), bf16[16,96,128]{2,1,0:T(8,128)(2,1)S(1)}, u32[]{:S(2)}, u32[]{:S(2)}) async-start(bf16[16,96,128]{2,1,0:T(8,128)(2,1)} %last_stage.1), calls=%async_computation | async-start | bytes 786432 | tf_op jit(solution)/shard_map/all_to_all | solution.py:426
  62.4 8.4 %all-to-all-done = bf16[16,96,128]{2,1,0:T(8,128)(2,1)S(1)} async-done(((bf16[16,96,128]{2,1,0:T(8,128)(2,1)}), bf16[16,96,128]{2,1,0:T(8,128)(2,1)S(1)}, u32[]{:S(2)}, u32[]{:S(2)}) %all-to-all-start) | async-done | bytes 393248 | tf_op jit(solution)/shard_map/all_to_all | solution.py:426
  71.6 9.2 %all-to-all-start.1 = ((bf16[16,32,128]{2,1,0:T(8,128)(2,1)}), bf16[16,32,128]{2,1,0:T(8,128)(2,1)S(1)}, u32[]{:S(2)}, u32[]{:S(2)}) async-start(bf16[16,32,128]{2,1,0:T(8,128)(2,1)} %broadcast_in_dim.10), calls=%async_computation.1 | async-start | bytes 262144 | tf_op jit(solution)/shard_map/all_to_all | solution.py:430
  81.3 9.5 %all-to-all-done.1 = bf16[16,32,128]{2,1,0:T(8,128)(2,1)S(1)} async-done(((bf16[16,32,128]{2,1,0:T(8,128)(2,1)}), bf16[16,32,128]{2,1,0:T(8,128)(2,1)S(1)}, u32[]{:S(2)}, u32[]{:S(2)}) %all-to-all-start.1) | async-done | bytes 131104 | tf_op jit(solution)/shard_map/all_to_all | solution.py:430
  91.1 2.2 %collective-permute-start.15 = (f32[17,2]{0,1:T(2,128)S(1)}, f32[17,2]{0,1:T(2,128)S(1)}, u32[]{:S(2)}, u32[]{:S(2)}) collective-permute-start(f32[17,2]{0,1:T(2,128)S(1)} %pad_maximum_fusion), channel_id=1, source_target_pairs={{0,1},{1,0},{2,3},{3,2},{4,5},{5,4},{6,7},{7,6},{8,9},{9,8},{10,11... | collective-permute-start | bytes 416 | tf_op jit(solution)/shard_map/ppermute | solution.py:44
  (71 shorter events, 8.2 us)
Async XLA Ops:
  0.6 61.6 %copy-start = (f32[2,64,64]{2,1,0:T(8,128)S(1)}, f32[2,64,64]{2,1,0:T(8,128)}, u32[]{:S(2)}) copy-start(f32[2,64,64]{2,1,0:T(8,128)} %param.23) | copy-start | bytes 98308
  2.1 9.1 %copy-start.2 = (bf16[320,768]{1,0:T(8,128)(2,1)}, bf16[320,768]{1,0:T(8,128)(2,1)S(1)}, u32[]{:S(2)}) copy-start(bf16[320,768]{1,0:T(8,128)(2,1)S(1)} %first.1.refs_0_) | copy-start | bytes 1474564
  2.1 9.8 %collective-permute-start.1 = (bf16[320,768]{1,0:T(8,128)(2,1)S(1)}, bf16[320,768]{1,0:T(8,128)(2,1)S(1)}, u32[]{:S(2)}, u32[]{:S(2)}) collective-permute-start(bf16[320,768]{1,0:T(8,128)(2,1)S(1)} %first.1.refs_0_), channel_id=1, source_target_pairs={{0,1},{1,0},{2,3},{3,2},{4,5},{5,4},{6,7},{7,6},{8,9},{9,8},{10,11... | collective-permute-start | bytes 1474568 | tf_op jit(solution)/shard_map/ppermute | solution.py:44
  5.4 14.1 %collective-permute-start = (bf16[320,768]{1,0:T(8,128)(2,1)S(1)}, bf16[320,768]{1,0:T(8,128)(2,1)}, u32[]{:S(2)}, u32[]{:S(2)}) collective-permute-start(bf16[320,768]{1,0:T(8,128)(2,1)S(1)} %first.1.refs_0_), channel_id=1, source_target_pairs={{0,4},{1,5},{2,6},{3,7},{4,8},{5,9},{6,10},{7,11},{8,12},{9,13},{1... | collective-permute-start | bytes 1474568 | tf_op jit(solution)/shard_map/ppermute | solution.py:44
  5.4 14.1 %collective-permute-start.4 = (bf16[320,768]{1,0:T(8,128)(2,1)S(1)}, bf16[320,768]{1,0:T(8,128)(2,1)}, u32[]{:S(2)}, u32[]{:S(2)}) collective-permute-start(bf16[320,768]{1,0:T(8,128)(2,1)S(1)} %first.1.refs_0_), channel_id=1, source_target_pairs={{0,12},{1,13},{2,14},{3,15},{4,0},{5,1},{6,2},{7,3},{8,4},{9,5},{1... | collective-permute-start | bytes 1474568 | tf_op jit(solution)/shard_map/ppermute | solution.py:44
  8.1 12.2 %collective-permute-start.5 = (bf16[320,768]{1,0:T(8,128)(2,1)S(1)}, bf16[320,768]{1,0:T(8,128)(2,1)}, u32[]{:S(2)}, u32[]{:S(2)}) collective-permute-start(bf16[320,768]{1,0:T(8,128)(2,1)S(1)} %first.1.refs_0_), channel_id=1, source_target_pairs={{0,2},{1,3},{2,0},{3,1},{4,6},{5,7},{6,4},{7,5},{8,10},{9,11},{10,... | collective-permute-start | bytes 1474568 | tf_op jit(solution)/shard_map/ppermute | solution.py:44
  8.1 4.6 %copy-start.1 = (bf16[1024,64]{0,1:T(8,128)(2,1)S(1)}, bf16[1024,64]{0,1:T(8,128)(2,1)}, u32[]{:S(2)}) copy-start(bf16[1024,64]{0,1:T(8,128)(2,1)} %param.18) | copy-start | bytes 393220
  20.3 3.3 %collective-permute-start.8 = (bf16[320,768]{1,0:T(8,128)(2,1)}, bf16[320,768]{1,0:T(8,128)(2,1)}, u32[]{:S(2)}, u32[]{:S(2)}) collective-permute-start(bf16[320,768]{1,0:T(8,128)(2,1)} %collective-permute-done.4.refs_2_), channel_id=1, source_target_pairs={{0,1},{1,0},{2,3},{3,2},{4,5},{5,4},{6,7},{7,6},{8,9},{9,8},{10,11... | collective-permute-start | bytes 1474568 | tf_op jit(solution)/shard_map/ppermute | solution.py:44
  21.8 3.2 %collective-permute-start.9 = (bf16[320,768]{1,0:T(8,128)(2,1)}, bf16[320,768]{1,0:T(8,128)(2,1)}, u32[]{:S(2)}, u32[]{:S(2)}) collective-permute-start(bf16[320,768]{1,0:T(8,128)(2,1)} %collective-permute-done.5.refs_4_), channel_id=1, source_target_pairs={{0,1},{1,0},{2,3},{3,2},{4,5},{5,4},{6,7},{7,6},{8,9},{9,8},{10,11... | collective-permute-start | bytes 1474568 | tf_op jit(solution)/shard_map/ppermute | solution.py:44
  21.8 3.2 %collective-permute-start.7 = (bf16[320,768]{1,0:T(8,128)(2,1)}, bf16[320,768]{1,0:T(8,128)(2,1)}, u32[]{:S(2)}, u32[]{:S(2)}) collective-permute-start(bf16[320,768]{1,0:T(8,128)(2,1)} %collective-permute-done.refs_0_), channel_id=1, source_target_pairs={{0,1},{1,0},{2,3},{3,2},{4,5},{5,4},{6,7},{7,6},{8,9},{9,8},{10,11... | collective-permute-start | bytes 1474568 | tf_op jit(solution)/shard_map/ppermute | solution.py:44
  22.3 14.3 %collective-permute-start.2 = (bf16[320,768]{1,0:T(8,128)(2,1)}, bf16[320,768]{1,0:T(8,128)(2,1)S(1)}, u32[]{:S(2)}, u32[]{:S(2)}) collective-permute-start(bf16[320,768]{1,0:T(8,128)(2,1)} %collective-permute-done.refs_0_), channel_id=1, source_target_pairs={{0,4},{1,5},{2,6},{3,7},{4,8},{5,9},{6,10},{7,11},{8,12},{9,13},{1... | collective-permute-start | bytes 1474568 | tf_op jit(solution)/shard_map/ppermute | solution.py:44
  22.3 14.3 %collective-permute-start.3 = (bf16[320,768]{1,0:T(8,128)(2,1)}, bf16[320,768]{1,0:T(8,128)(2,1)S(1)}, u32[]{:S(2)}, u32[]{:S(2)}) collective-permute-start(bf16[320,768]{1,0:T(8,128)(2,1)} %collective-permute-done.refs_0_), channel_id=1, source_target_pairs={{0,2},{1,3},{2,0},{3,1},{4,6},{5,7},{6,4},{7,5},{8,10},{9,11},{10,... | collective-permute-start | bytes 1474568 | tf_op jit(solution)/shard_map/ppermute | solution.py:44
  23.7 13.0 %collective-permute-start.6 = (bf16[320,768]{1,0:T(8,128)(2,1)}, bf16[320,768]{1,0:T(8,128)(2,1)S(1)}, u32[]{:S(2)}, u32[]{:S(2)}) collective-permute-start(bf16[320,768]{1,0:T(8,128)(2,1)} %collective-permute-done.5.refs_4_), channel_id=1, source_target_pairs={{0,12},{1,13},{2,14},{3,15},{4,0},{5,1},{6,2},{7,3},{8,4},{9,5},{1... | collective-permute-start | bytes 1474568 | tf_op jit(solution)/shard_map/ppermute | solution.py:44
  36.7 12.1 %copy-start.12 = (s32[3,2]{0,1:T(2,128)S(1)}, s32[3,2]{0,1:T(2,128)}, u32[]{:S(2)}) copy-start(s32[3,2]{0,1:T(2,128)} %param.21) | copy-start | bytes 76
  36.7 12.2 %copy-start.13 = (f32[3]{0:T(128)S(1)}, f32[3]{0:T(128)}, u32[]{:S(2)}) copy-start(f32[3]{0:T(128)} %param.22) | copy-start | bytes 40
  36.7 3.8 %copy-start.7 = (bf16[320,768]{1,0:T(8,128)(2,1)}, bf16[320,768]{1,0:T(8,128)(2,1)S(1)}, u32[]{:S(2)}) copy-start(bf16[320,768]{1,0:T(8,128)(2,1)S(1)} %collective-permute-done.6.refs_2_) | copy-start | bytes 1474564
  36.7 2.4 %collective-permute-start.11 = (bf16[320,768]{1,0:T(8,128)(2,1)S(1)}, bf16[320,768]{1,0:T(8,128)(2,1)S(1)}, u32[]{:S(2)}, u32[]{:S(2)}) collective-permute-start(bf16[320,768]{1,0:T(8,128)(2,1)S(1)} %collective-permute-done.2.refs_0_), channel_id=1, source_target_pairs={{0,1},{1,0},{2,3},{3,2},{4,5},{5,4},{6,7},{7,6},{8,9},{9,8},{10,11... | collective-permute-start | bytes 1474568 | tf_op jit(solution)/shard_map/ppermute | solution.py:44
  37.6 2.2 %collective-permute-start.12 = (bf16[320,768]{1,0:T(8,128)(2,1)S(1)}, bf16[320,768]{1,0:T(8,128)(2,1)S(1)}, u32[]{:S(2)}, u32[]{:S(2)}) collective-permute-start(bf16[320,768]{1,0:T(8,128)(2,1)S(1)} %collective-permute-done.6.refs_2_), channel_id=1, source_target_pairs={{0,1},{1,0},{2,3},{3,2},{4,5},{5,4},{6,7},{7,6},{8,9},{9,8},{10,11... | collective-permute-start | bytes 1474568 | tf_op jit(solution)/shard_map/ppermute | solution.py:44
  37.7 2.8 %collective-permute-start.13 = (bf16[320,768]{1,0:T(8,128)(2,1)S(1)}, bf16[320,768]{1,0:T(8,128)(2,1)S(1)}, u32[]{:S(2)}, u32[]{:S(2)}) collective-permute-start(bf16[320,768]{1,0:T(8,128)(2,1)S(1)} %collective-permute-done.3.refs_4_), channel_id=1, source_target_pairs={{0,1},{1,0},{2,3},{3,2},{4,5},{5,4},{6,7},{7,6},{8,9},{9,8},{10,11... | collective-permute-start | bytes 1474568 | tf_op jit(solution)/shard_map/ppermute | solution.py:44
  38.1 10.2 %collective-permute-start.10 = (bf16[320,768]{1,0:T(8,128)(2,1)S(1)}, bf16[320,768]{1,0:T(8,128)(2,1)}, u32[]{:S(2)}, u32[]{:S(2)}) collective-permute-start(bf16[320,768]{1,0:T(8,128)(2,1)S(1)} %broadcast_select_fusion), channel_id=1, source_target_pairs={{0,2},{1,5},{2,0},{3,7},{4,6},{5,9},{6,4},{7,11},{8,10},{9,13},{10... | collective-permute-start | bytes 1474568 | tf_op jit(solution)/shard_map/ppermute | solution.py:44
  48.4 2.3 %collective-permute-start.14 = (bf16[320,768]{1,0:T(8,128)(2,1)}, bf16[320,768]{1,0:T(8,128)(2,1)}, u32[]{:S(2)}, u32[]{:S(2)}) collective-permute-start(bf16[320,768]{1,0:T(8,128)(2,1)} %collective-permute-done.10.refs_0_), channel_id=1, source_target_pairs={{0,1},{1,0},{2,3},{3,2},{4,5},{5,4},{6,7},{7,6},{8,9},{9,8},{10,11... | collective-permute-start | bytes 1474568 | tf_op jit(solution)/shard_map/ppermute | solution.py:44
  56.6 14.2 %all-to-all-start = ((bf16[16,96,128]{2,1,0:T(8,128)(2,1)}), bf16[16,96,128]{2,1,0:T(8,128)(2,1)S(1)}, u32[]{:S(2)}, u32[]{:S(2)}) async-start(bf16[16,96,128]{2,1,0:T(8,128)(2,1)} %last_stage.1), calls=%async_computation | async-start | bytes 786432 | tf_op jit(solution)/shard_map/all_to_all | solution.py:426
  71.6 19.2 %all-to-all-start.1 = ((bf16[16,32,128]{2,1,0:T(8,128)(2,1)}), bf16[16,32,128]{2,1,0:T(8,128)(2,1)S(1)}, u32[]{:S(2)}, u32[]{:S(2)}) async-start(bf16[16,32,128]{2,1,0:T(8,128)(2,1)} %broadcast_in_dim.10), calls=%async_computation.1 | async-start | bytes 262144 | tf_op jit(solution)/shard_map/all_to_all | solution.py:430
  91.1 3.0 %collective-permute-start.15 = (f32[17,2]{0,1:T(2,128)S(1)}, f32[17,2]{0,1:T(2,128)S(1)}, u32[]{:S(2)}, u32[]{:S(2)}) collective-permute-start(f32[17,2]{0,1:T(2,128)S(1)} %pad_maximum_fusion), channel_id=1, source_target_pairs={{0,1},{1,0},{2,3},{3,2},{4,5},{5,4},{6,7},{7,6},{8,9},{9,8},{10,11... | collective-permute-start | bytes 416 | tf_op jit(solution)/shard_map/ppermute | solution.py:44
  (8 other events, 11.7 us)

commit v4 on v3

--- a/solution.py
+++ b/solution.py
@@ -48,8 +48,8 @@
     return lax.dot_general(a, b, (((0,), (0,)), ((), ())), precision=precision, preferred_element_type=F32)
 
 
-def dot_t(a, b, precision=None):
-    return lax.dot_general(a, b, (((1,), (1,)), ((), ())), precision=precision, preferred_element_type=F32)
+def dot_t(a, b):
+    return lax.dot_general(a, b, (((1,), (1,)), ((), ())), preferred_element_type=F32)
 
 
 def in_hbm(array):
@@ -115,7 +115,7 @@
         ),
         out_shape=(
             pltpu.VMEM((hidden, tokens), BF16),
-            jax.ShapeDtypeStruct((PROJ, tokens), F32),
+            pltpu.HBM((PROJ, tokens), F32),
         ),
         compiler_params=PARAMS,
         name="prepare",
@@ -215,12 +215,11 @@
         copy.wait()
 
 
-def middle_stage(core, chips, first_chip, pieces, weights, gates, basis_t, out_basis_t, before=None, next_chips=0):
+def middle_stage(core, chips, first_chip, pieces, weights, gates, basis_t, out_basis_t, before=None):
     count = len(pieces) // NC
     height, tokens = pieces[0].shape
     hidden = gates.shape[0]
     plan = Stage(count, height - PROJ, hidden, tokens)
-    follow = Stage(next_chips, height - PROJ, hidden, tokens)
 
     def body(core_ref, chips_ref, *refs):
         refs = list(refs)
@@ -228,13 +227,9 @@
         w_hbm, out_hbm, g_ref, b_ref = [refs.pop(0) for _ in range(4)]
         before_ref = refs.pop(0) if before is not None else None
         sums = refs.pop(0)
-        next_ref = refs.pop(0) if next_chips else None
         cat, proj, scaled, sem, w_ref, w_sem = refs[:6]
         features = plan.feature_copies(core_ref[0], piece_refs, cat, proj, sem)
         columns = plan.weight_copies(chips_ref, first_chip, w_hbm, out_hbm, w_ref, w_sem)
-        more = []
-        if next_chips:
-            more = follow.weight_copies(chips_ref, first_chip + count, w_hbm, out_hbm, next_ref, refs[6])
         groups = [(features[i] if i < plan.blocks else []) + columns[i] for i in range(plan.steps)]
         start(groups[0])
         start(groups[1])
@@ -244,8 +239,6 @@
                 start(groups[i + 2])
             elif i + 2 == plan.steps:
                 start(features[-1])
-                for group in more:
-                    start(group)
             for step in range(i + 1):
                 for t in range(min(i + 1, plan.blocks)):
                     if step == i or t == i:
@@ -266,26 +259,19 @@
         if before_ref is not None:
             total = total + before_ref[2 * PROJ :, :]
         sums[2 * PROJ :, :] = total
-        for group in more:
-            wait(group)
-
-    operands = [core, chips, *[in_hbm(piece) for piece in pieces], in_hbm(weights), in_hbm(out_basis_t)]
+
+    operands = [core, chips, *pieces, in_hbm(weights), in_hbm(out_basis_t)]
     operands += [in_vmem(gates), basis_t]
     in_specs = [SMEM, SMEM] + [ANY] * (len(pieces) + 2) + [VMEM, VMEM]
     scratch = plan.scratch() + [pltpu.VMEM(plan.weights_shape, BF16), plan.weight_semaphores()]
-    out_specs, out_shape = [VMEM], [jax.ShapeDtypeStruct((3 * PROJ, tokens), F32)]
     if before is not None:
         operands.append(before)
         in_specs.append(VMEM)
-    if next_chips:
-        out_specs.append(VMEM)
-        out_shape.append(pltpu.VMEM(follow.weights_shape, BF16))
-        scratch.append(follow.weight_semaphores())
     return pl.pallas_call(
         body,
         in_specs=in_specs,
-        out_specs=out_specs,
-        out_shape=out_shape,
+        out_specs=VMEM,
+        out_shape=jax.ShapeDtypeStruct((3 * PROJ, tokens), F32),
         scratch_shapes=scratch,
         compiler_params=PARAMS,
         cost_estimate=plan.cost(),
@@ -293,7 +279,9 @@
     )(*operands)
 
 
-def last_stage(core, lengths, pair_weights, pieces, near, weights, gates, basis_t, act, seq_len, devices):
+def last_stage(
+    core, chips, first_chip, lengths, pair_weights, pieces, before, weights, gates, basis_t, out_basis_t, act, seq_len, devices
+):
     count = len(pieces) // NC
     height, tokens = pieces[0].shape
     hidden = gates.shape[0]
@@ -302,26 +290,32 @@
     pairs = tokens // pair_tokens
     share = PROJ // devices
 
-    def body(core_ref, lengths_ref, pair_ref, *refs):
+    def body(core_ref, chips_ref, lengths_ref, pair_ref, *refs):
         piece_refs, refs = refs[: len(pieces)], refs[len(pieces) :]
-        near_ref, w_ref, g_ref, b_ref, act_ref, o_ref, cat, proj, scaled, sem, left, sums = refs
+        before_ref, w_hbm, out_hbm, g_ref, b_ref, act_ref, o_ref = refs[:7]
+        cat, proj, scaled, sem, left, sums, act_sem, w_ref, w_sem = refs[7:]
+        columns = plan.weight_copies(chips_ref, first_chip, w_hbm, out_hbm, w_ref, w_sem)
         features = plan.feature_copies(core_ref[0], piece_refs, cat, proj, sem)
+        act_copy = pltpu.make_async_copy(act_ref, left.at[pl.ds(PROJ, PROJ)], act_sem)
         start(features[0])
-        start(features[1])
+        for group in columns:
+            start(group)
+        start(features[1] + [act_copy])
         for t in range(plan.blocks):
             wait(features[t])
             if t + 2 <= plan.blocks:
                 start(features[t + 2])
             span = plan.span(t)
             for step in range(plan.steps):
+                if t == 0:
+                    wait(columns[step])
                 down = plan.dots(step, t, w_ref, g_ref, cat, scaled)
                 if step == 0:
-                    sums[PROJ:, span] = down + near_ref[PROJ : 2 * PROJ, span]
+                    sums[PROJ:, span] = down + before_ref[PROJ : 2 * PROJ, span]
             up = jnp.dot(b_ref[...], scaled[:, span], preferred_element_type=F32)
-            sums[:PROJ, span] = up + near_ref[:PROJ, span]
-        wait(features[-1])
-        left[:PROJ, :] = plan.projections(proj) + near_ref[2 * PROJ :, :]
-        left[PROJ:, :] = act_ref[...]
+            sums[:PROJ, span] = up + before_ref[:PROJ, span]
+        wait(features[-1] + [act_copy])
+        left[:PROJ, :] = plan.projections(proj) + before_ref[2 * PROJ :, :]
         lane = lax.broadcasted_iota(jnp.int32, (1, seq_len), 1)
         for s in range(tokens // seq_len):
             columns = slice(s * seq_len, (s + 1) * seq_len)
@@ -331,27 +325,33 @@
         half = lax.broadcasted_iota(jnp.int32, (PROJ, LANES), 1) < PROJ
         for pair in range(pairs):
             span = slice(pair * pair_tokens, (pair + 1) * pair_tokens)
-            both = dot_t(left[:, span], sums[:, span], highest)
+            a, b = left[:, span], sums[:, span]
+            a_high, b_high = a.astype(BF16), b.astype(BF16)
+            a_low, b_low = (a - a_high.astype(F32)).astype(BF16), (b - b_high.astype(F32)).astype(BF16)
+            both = dot_t(
+                jnp.concatenate([a_high, a_high, a_low], axis=1), jnp.concatenate([b_high, b_low, b_high], axis=1)
+            )
             grads = jnp.where(half, both[:PROJ], both[PROJ:])
-            grads = grads.astype(BF16).reshape(devices, share, LANES)
             for c in range(NC):
-                mine = jnp.concatenate([grads[k] for k in range(c, devices, NC)], axis=0)
+                blocks = [grads[k * share : (k + 1) * share] for k in range(c, devices, NC)]
+                mine = jnp.concatenate(blocks, axis=0).astype(BF16)
                 for k in range(c, devices, NC):
                     o_ref[k, pair * PROJ // NC : (pair + 1) * PROJ // NC, :] = mine
 
     return pl.pallas_call(
         body,
-        in_specs=[SMEM, SMEM, SMEM] + [ANY] * len(pieces) + [VMEM] * 5,
+        in_specs=[SMEM] * 4 + [ANY] * len(pieces) + [VMEM, ANY, ANY, VMEM, VMEM, ANY],
         out_specs=VMEM,
         out_shape=jax.ShapeDtypeStruct((devices, pairs * PROJ // NC, LANES), BF16),
         scratch_shapes=plan.scratch()
-        + [pltpu.VMEM((2 * PROJ, tokens), F32), pltpu.VMEM((2 * PROJ, tokens), F32)],
+        + [pltpu.VMEM((2 * PROJ, tokens), F32), pltpu.VMEM((2 * PROJ, tokens), F32), pltpu.SemaphoreType.DMA]
+        + [pltpu.VMEM(plan.weights_shape, BF16), plan.weight_semaphores()],
         compiler_params=PARAMS,
         cost_estimate=plan.cost(),
         name="last_stage",
     )(
-        core, lengths, pair_weights, *[in_hbm(piece) for piece in pieces],
-        near, in_vmem(weights), in_vmem(gates), basis_t, act,
+        core, chips, lengths, pair_weights, *pieces,
+        before, in_hbm(weights), in_hbm(out_basis_t), in_vmem(gates), basis_t, in_hbm(act),
     )
 
 
@@ -407,21 +407,19 @@
         return [shard for piece in pieces for shard in (piece, send(piece, CORE_SWAP))]
 
     near = (send(own, X_UP), send(own, X_DOWN), send(own, Y_SWAP))
-    (sums,) = middle_stage(core[None], chips, 0, with_twins([own]), w_down, gates, *bases)
+    sums = middle_stage(core[None], chips, 0, with_twins([own]), w_down, gates, *bases)
     left_own, first_sums = lax.optimization_barrier((near[0], sums))
     right_own, across, sums = lax.optimization_barrier((*near[1:], first_sums))
     near = (left_own, right_own, across)
     x2, pr, pl_ = send(left_own, X_UP), send(across, X_DOWN), send(left_own, Y_SWAP)
-    (sums,) = middle_stage(core[None], chips, 1, with_twins(near), w_down, gates, *bases, before=sums)
+    sums = middle_stage(core[None], chips, 1, with_twins(near), w_down, gates, *bases, before=sums)
     third, far, sums = lax.optimization_barrier((jnp.where(core == 0, x2, pl_), (x2, pr, pl_), sums))
     last_hop = send(third, Y_OR_X)
-    sums, last_weights = middle_stage(
-        core[None], chips, 4, with_twins(far), w_down, gates, *bases, before=sums, next_chips=1
-    )
+    sums = middle_stage(core[None], chips, 4, with_twins(far), w_down, gates, *bases, before=sums)
     last_hop, sums = lax.optimization_barrier((last_hop, sums))
     grads = last_stage(
-        core[None], lengths, pair_weights, with_twins([last_hop]),
-        sums, last_weights, gates, up_out_basis.T, act, seq_len, tensor_size,
+        core[None], chips, 7, lengths, pair_weights, with_twins([last_hop]),
+        sums, w_down, gates, *bases, act, seq_len, tensor_size,
     )
     grad_parts = lax.all_to_all(grads, "tensor", 0, 0, tiled=True)
     half_rows = PROJ // NC

time: 95.4 us -> 94.4 us (0.990)
  local copies, waits for them, and re-layouts: 5.23 us -> 1.95 us
  Pallas kernels: 27.5 us -> 29.1 us
    unnamed x30 -> x10, local copies, waits for them, and re-layouts: 3.99 us -> 0.72 us
    pallas_call x4, Pallas kernels: 23 us -> 24.1 us  [the longest x3 18.4 us: middle_stage(): pl.pallas_call(body, in_specs=in_specs, out_specs=VMEM, out_shape=jax.Sha...]
  transfers between devices with their start and end apart: 18 -> 18, of which waited for: 11 -> 11; matrix products, arithmetic and copies ran while one was open for 2% -> 2% of each run, Pallas kernels for 22% -> 23%
where the time goes in v4:
time: 94.4 us; the launch traced here: 94.1 us
  waiting for transfers between devices  32.5 us (34%)
  Pallas kernels  29.1 us (31%)
  starting transfers between devices  28.2 us (30%)
  local copies, waits for them, and re-layouts  1.95 us (2%)
  other arithmetic  1.51 us (2%)
    pallas_call x3, Pallas kernels, middle_stage(): pl.pallas_call(body, in_specs=in_specs, out_specs=VMEM, out_shape=jax.Sha...  18.4 us
    ppermute x16, waiting for transfers between devices, send(): return lax.ppermute(value, 'tensor', pairs)  14.6 us
    ppermute x16, starting transfers between devices, send(): return lax.ppermute(value, 'tensor', pairs)  13.4 us
    all_to_all x1, waiting for transfers between devices, shards(): lax.all_to_all(jnp.broadcast_to(query_rows.astype(BF16), (dp_size, half_r...  9.47 us
    all_to_all x1, starting transfers between devices, shards(): lax.all_to_all(jnp.broadcast_to(query_rows.astype(BF16), (dp_size, half_r...  9.18 us
    all_to_all x1, waiting for transfers between devices, shards(): grad_parts = lax.all_to_all(grads, 'tensor', 0, 0, tiled=True)  8.43 us
    pallas_call x1, Pallas kernels, last_stage(): pl.pallas_call(body, in_specs=[SMEM] * 4 + [ANY] * len(pieces) + [VMEM, A...  5.65 us
    all_to_all x1, starting transfers between devices, shards(): grad_parts = lax.all_to_all(grads, 'tensor', 0, 0, tiled=True)  5.64 us
  transfers between devices with their start and end apart: 18, of which 11 were waited for; matrix products, arithmetic and copies ran while one was open for 2% of the time, Pallas kernels for 23%

profile of v4, /device:TPU:1, one launch (start us, length us, event | category | flops | bytes accessed | tf_op | source)
XLA Modules:
  0.0 94.1 jit_solution(7899617195787318608)
XLA Ops:
  0.7 1.4 %first.1.refs_0_ = bf16[320,768]{1,0:T(8,128)(2,1)S(1)} custom-call(s32[1]{0:T(128)} %bitcast.9.place_ref, bf16[768,256]{1,0:T(8,128)(2,1)} %bitcast.41, bf16[768,256]{1,0:T(8,128)(2,1)} %bitcast.42, bf16[64,4096]{1,0:T(8,128)(2,1)} %bitcast.40), custom_call_target="tpu_custom_call" | custom-call | tf_op jit(solution)/shard_map/first/pallas_call | solution.py:74
  2.1 3.3 %collective-permute-start.1 = (bf16[320,768]{1,0:T(8,128)(2,1)S(1)}, bf16[320,768]{1,0:T(8,128)(2,1)S(1)}, u32[]{:S(2)}, u32[]{:S(2)}) collective-permute-start(bf16[320,768]{1,0:T(8,128)(2,1)S(1)} %first.1.refs_0_), channel_id=1, source_target_pairs={{0,1},{1,0},{2,3},{3,2},{4,5},{5,4},{6,7},{7,6},{8,9},{9,8},{10,11... | collective-permute-start | bytes 1474568 | tf_op jit(solution)/shard_map/ppermute | solution.py:44
  5.4 2.7 %collective-permute-start.4 = (bf16[320,768]{1,0:T(8,128)(2,1)S(1)}, bf16[320,768]{1,0:T(8,128)(2,1)}, u32[]{:S(2)}, u32[]{:S(2)}) collective-permute-start(bf16[320,768]{1,0:T(8,128)(2,1)S(1)} %first.1.refs_0_), channel_id=1, source_target_pairs={{0,12},{1,13},{2,14},{3,15},{4,0},{5,1},{6,2},{7,3},{8,4},{9,5},{1... | collective-permute-start | bytes 1474568 | tf_op jit(solution)/shard_map/ppermute | solution.py:44
  8.1 3.6 %prepare.1 = (bf16[1024,768]{1,0:T(8,128)(2,1)S(1)}, f32[64,768]{1,0:T(8,128)}) custom-call(bf16[768,1024]{1,0:T(8,128)(2,1)} %bitcast.38, bf16[768,1024]{1,0:T(8,128)(2,1)} %bitcast.39, bf16[64,1024]{1,0:T(8,128)(2,1)} %bitcast.45), custom_call_target="tpu_custom_call" | custom-call | tf_op jit(solution)/shard_map/prepare/pallas_call | solution.py:104
  11.8 4.1 %middle_stage.3.refs_10_ = f32[192,768]{1,0:T(8,128)S(1)} custom-call(s32[1]{0:T(128)} %bitcast.core_ref, s32[8]{0:T(128)S(1)} %stack.35.chips_ref, bf16[320,768]{1,0:T(8,128)(2,1)S(1)} %first.1.refs_0_, bf16[320,768]{1,0:T(8,128)(2,1)S(1)} %collective-permute-done.1.refs_1_, bf16[1024,4096]{1,0:T(8,128)(2,1)} %refs_3_.1, bf16[64,4096]{1,0:T(8,128)(2,1)} %bitcast.34, ...), custom_call_target="tpu_custom_call" | custom-call | flops 1006632960 | bytes 1835008 | tf_op jit(solution)/shard_map/middle_stage/pallas_call | solution.py:270
  15.9 3.6 %collective-permute-done.refs_0_ = bf16[320,768]{1,0:T(8,128)(2,1)} collective-permute-done((bf16[320,768]{1,0:T(8,128)(2,1)S(1)}, bf16[320,768]{1,0:T(8,128)(2,1)}, u32[]{:S(2)}, u32[]{:S(2)}) %collective-permute-start) | collective-permute-done | bytes 491552 | tf_op jit(solution)/shard_map/ppermute | solution.py:44
  19.5 0.8 collective-permute-done.5.refs_4_
  20.3 1.5 %collective-permute-start.8 = (bf16[320,768]{1,0:T(8,128)(2,1)}, bf16[320,768]{1,0:T(8,128)(2,1)}, u32[]{:S(2)}, u32[]{:S(2)}) collective-permute-start(bf16[320,768]{1,0:T(8,128)(2,1)} %collective-permute-done.4.refs_2_), channel_id=1, source_target_pairs={{0,1},{1,0},{2,3},{3,2},{4,5},{5,4},{6,7},{7,6},{8,9},{9,8},{10,11... | collective-permute-start | bytes 1474568 | tf_op jit(solution)/shard_map/ppermute | solution.py:44
  22.3 1.3 %collective-permute-done.8.refs_3_ = bf16[320,768]{1,0:T(8,128)(2,1)} collective-permute-done((bf16[320,768]{1,0:T(8,128)(2,1)}, bf16[320,768]{1,0:T(8,128)(2,1)}, u32[]{:S(2)}, u32[]{:S(2)}) %collective-permute-start.8) | collective-permute-done | bytes 491552 | tf_op jit(solution)/shard_map/ppermute | solution.py:44
  23.7 1.4 %collective-permute-start.6 = (bf16[320,768]{1,0:T(8,128)(2,1)}, bf16[320,768]{1,0:T(8,128)(2,1)S(1)}, u32[]{:S(2)}, u32[]{:S(2)}) collective-permute-start(bf16[320,768]{1,0:T(8,128)(2,1)} %collective-permute-done.5.refs_4_), channel_id=1, source_target_pairs={{0,12},{1,13},{2,14},{3,15},{4,0},{5,1},{6,2},{7,3},{8,4},{9,5},{1... | collective-permute-start | bytes 1474568 | tf_op jit(solution)/shard_map/ppermute | solution.py:44
  25.1 6.9 %middle_stage.4.refs_10_ = f32[192,768]{1,0:T(8,128)S(1)} custom-call(s32[1]{0:T(128)} %bitcast.core_ref, s32[8]{0:T(128)S(1)} %stack.35.chips_ref, bf16[320,768]{1,0:T(8,128)(2,1)} %collective-permute-done.refs_0_, bf16[320,768]{1,0:T(8,128)(2,1)} %collective-permute-done.7.refs_1_, bf16[320,768]{1,0:T(8,128)(2,1)} %collective-permute-done.4.refs_2_, ...), custom_call_target="tpu_custom_call" | custom-call | flops 2617245696 | bytes 5505024 | tf_op jit(solution)/shard_map/middle_stage/pallas_call | solution.py:270
  32.0 4.6 %collective-permute-done.2.refs_0_ = bf16[320,768]{1,0:T(8,128)(2,1)S(1)} collective-permute-done((bf16[320,768]{1,0:T(8,128)(2,1)}, bf16[320,768]{1,0:T(8,128)(2,1)S(1)}, u32[]{:S(2)}, u32[]{:S(2)}) %collective-permute-start.2) | collective-permute-done | bytes 491552 | tf_op jit(solution)/shard_map/ppermute | solution.py:44
  36.7 0.9 collective-permute-start.11
  38.1 1.0 %collective-permute-done.11.refs_1_ = bf16[320,768]{1,0:T(8,128)(2,1)S(1)} collective-permute-done((bf16[320,768]{1,0:T(8,128)(2,1)S(1)}, bf16[320,768]{1,0:T(8,128)(2,1)S(1)}, u32[]{:S(2)}, u32[]{:S(2)}) %collective-permute-start.11) | collective-permute-done | bytes 491552 | tf_op jit(solution)/shard_map/ppermute | solution.py:44
  39.1 0.7 collective-permute-done.12.refs_3_
  39.8 0.7 collective-permute-done.13.refs_5_
  40.5 7.4 %middle_stage.5.refs_2_ = f32[192,768]{1,0:T(8,128)S(1)} custom-call(s32[1]{0:T(128)} %bitcast.core_ref, s32[8]{0:T(128)S(1)} %stack.35.chips_ref, bf16[320,768]{1,0:T(8,128)(2,1)S(1)} %collective-permute-done.2.refs_0_, bf16[320,768]{1,0:T(8,128)(2,1)S(1)} %collective-permute-done.11.refs_1_, bf16[320,768]{1,0:T(8,128)(2,1)S(1)} %collective-permute-done.6.refs_2_, ...), custom_call_target="tpu_custom_call" | custom-call | flops 2617245696 | bytes 5505024 | tf_op jit(solution)/shard_map/middle_stage/pallas_call | solution.py:270
  48.5 1.6 %collective-permute-done.14.refs_1_ = bf16[320,768]{1,0:T(8,128)(2,1)S(1)} collective-permute-done((bf16[320,768]{1,0:T(8,128)(2,1)}, bf16[320,768]{1,0:T(8,128)(2,1)S(1)}, u32[]{:S(2)}, u32[]{:S(2)}) %collective-permute-start.14) | collective-permute-done | bytes 491552 | tf_op jit(solution)/shard_map/ppermute | solution.py:44
  50.0 5.6 %last_stage.1 = bf16[16,96,128]{2,1,0:T(8,128)(2,1)} custom-call(s32[1]{0:T(128)} %bitcast.core_ref, s32[8]{0:T(128)S(1)} %stack.35.chips_ref, s32[3,2]{1,0:T(4,128)S(1)} %copy.29.lengths_ref, f32[3]{0:T(128)S(1)} %add_divide_fusion.pair_ref, bf16[320,768]{1,0:T(8,128)(2,1)} %collective-permute-done.10.refs_0_, ...), custom_call_target="tpu_custom_call" | custom-call | flops 1006632960 | bytes 1835008 | tf_op jit(solution)/shard_map/last_stage/pallas_call | solution.py:341
  55.7 5.6 %all-to-all-start = ((bf16[16,96,128]{2,1,0:T(8,128)(2,1)}), bf16[16,96,128]{2,1,0:T(8,128)(2,1)S(1)}, u32[]{:S(2)}, u32[]{:S(2)}) async-start(bf16[16,96,128]{2,1,0:T(8,128)(2,1)} %last_stage.1), calls=%async_computation | async-start | bytes 786432 | tf_op jit(solution)/shard_map/all_to_all | solution.py:424
  61.5 8.4 %all-to-all-done = bf16[16,96,128]{2,1,0:T(8,128)(2,1)S(1)} async-done(((bf16[16,96,128]{2,1,0:T(8,128)(2,1)}), bf16[16,96,128]{2,1,0:T(8,128)(2,1)S(1)}, u32[]{:S(2)}, u32[]{:S(2)}) %all-to-all-start) | async-done | bytes 393248 | tf_op jit(solution)/shard_map/all_to_all | solution.py:424
  70.6 9.2 %all-to-all-start.1 = ((bf16[16,32,128]{2,1,0:T(8,128)(2,1)}), bf16[16,32,128]{2,1,0:T(8,128)(2,1)S(1)}, u32[]{:S(2)}, u32[]{:S(2)}) async-start(bf16[16,32,128]{2,1,0:T(8,128)(2,1)} %broadcast_in_dim.10), calls=%async_computation.1 | async-start | bytes 262144 | tf_op jit(solution)/shard_map/all_to_all | solution.py:428
  80.4 9.5 %all-to-all-done.1 = bf16[16,32,128]{2,1,0:T(8,128)(2,1)S(1)} async-done(((bf16[16,32,128]{2,1,0:T(8,128)(2,1)}), bf16[16,32,128]{2,1,0:T(8,128)(2,1)S(1)}, u32[]{:S(2)}, u32[]{:S(2)}) %all-to-all-start.1) | async-done | bytes 131104 | tf_op jit(solution)/shard_map/all_to_all | solution.py:428
  90.2 2.2 %collective-permute-start.15 = (f32[17,2]{0,1:T(2,128)S(1)}, f32[17,2]{0,1:T(2,128)S(1)}, u32[]{:S(2)}, u32[]{:S(2)}) collective-permute-start(f32[17,2]{0,1:T(2,128)S(1)} %pad_maximum_fusion), channel_id=1, source_target_pairs={{0,1},{1,0},{2,3},{3,2},{4,5},{5,4},{6,7},{7,6},{8,9},{9,8},{10,11... | collective-permute-start | bytes 416 | tf_op jit(solution)/shard_map/ppermute | solution.py:44
  (51 shorter events, 5.2 us)
Async XLA Ops:
  0.6 60.7 %copy-start = (f32[2,64,64]{2,1,0:T(8,128)S(1)}, f32[2,64,64]{2,1,0:T(8,128)}, u32[]{:S(2)}) copy-start(f32[2,64,64]{2,1,0:T(8,128)} %param.23) | copy-start | bytes 98308
  2.1 9.7 %collective-permute-start.1 = (bf16[320,768]{1,0:T(8,128)(2,1)S(1)}, bf16[320,768]{1,0:T(8,128)(2,1)S(1)}, u32[]{:S(2)}, u32[]{:S(2)}) collective-permute-start(bf16[320,768]{1,0:T(8,128)(2,1)S(1)} %first.1.refs_0_), channel_id=1, source_target_pairs={{0,1},{1,0},{2,3},{3,2},{4,5},{5,4},{6,7},{7,6},{8,9},{9,8},{10,11... | collective-permute-start | bytes 1474568 | tf_op jit(solution)/shard_map/ppermute | solution.py:44
  5.4 14.1 %collective-permute-start = (bf16[320,768]{1,0:T(8,128)(2,1)S(1)}, bf16[320,768]{1,0:T(8,128)(2,1)}, u32[]{:S(2)}, u32[]{:S(2)}) collective-permute-start(bf16[320,768]{1,0:T(8,128)(2,1)S(1)} %first.1.refs_0_), channel_id=1, source_target_pairs={{0,4},{1,5},{2,6},{3,7},{4,8},{5,9},{6,10},{7,11},{8,12},{9,13},{1... | collective-permute-start | bytes 1474568 | tf_op jit(solution)/shard_map/ppermute | solution.py:44
  5.4 14.1 %collective-permute-start.4 = (bf16[320,768]{1,0:T(8,128)(2,1)S(1)}, bf16[320,768]{1,0:T(8,128)(2,1)}, u32[]{:S(2)}, u32[]{:S(2)}) collective-permute-start(bf16[320,768]{1,0:T(8,128)(2,1)S(1)} %first.1.refs_0_), channel_id=1, source_target_pairs={{0,12},{1,13},{2,14},{3,15},{4,0},{5,1},{6,2},{7,3},{8,4},{9,5},{1... | collective-permute-start | bytes 1474568 | tf_op jit(solution)/shard_map/ppermute | solution.py:44
  8.1 12.2 %collective-permute-start.5 = (bf16[320,768]{1,0:T(8,128)(2,1)S(1)}, bf16[320,768]{1,0:T(8,128)(2,1)}, u32[]{:S(2)}, u32[]{:S(2)}) collective-permute-start(bf16[320,768]{1,0:T(8,128)(2,1)S(1)} %first.1.refs_0_), channel_id=1, source_target_pairs={{0,2},{1,3},{2,0},{3,1},{4,6},{5,7},{6,4},{7,5},{8,10},{9,11},{10,... | collective-permute-start | bytes 1474568 | tf_op jit(solution)/shard_map/ppermute | solution.py:44
  8.1 3.7 %copy-start.1 = (bf16[1024,64]{0,1:T(8,128)(2,1)S(1)}, bf16[1024,64]{0,1:T(8,128)(2,1)}, u32[]{:S(2)}) copy-start(bf16[1024,64]{0,1:T(8,128)(2,1)} %param.18) | copy-start | bytes 393220
  20.3 3.3 %collective-permute-start.8 = (bf16[320,768]{1,0:T(8,128)(2,1)}, bf16[320,768]{1,0:T(8,128)(2,1)}, u32[]{:S(2)}, u32[]{:S(2)}) collective-permute-start(bf16[320,768]{1,0:T(8,128)(2,1)} %collective-permute-done.4.refs_2_), channel_id=1, source_target_pairs={{0,1},{1,0},{2,3},{3,2},{4,5},{5,4},{6,7},{7,6},{8,9},{9,8},{10,11... | collective-permute-start | bytes 1474568 | tf_op jit(solution)/shard_map/ppermute | solution.py:44
  21.8 3.2 %collective-permute-start.9 = (bf16[320,768]{1,0:T(8,128)(2,1)}, bf16[320,768]{1,0:T(8,128)(2,1)}, u32[]{:S(2)}, u32[]{:S(2)}) collective-permute-start(bf16[320,768]{1,0:T(8,128)(2,1)} %collective-permute-done.5.refs_4_), channel_id=1, source_target_pairs={{0,1},{1,0},{2,3},{3,2},{4,5},{5,4},{6,7},{7,6},{8,9},{9,8},{10,11... | collective-permute-start | bytes 1474568 | tf_op jit(solution)/shard_map/ppermute | solution.py:44
  21.8 3.2 %collective-permute-start.7 = (bf16[320,768]{1,0:T(8,128)(2,1)}, bf16[320,768]{1,0:T(8,128)(2,1)}, u32[]{:S(2)}, u32[]{:S(2)}) collective-permute-start(bf16[320,768]{1,0:T(8,128)(2,1)} %collective-permute-done.refs_0_), channel_id=1, source_target_pairs={{0,1},{1,0},{2,3},{3,2},{4,5},{5,4},{6,7},{7,6},{8,9},{9,8},{10,11... | collective-permute-start | bytes 1474568 | tf_op jit(solution)/shard_map/ppermute | solution.py:44
  22.3 14.3 %collective-permute-start.2 = (bf16[320,768]{1,0:T(8,128)(2,1)}, bf16[320,768]{1,0:T(8,128)(2,1)S(1)}, u32[]{:S(2)}, u32[]{:S(2)}) collective-permute-start(bf16[320,768]{1,0:T(8,128)(2,1)} %collective-permute-done.refs_0_), channel_id=1, source_target_pairs={{0,4},{1,5},{2,6},{3,7},{4,8},{5,9},{6,10},{7,11},{8,12},{9,13},{1... | collective-permute-start | bytes 1474568 | tf_op jit(solution)/shard_map/ppermute | solution.py:44
  22.3 14.3 %collective-permute-start.3 = (bf16[320,768]{1,0:T(8,128)(2,1)}, bf16[320,768]{1,0:T(8,128)(2,1)S(1)}, u32[]{:S(2)}, u32[]{:S(2)}) collective-permute-start(bf16[320,768]{1,0:T(8,128)(2,1)} %collective-permute-done.refs_0_), channel_id=1, source_target_pairs={{0,2},{1,3},{2,0},{3,1},{4,6},{5,7},{6,4},{7,5},{8,10},{9,11},{10,... | collective-permute-start | bytes 1474568 | tf_op jit(solution)/shard_map/ppermute | solution.py:44
  23.7 13.0 %collective-permute-start.6 = (bf16[320,768]{1,0:T(8,128)(2,1)}, bf16[320,768]{1,0:T(8,128)(2,1)S(1)}, u32[]{:S(2)}, u32[]{:S(2)}) collective-permute-start(bf16[320,768]{1,0:T(8,128)(2,1)} %collective-permute-done.5.refs_4_), channel_id=1, source_target_pairs={{0,12},{1,13},{2,14},{3,15},{4,0},{5,1},{6,2},{7,3},{8,4},{9,5},{1... | collective-permute-start | bytes 1474568 | tf_op jit(solution)/shard_map/ppermute | solution.py:44
  36.7 11.7 %copy-start.2 = (s32[3,2]{0,1:T(2,128)S(1)}, s32[3,2]{0,1:T(2,128)}, u32[]{:S(2)}) copy-start(s32[3,2]{0,1:T(2,128)} %param.21) | copy-start | bytes 76
  36.7 11.8 %copy-start.3 = (f32[3]{0:T(128)S(1)}, f32[3]{0:T(128)}, u32[]{:S(2)}) copy-start(f32[3]{0:T(128)} %param.22) | copy-start | bytes 40
  36.7 2.4 %collective-permute-start.11 = (bf16[320,768]{1,0:T(8,128)(2,1)S(1)}, bf16[320,768]{1,0:T(8,128)(2,1)S(1)}, u32[]{:S(2)}, u32[]{:S(2)}) collective-permute-start(bf16[320,768]{1,0:T(8,128)(2,1)S(1)} %collective-permute-done.2.refs_0_), channel_id=1, source_target_pairs={{0,1},{1,0},{2,3},{3,2},{4,5},{5,4},{6,7},{7,6},{8,9},{9,8},{10,11... | collective-permute-start | bytes 1474568 | tf_op jit(solution)/shard_map/ppermute | solution.py:44
  37.6 2.2 %collective-permute-start.12 = (bf16[320,768]{1,0:T(8,128)(2,1)S(1)}, bf16[320,768]{1,0:T(8,128)(2,1)S(1)}, u32[]{:S(2)}, u32[]{:S(2)}) collective-permute-start(bf16[320,768]{1,0:T(8,128)(2,1)S(1)} %collective-permute-done.6.refs_2_), channel_id=1, source_target_pairs={{0,1},{1,0},{2,3},{3,2},{4,5},{5,4},{6,7},{7,6},{8,9},{9,8},{10,11... | collective-permute-start | bytes 1474568 | tf_op jit(solution)/shard_map/ppermute | solution.py:44
  37.7 2.8 %collective-permute-start.13 = (bf16[320,768]{1,0:T(8,128)(2,1)S(1)}, bf16[320,768]{1,0:T(8,128)(2,1)S(1)}, u32[]{:S(2)}, u32[]{:S(2)}) collective-permute-start(bf16[320,768]{1,0:T(8,128)(2,1)S(1)} %collective-permute-done.3.refs_4_), channel_id=1, source_target_pairs={{0,1},{1,0},{2,3},{3,2},{4,5},{5,4},{6,7},{7,6},{8,9},{9,8},{10,11... | collective-permute-start | bytes 1474568 | tf_op jit(solution)/shard_map/ppermute | solution.py:44
  38.1 9.8 %collective-permute-start.10 = (bf16[320,768]{1,0:T(8,128)(2,1)S(1)}, bf16[320,768]{1,0:T(8,128)(2,1)}, u32[]{:S(2)}, u32[]{:S(2)}) collective-permute-start(bf16[320,768]{1,0:T(8,128)(2,1)S(1)} %broadcast_select_fusion), channel_id=1, source_target_pairs={{0,2},{1,5},{2,0},{3,7},{4,6},{5,9},{6,4},{7,11},{8,10},{9,13},{10... | collective-permute-start | bytes 1474568 | tf_op jit(solution)/shard_map/ppermute | solution.py:44
  47.9 2.2 %collective-permute-start.14 = (bf16[320,768]{1,0:T(8,128)(2,1)}, bf16[320,768]{1,0:T(8,128)(2,1)S(1)}, u32[]{:S(2)}, u32[]{:S(2)}) collective-permute-start(bf16[320,768]{1,0:T(8,128)(2,1)} %collective-permute-done.10.refs_0_), channel_id=1, source_target_pairs={{0,1},{1,0},{2,3},{3,2},{4,5},{5,4},{6,7},{7,6},{8,9},{9,8},{10,11... | collective-permute-start | bytes 1474568 | tf_op jit(solution)/shard_map/ppermute | solution.py:44
  55.7 14.2 %all-to-all-start = ((bf16[16,96,128]{2,1,0:T(8,128)(2,1)}), bf16[16,96,128]{2,1,0:T(8,128)(2,1)S(1)}, u32[]{:S(2)}, u32[]{:S(2)}) async-start(bf16[16,96,128]{2,1,0:T(8,128)(2,1)} %last_stage.1), calls=%async_computation | async-start | bytes 786432 | tf_op jit(solution)/shard_map/all_to_all | solution.py:424
  70.6 19.2 %all-to-all-start.1 = ((bf16[16,32,128]{2,1,0:T(8,128)(2,1)}), bf16[16,32,128]{2,1,0:T(8,128)(2,1)S(1)}, u32[]{:S(2)}, u32[]{:S(2)}) async-start(bf16[16,32,128]{2,1,0:T(8,128)(2,1)} %broadcast_in_dim.10), calls=%async_computation.1 | async-start | bytes 262144 | tf_op jit(solution)/shard_map/all_to_all | solution.py:428
  90.2 3.0 %collective-permute-start.15 = (f32[17,2]{0,1:T(2,128)S(1)}, f32[17,2]{0,1:T(2,128)S(1)}, u32[]{:S(2)}, u32[]{:S(2)}) collective-permute-start(f32[17,2]{0,1:T(2,128)S(1)} %pad_maximum_fusion), channel_id=1, source_target_pairs={{0,1},{1,0},{2,3},{3,2},{4,5},{5,4},{6,7},{7,6},{8,9},{9,8},{10,11... | collective-permute-start | bytes 416 | tf_op jit(solution)/shard_map/ppermute | solution.py:44

commit v5 on v4

--- a/solution.py
+++ b/solution.py
@@ -32,6 +32,7 @@
 X_DOWN = moves(lambda x, y, c: (x - 1, y, c))
 Y_SWAP = moves(lambda x, y, c: (x, y + 1, c))
 CORE_SWAP = moves(lambda x, y, c: (x, y, c + 1))
+X_OR_Y = moves(lambda x, y, c: (x + 1 - c, y + c, c))
 Y_OR_X = moves(lambda x, y, c: (x + c, y + 1 - c, c))
 
 VMEM = pl.BlockSpec(memory_space=pltpu.VMEM)
@@ -399,7 +400,9 @@
 
     flip = 1 - y
     near_chips = [chip_at(0, y), chip_at(3, y), chip_at(1, y), chip_at(0, flip)]
-    far_chips = [chip_at(2, y), chip_at(1, flip), chip_at(3, flip), chip_at(2, flip)]
+    opposite, bend = chip_at(2, y), chip_at(3, flip)
+    far_chips = [jnp.where(core == 0, opposite, bend), chip_at(1, flip), jnp.where(core == 0, bend, opposite)]
+    far_chips.append(chip_at(2, flip))
     chips = jnp.stack(near_chips + far_chips).astype(jnp.int32)
     bases = (up_out_basis.T, down_out_basis.T)
 
@@ -411,11 +414,13 @@
     left_own, first_sums = lax.optimization_barrier((near[0], sums))
     right_own, across, sums = lax.optimization_barrier((*near[1:], first_sums))
     near = (left_own, right_own, across)
-    x2, pr, pl_ = send(left_own, X_UP), send(across, X_DOWN), send(left_own, Y_SWAP)
+    straight, right_across, bent = send(left_own, X_OR_Y), send(across, X_DOWN), send(left_own, Y_OR_X)
     sums = middle_stage(core[None], chips, 1, with_twins(near), w_down, gates, *bases, before=sums)
-    third, far, sums = lax.optimization_barrier((jnp.where(core == 0, x2, pl_), (x2, pr, pl_), sums))
-    last_hop = send(third, Y_OR_X)
-    sums = middle_stage(core[None], chips, 4, with_twins(far), w_down, gates, *bases, before=sums)
+    far, sums = lax.optimization_barrier(((straight, right_across, bent), sums))
+    last_hop = send(far[0], Y_OR_X)
+    twins = [send(piece, CORE_SWAP) for piece in far]
+    shards = [far[0], twins[2], far[1], twins[1], far[2], twins[0]]
+    sums = middle_stage(core[None], chips, 4, shards, w_down, gates, *bases, before=sums)
     last_hop, sums = lax.optimization_barrier((last_hop, sums))
     grads = last_stage(
         core[None], chips, 7, lengths, pair_weights, with_twins([last_hop]),

time: 94.4 us -> 93.9 us (level)
  starting transfers between devices: 28.2 us -> 27.2 us
    all_to_all x1, starting transfers between devices: 5.64 us -> 3.71 us  [shards(): grad_parts = lax.all_to_all(grads, 'tensor', 0, 0, tiled=True)]
  transfers between devices with their start and end apart: 18 -> 18, of which waited for: 11 -> 13; matrix products, arithmetic and copies ran while one was open for 2% -> 2% of each run, Pallas kernels for 23% -> 24%
where the time goes in v5:
time: 93.9 us; the launch traced here: 93.5 us
  waiting for transfers between devices  32.6 us (35%)
  Pallas kernels  29.5 us (31%)
  starting transfers between devices  27.2 us (29%)
  local copies, waits for them, and re-layouts  1.95 us (2%)
  other arithmetic  1.46 us (2%)
    pallas_call x3, Pallas kernels, middle_stage(): pl.pallas_call(body, in_specs=in_specs, out_specs=VMEM, out_shape=jax.Sha...  18.7 us
    ppermute x16, waiting for transfers between devices, send(): return lax.ppermute(value, 'tensor', pairs)  14.6 us
    ppermute x16, starting transfers between devices, send(): return lax.ppermute(value, 'tensor', pairs)  13.8 us
    all_to_all x1, starting transfers between devices, shards(): lax.all_to_all(jnp.broadcast_to(query_rows.astype(BF16), (dp_size, half_r...  9.71 us
    all_to_all x1, waiting for transfers between devices, shards(): lax.all_to_all(jnp.broadcast_to(query_rows.astype(BF16), (dp_size, half_r...  9.47 us
    all_to_all x1, waiting for transfers between devices, shards(): grad_parts = lax.all_to_all(grads, 'tensor', 0, 0, tiled=True)  8.49 us
    pallas_call x1, Pallas kernels, last_stage(): pl.pallas_call(body, in_specs=[SMEM] * 4 + [ANY] * len(pieces) + [VMEM, A...  5.73 us
    all_to_all x1, starting transfers between devices, shards(): grad_parts = lax.all_to_all(grads, 'tensor', 0, 0, tiled=True)  3.71 us
  transfers between devices with their start and end apart: 18, of which 13 were waited for; matrix products, arithmetic and copies ran while one was open for 2% of the time, Pallas kernels for 24%

profile of v5, /device:TPU:1, one launch (start us, length us, event | category | flops | bytes accessed | tf_op | source)
XLA Modules:
  0.0 93.5 jit_solution(14390179721691014900)
XLA Ops:
  0.7 1.4 %first.1.refs_0_ = bf16[320,768]{1,0:T(8,128)(2,1)S(1)} custom-call(s32[1]{0:T(128)} %bitcast.9.place_ref, bf16[768,256]{1,0:T(8,128)(2,1)} %bitcast.41, bf16[768,256]{1,0:T(8,128)(2,1)} %bitcast.42, bf16[64,4096]{1,0:T(8,128)(2,1)} %bitcast.40), custom_call_target="tpu_custom_call" | custom-call | tf_op jit(solution)/shard_map/first/pallas_call | solution.py:75
  2.1 3.3 %collective-permute-start.1 = (bf16[320,768]{1,0:T(8,128)(2,1)S(1)}, bf16[320,768]{1,0:T(8,128)(2,1)S(1)}, u32[]{:S(2)}, u32[]{:S(2)}) collective-permute-start(bf16[320,768]{1,0:T(8,128)(2,1)S(1)} %first.1.refs_0_), channel_id=1, source_target_pairs={{0,1},{1,0},{2,3},{3,2},{4,5},{5,4},{6,7},{7,6},{8,9},{9,8},{10,11... | collective-permute-start | bytes 1474568 | tf_op jit(solution)/shard_map/ppermute | solution.py:45
  5.4 2.7 %collective-permute-start.3 = (bf16[320,768]{1,0:T(8,128)(2,1)S(1)}, bf16[320,768]{1,0:T(8,128)(2,1)}, u32[]{:S(2)}, u32[]{:S(2)}) collective-permute-start(bf16[320,768]{1,0:T(8,128)(2,1)S(1)} %first.1.refs_0_), channel_id=1, source_target_pairs={{0,12},{1,13},{2,14},{3,15},{4,0},{5,1},{6,2},{7,3},{8,4},{9,5},{1... | collective-permute-start | bytes 1474568 | tf_op jit(solution)/shard_map/ppermute | solution.py:45
  8.1 3.6 %prepare.1 = (bf16[1024,768]{1,0:T(8,128)(2,1)S(1)}, f32[64,768]{1,0:T(8,128)}) custom-call(bf16[768,1024]{1,0:T(8,128)(2,1)} %bitcast.38, bf16[768,1024]{1,0:T(8,128)(2,1)} %bitcast.39, bf16[64,1024]{1,0:T(8,128)(2,1)} %bitcast.45), custom_call_target="tpu_custom_call" | custom-call | tf_op jit(solution)/shard_map/prepare/pallas_call | solution.py:105
  11.8 4.1 %middle_stage.3.refs_10_ = f32[192,768]{1,0:T(8,128)S(1)} custom-call(s32[1]{0:T(128)} %bitcast.core_ref, s32[8]{0:T(128)S(1)} %stack.35.chips_ref, bf16[320,768]{1,0:T(8,128)(2,1)S(1)} %first.1.refs_0_, bf16[320,768]{1,0:T(8,128)(2,1)S(1)} %collective-permute-done.1.refs_1_, bf16[1024,4096]{1,0:T(8,128)(2,1)} %refs_3_.1, bf16[64,4096]{1,0:T(8,128)(2,1)} %bitcast.34, ...), custom_call_target="tpu_custom_call" | custom-call | flops 1006632960 | bytes 1835008 | tf_op jit(solution)/shard_map/middle_stage/pallas_call | solution.py:271
  15.9 3.4 %collective-permute-done.refs_0_ = bf16[320,768]{1,0:T(8,128)(2,1)S(1)} collective-permute-done((bf16[320,768]{1,0:T(8,128)(2,1)S(1)}, bf16[320,768]{1,0:T(8,128)(2,1)S(1)}, u32[]{:S(2)}, u32[]{:S(2)}) %collective-permute-start) | collective-permute-done | bytes 491552 | tf_op jit(solution)/shard_map/ppermute | solution.py:45
  19.4 0.9 collective-permute-done.4.refs_4_
  20.3 1.5 %collective-permute-start.8 = (bf16[320,768]{1,0:T(8,128)(2,1)}, bf16[320,768]{1,0:T(8,128)(2,1)S(1)}, u32[]{:S(2)}, u32[]{:S(2)}) collective-permute-start(bf16[320,768]{1,0:T(8,128)(2,1)} %collective-permute-done.3.refs_2_), channel_id=1, source_target_pairs={{0,1},{1,0},{2,3},{3,2},{4,5},{5,4},{6,7},{7,6},{8,9},{9,8},{10,11... | collective-permute-start | bytes 1474568 | tf_op jit(solution)/shard_map/ppermute | solution.py:45
  22.3 1.2 %collective-permute-start.5 = (bf16[320,768]{1,0:T(8,128)(2,1)}, bf16[320,768]{1,0:T(8,128)(2,1)S(1)}, u32[]{:S(2)}, u32[]{:S(2)}) collective-permute-start(bf16[320,768]{1,0:T(8,128)(2,1)} %collective-permute-done.4.refs_4_), channel_id=1, source_target_pairs={{0,12},{1,13},{2,14},{3,15},{4,0},{5,1},{6,2},{7,3},{8,4},{9,5},{1... | collective-permute-start | bytes 1474568 | tf_op jit(solution)/shard_map/ppermute | solution.py:45
  23.8 1.1 %collective-permute-done.9.refs_5_ = bf16[320,768]{1,0:T(8,128)(2,1)S(1)} collective-permute-done((bf16[320,768]{1,0:T(8,128)(2,1)}, bf16[320,768]{1,0:T(8,128)(2,1)S(1)}, u32[]{:S(2)}, u32[]{:S(2)}) %collective-permute-start.9) | collective-permute-done | bytes 491552 | tf_op jit(solution)/shard_map/ppermute | solution.py:45
  24.9 7.2 %middle_stage.4.refs_10_ = f32[192,768]{1,0:T(8,128)S(1)} custom-call(s32[1]{0:T(128)} %bitcast.core_ref, s32[8]{0:T(128)S(1)} %stack.35.chips_ref, bf16[320,768]{1,0:T(8,128)(2,1)S(1)} %collective-permute-done.refs_0_, bf16[320,768]{1,0:T(8,128)(2,1)S(1)} %collective-permute-done.7.refs_1_, bf16[320,768]{1,0:T(8,128)(2,1)} %collective-permute-done.3.refs_2_, ...), custom_call_target="tpu_custom_call" | custom-call | flops 2617245696 | bytes 5505024 | tf_op jit(solution)/shard_map/middle_stage/pallas_call | solution.py:271
  32.2 3.2 %collective-permute-done.5.refs_2_ = bf16[320,768]{1,0:T(8,128)(2,1)S(1)} collective-permute-done((bf16[320,768]{1,0:T(8,128)(2,1)}, bf16[320,768]{1,0:T(8,128)(2,1)S(1)}, u32[]{:S(2)}, u32[]{:S(2)}) %collective-permute-start.5) | collective-permute-done | bytes 491552 | tf_op jit(solution)/shard_map/ppermute | solution.py:45
  35.5 1.8 %collective-permute-done.6.refs_4_ = bf16[320,768]{1,0:T(8,128)(2,1)S(1)} collective-permute-done((bf16[320,768]{1,0:T(8,128)(2,1)S(1)}, bf16[320,768]{1,0:T(8,128)(2,1)S(1)}, u32[]{:S(2)}, u32[]{:S(2)}) %collective-permute-start.6) | collective-permute-done | bytes 491552 | tf_op jit(solution)/shard_map/ppermute | solution.py:45
  37.3 1.1 %collective-permute-start.11 = (bf16[320,768]{1,0:T(8,128)(2,1)S(1)}, bf16[320,768]{1,0:T(8,128)(2,1)S(1)}, u32[]{:S(2)}, u32[]{:S(2)}) collective-permute-start(bf16[320,768]{1,0:T(8,128)(2,1)S(1)} %collective-permute-done.6.refs_4_), channel_id=1, source_target_pairs={{0,1},{1,0},{2,3},{3,2},{4,5},{5,4},{6,7},{7,6},{8,9},{9,8},{10,11... | collective-permute-start | bytes 1474568 | tf_op jit(solution)/shard_map/ppermute | solution.py:45
  38.9 1.0 %collective-permute-done.11.refs_1_ = bf16[320,768]{1,0:T(8,128)(2,1)S(1)} collective-permute-done((bf16[320,768]{1,0:T(8,128)(2,1)S(1)}, bf16[320,768]{1,0:T(8,128)(2,1)S(1)}, u32[]{:S(2)}, u32[]{:S(2)}) %collective-permute-start.11) | collective-permute-done | bytes 491552 | tf_op jit(solution)/shard_map/ppermute | solution.py:45
  39.9 0.7 collective-permute-done.12.refs_3_
  41.3 7.4 %middle_stage.5.refs_2_ = f32[192,768]{1,0:T(8,128)S(1)} custom-call(s32[1]{0:T(128)} %bitcast.core_ref, s32[8]{0:T(128)S(1)} %stack.35.chips_ref, bf16[320,768]{1,0:T(8,128)(2,1)S(1)} %collective-permute-done.2.refs_0_, bf16[320,768]{1,0:T(8,128)(2,1)S(1)} %collective-permute-done.11.refs_1_, bf16[320,768]{1,0:T(8,128)(2,1)S(1)} %collective-permute-done.5.refs_2_, ...), custom_call_target="tpu_custom_call" | custom-call | flops 2617245696 | bytes 5505024 | tf_op jit(solution)/shard_map/middle_stage/pallas_call | solution.py:271
  49.3 1.4 %collective-permute-done.14.refs_1_ = bf16[320,768]{1,0:T(8,128)(2,1)S(1)} collective-permute-done((bf16[320,768]{1,0:T(8,128)(2,1)S(1)}, bf16[320,768]{1,0:T(8,128)(2,1)S(1)}, u32[]{:S(2)}, u32[]{:S(2)}) %collective-permute-start.14) | collective-permute-done | bytes 491552 | tf_op jit(solution)/shard_map/ppermute | solution.py:45
  50.7 5.7 %last_stage.1 = bf16[16,96,128]{2,1,0:T(8,128)(2,1)} custom-call(s32[1]{0:T(128)} %bitcast.core_ref, s32[8]{0:T(128)S(1)} %stack.35.chips_ref, s32[3,2]{1,0:T(4,128)S(1)} %copy.29.lengths_ref, f32[3]{0:T(128)S(1)} %add_divide_fusion.pair_ref, bf16[320,768]{1,0:T(8,128)(2,1)S(1)} %collective-permute-done.10.refs_0_, ...), custom_call_target="tpu_custom_call" | custom-call | flops 1006632960 | bytes 1835008 | tf_op jit(solution)/shard_map/last_stage/pallas_call | solution.py:342
  56.4 3.7 %all-to-all-start = ((bf16[16,96,128]{2,1,0:T(8,128)(2,1)}), bf16[16,96,128]{2,1,0:T(8,128)(2,1)S(1)}, u32[]{:S(2)}, u32[]{:S(2)}) async-start(bf16[16,96,128]{2,1,0:T(8,128)(2,1)} %last_stage.1), calls=%async_computation | async-start | bytes 786432 | tf_op jit(solution)/shard_map/all_to_all | solution.py:429
  60.3 8.5 %all-to-all-done = bf16[16,96,128]{2,1,0:T(8,128)(2,1)S(1)} async-done(((bf16[16,96,128]{2,1,0:T(8,128)(2,1)}), bf16[16,96,128]{2,1,0:T(8,128)(2,1)S(1)}, u32[]{:S(2)}, u32[]{:S(2)}) %all-to-all-start) | async-done | bytes 393248 | tf_op jit(solution)/shard_map/all_to_all | solution.py:429
  69.5 9.7 %all-to-all-start.1 = ((bf16[16,32,128]{2,1,0:T(8,128)(2,1)}), bf16[16,32,128]{2,1,0:T(8,128)(2,1)S(1)}, u32[]{:S(2)}, u32[]{:S(2)}) async-start(bf16[16,32,128]{2,1,0:T(8,128)(2,1)} %broadcast_in_dim.10), calls=%async_computation.1 | async-start | bytes 262144 | tf_op jit(solution)/shard_map/all_to_all | solution.py:433
  79.7 9.5 %all-to-all-done.1 = bf16[16,32,128]{2,1,0:T(8,128)(2,1)S(1)} async-done(((bf16[16,32,128]{2,1,0:T(8,128)(2,1)}), bf16[16,32,128]{2,1,0:T(8,128)(2,1)S(1)}, u32[]{:S(2)}, u32[]{:S(2)}) %all-to-all-start.1) | async-done | bytes 131104 | tf_op jit(solution)/shard_map/all_to_all | solution.py:433
  89.5 2.2 %collective-permute-start.15 = (f32[17,2]{0,1:T(2,128)S(1)}, f32[17,2]{0,1:T(2,128)S(1)}, u32[]{:S(2)}, u32[]{:S(2)}) collective-permute-start(f32[17,2]{0,1:T(2,128)S(1)} %pad_maximum_fusion), channel_id=1, source_target_pairs={{0,1},{1,0},{2,3},{3,2},{4,5},{5,4},{6,7},{7,6},{8,9},{9,8},{10,11... | collective-permute-start | bytes 416 | tf_op jit(solution)/shard_map/ppermute | solution.py:45
  (50 shorter events, 6.2 us)
Async XLA Ops:
  0.6 59.5 %copy-start = (f32[2,64,64]{2,1,0:T(8,128)S(1)}, f32[2,64,64]{2,1,0:T(8,128)}, u32[]{:S(2)}) copy-start(f32[2,64,64]{2,1,0:T(8,128)} %param.23) | copy-start | bytes 98308
  2.1 9.7 %collective-permute-start.1 = (bf16[320,768]{1,0:T(8,128)(2,1)S(1)}, bf16[320,768]{1,0:T(8,128)(2,1)S(1)}, u32[]{:S(2)}, u32[]{:S(2)}) collective-permute-start(bf16[320,768]{1,0:T(8,128)(2,1)S(1)} %first.1.refs_0_), channel_id=1, source_target_pairs={{0,1},{1,0},{2,3},{3,2},{4,5},{5,4},{6,7},{7,6},{8,9},{9,8},{10,11... | collective-permute-start | bytes 1474568 | tf_op jit(solution)/shard_map/ppermute | solution.py:45
  5.4 14.0 %collective-permute-start = (bf16[320,768]{1,0:T(8,128)(2,1)S(1)}, bf16[320,768]{1,0:T(8,128)(2,1)S(1)}, u32[]{:S(2)}, u32[]{:S(2)}) collective-permute-start(bf16[320,768]{1,0:T(8,128)(2,1)S(1)} %first.1.refs_0_), channel_id=1, source_target_pairs={{0,4},{1,5},{2,6},{3,7},{4,8},{5,9},{6,10},{7,11},{8,12},{9,13},{1... | collective-permute-start | bytes 1474568 | tf_op jit(solution)/shard_map/ppermute | solution.py:45
  5.4 14.0 %collective-permute-start.3 = (bf16[320,768]{1,0:T(8,128)(2,1)S(1)}, bf16[320,768]{1,0:T(8,128)(2,1)}, u32[]{:S(2)}, u32[]{:S(2)}) collective-permute-start(bf16[320,768]{1,0:T(8,128)(2,1)S(1)} %first.1.refs_0_), channel_id=1, source_target_pairs={{0,12},{1,13},{2,14},{3,15},{4,0},{5,1},{6,2},{7,3},{8,4},{9,5},{1... | collective-permute-start | bytes 1474568 | tf_op jit(solution)/shard_map/ppermute | solution.py:45
  8.1 12.2 %collective-permute-start.4 = (bf16[320,768]{1,0:T(8,128)(2,1)S(1)}, bf16[320,768]{1,0:T(8,128)(2,1)}, u32[]{:S(2)}, u32[]{:S(2)}) collective-permute-start(bf16[320,768]{1,0:T(8,128)(2,1)S(1)} %first.1.refs_0_), channel_id=1, source_target_pairs={{0,2},{1,3},{2,0},{3,1},{4,6},{5,7},{6,4},{7,5},{8,10},{9,11},{10,... | collective-permute-start | bytes 1474568 | tf_op jit(solution)/shard_map/ppermute | solution.py:45
  8.1 3.7 %copy-start.1 = (bf16[1024,64]{0,1:T(8,128)(2,1)S(1)}, bf16[1024,64]{0,1:T(8,128)(2,1)}, u32[]{:S(2)}) copy-start(bf16[1024,64]{0,1:T(8,128)(2,1)} %param.18) | copy-start | bytes 393220
  20.3 3.2 %collective-permute-start.8 = (bf16[320,768]{1,0:T(8,128)(2,1)}, bf16[320,768]{1,0:T(8,128)(2,1)S(1)}, u32[]{:S(2)}, u32[]{:S(2)}) collective-permute-start(bf16[320,768]{1,0:T(8,128)(2,1)} %collective-permute-done.3.refs_2_), channel_id=1, source_target_pairs={{0,1},{1,0},{2,3},{3,2},{4,5},{5,4},{6,7},{7,6},{8,9},{9,8},{10,11... | collective-permute-start | bytes 1474568 | tf_op jit(solution)/shard_map/ppermute | solution.py:45
  21.8 3.1 %collective-permute-start.9 = (bf16[320,768]{1,0:T(8,128)(2,1)}, bf16[320,768]{1,0:T(8,128)(2,1)S(1)}, u32[]{:S(2)}, u32[]{:S(2)}) collective-permute-start(bf16[320,768]{1,0:T(8,128)(2,1)} %collective-permute-done.4.refs_4_), channel_id=1, source_target_pairs={{0,1},{1,0},{2,3},{3,2},{4,5},{5,4},{6,7},{7,6},{8,9},{9,8},{10,11... | collective-permute-start | bytes 1474568 | tf_op jit(solution)/shard_map/ppermute | solution.py:45
  21.8 3.1 %collective-permute-start.7 = (bf16[320,768]{1,0:T(8,128)(2,1)S(1)}, bf16[320,768]{1,0:T(8,128)(2,1)S(1)}, u32[]{:S(2)}, u32[]{:S(2)}) collective-permute-start(bf16[320,768]{1,0:T(8,128)(2,1)S(1)} %collective-permute-done.refs_0_), channel_id=1, source_target_pairs={{0,1},{1,0},{2,3},{3,2},{4,5},{5,4},{6,7},{7,6},{8,9},{9,8},{10,11... | collective-permute-start | bytes 1474568 | tf_op jit(solution)/shard_map/ppermute | solution.py:45
  22.3 13.1 %collective-permute-start.5 = (bf16[320,768]{1,0:T(8,128)(2,1)}, bf16[320,768]{1,0:T(8,128)(2,1)S(1)}, u32[]{:S(2)}, u32[]{:S(2)}) collective-permute-start(bf16[320,768]{1,0:T(8,128)(2,1)} %collective-permute-done.4.refs_4_), channel_id=1, source_target_pairs={{0,12},{1,13},{2,14},{3,15},{4,0},{5,1},{6,2},{7,3},{8,4},{9,5},{1... | collective-permute-start | bytes 1474568 | tf_op jit(solution)/shard_map/ppermute | solution.py:45
  23.5 11.9 %collective-permute-start.2 = (bf16[320,768]{1,0:T(8,128)(2,1)S(1)}, bf16[320,768]{1,0:T(8,128)(2,1)S(1)}, u32[]{:S(2)}, u32[]{:S(2)}) collective-permute-start(bf16[320,768]{1,0:T(8,128)(2,1)S(1)} %collective-permute-done.refs_0_), channel_id=1, source_target_pairs={{0,4},{1,3},{2,6},{3,1},{4,8},{5,7},{6,10},{7,5},{8,12},{9,11},{10... | collective-permute-start | bytes 1474568 | tf_op jit(solution)/shard_map/ppermute | solution.py:45
  23.6 13.8 %collective-permute-start.6 = (bf16[320,768]{1,0:T(8,128)(2,1)S(1)}, bf16[320,768]{1,0:T(8,128)(2,1)S(1)}, u32[]{:S(2)}, u32[]{:S(2)}) collective-permute-start(bf16[320,768]{1,0:T(8,128)(2,1)S(1)} %collective-permute-done.refs_0_), channel_id=1, source_target_pairs={{0,2},{1,5},{2,0},{3,7},{4,6},{5,9},{6,4},{7,11},{8,10},{9,13},{10... | collective-permute-start | bytes 1474568 | tf_op jit(solution)/shard_map/ppermute | solution.py:45
  32.2 17.0 %copy-start.2 = (s32[3,2]{0,1:T(2,128)S(1)}, s32[3,2]{0,1:T(2,128)}, u32[]{:S(2)}) copy-start(s32[3,2]{0,1:T(2,128)} %param.21) | copy-start | bytes 76
  32.2 17.1 %copy-start.3 = (f32[3]{0:T(128)S(1)}, f32[3]{0:T(128)}, u32[]{:S(2)}) copy-start(f32[3]{0:T(128)} %param.22) | copy-start | bytes 40
  37.3 2.6 %collective-permute-start.11 = (bf16[320,768]{1,0:T(8,128)(2,1)S(1)}, bf16[320,768]{1,0:T(8,128)(2,1)S(1)}, u32[]{:S(2)}, u32[]{:S(2)}) collective-permute-start(bf16[320,768]{1,0:T(8,128)(2,1)S(1)} %collective-permute-done.6.refs_4_), channel_id=1, source_target_pairs={{0,1},{1,0},{2,3},{3,2},{4,5},{5,4},{6,7},{7,6},{8,9},{9,8},{10,11... | collective-permute-start | bytes 1474568 | tf_op jit(solution)/shard_map/ppermute | solution.py:45
  38.4 2.2 %collective-permute-start.12 = (bf16[320,768]{1,0:T(8,128)(2,1)S(1)}, bf16[320,768]{1,0:T(8,128)(2,1)S(1)}, u32[]{:S(2)}, u32[]{:S(2)}) collective-permute-start(bf16[320,768]{1,0:T(8,128)(2,1)S(1)} %collective-permute-done.5.refs_2_), channel_id=1, source_target_pairs={{0,1},{1,0},{2,3},{3,2},{4,5},{5,4},{6,7},{7,6},{8,9},{9,8},{10,11... | collective-permute-start | bytes 1474568 | tf_op jit(solution)/shard_map/ppermute | solution.py:45
  38.4 2.9 %collective-permute-start.13 = (bf16[320,768]{1,0:T(8,128)(2,1)S(1)}, bf16[320,768]{1,0:T(8,128)(2,1)S(1)}, u32[]{:S(2)}, u32[]{:S(2)}) collective-permute-start(bf16[320,768]{1,0:T(8,128)(2,1)S(1)} %collective-permute-done.2.refs_0_), channel_id=1, source_target_pairs={{0,1},{1,0},{2,3},{3,2},{4,5},{5,4},{6,7},{7,6},{8,9},{9,8},{10,11... | collective-permute-start | bytes 1474568 | tf_op jit(solution)/shard_map/ppermute | solution.py:45
  38.9 9.8 %collective-permute-start.10 = (bf16[320,768]{1,0:T(8,128)(2,1)S(1)}, bf16[320,768]{1,0:T(8,128)(2,1)S(1)}, u32[]{:S(2)}, u32[]{:S(2)}) collective-permute-start(bf16[320,768]{1,0:T(8,128)(2,1)S(1)} %collective-permute-done.2.refs_0_), channel_id=1, source_target_pairs={{0,2},{1,5},{2,0},{3,7},{4,6},{5,9},{6,4},{7,11},{8,10},{9,13},{10... | collective-permute-start | bytes 1474568 | tf_op jit(solution)/shard_map/ppermute | solution.py:45
  48.7 2.0 %collective-permute-start.14 = (bf16[320,768]{1,0:T(8,128)(2,1)S(1)}, bf16[320,768]{1,0:T(8,128)(2,1)S(1)}, u32[]{:S(2)}, u32[]{:S(2)}) collective-permute-start(bf16[320,768]{1,0:T(8,128)(2,1)S(1)} %collective-permute-done.10.refs_0_), channel_id=1, source_target_pairs={{0,1},{1,0},{2,3},{3,2},{4,5},{5,4},{6,7},{7,6},{8,9},{9,8},{10,11... | collective-permute-start | bytes 1474568 | tf_op jit(solution)/shard_map/ppermute | solution.py:45
  56.4 12.3 %all-to-all-start = ((bf16[16,96,128]{2,1,0:T(8,128)(2,1)}), bf16[16,96,128]{2,1,0:T(8,128)(2,1)S(1)}, u32[]{:S(2)}, u32[]{:S(2)}) async-start(bf16[16,96,128]{2,1,0:T(8,128)(2,1)} %last_stage.1), calls=%async_computation | async-start | bytes 786432 | tf_op jit(solution)/shard_map/all_to_all | solution.py:429
  69.5 19.7 %all-to-all-start.1 = ((bf16[16,32,128]{2,1,0:T(8,128)(2,1)}), bf16[16,32,128]{2,1,0:T(8,128)(2,1)S(1)}, u32[]{:S(2)}, u32[]{:S(2)}) async-start(bf16[16,32,128]{2,1,0:T(8,128)(2,1)} %broadcast_in_dim.10), calls=%async_computation.1 | async-start | bytes 262144 | tf_op jit(solution)/shard_map/all_to_all | solution.py:433
  89.5 3.0 %collective-permute-start.15 = (f32[17,2]{0,1:T(2,128)S(1)}, f32[17,2]{0,1:T(2,128)S(1)}, u32[]{:S(2)}, u32[]{:S(2)}) collective-permute-start(f32[17,2]{0,1:T(2,128)S(1)} %pad_maximum_fusion), channel_id=1, source_target_pairs={{0,1},{1,0},{2,3},{3,2},{4,5},{5,4},{6,7},{7,6},{8,9},{9,8},{10,11... | collective-permute-start | bytes 416 | tf_op jit(solution)/shard_map/ppermute | solution.py:45

commit v6 on v5

--- a/solution.py
+++ b/solution.py
@@ -416,7 +416,7 @@
     near = (left_own, right_own, across)
     straight, right_across, bent = send(left_own, X_OR_Y), send(across, X_DOWN), send(left_own, Y_OR_X)
     sums = middle_stage(core[None], chips, 1, with_twins(near), w_down, gates, *bases, before=sums)
-    far, sums = lax.optimization_barrier(((straight, right_across, bent), sums))
+    far = [lax.optimization_barrier((piece, sums))[0] for piece in (straight, right_across, bent)]
     last_hop = send(far[0], Y_OR_X)
     twins = [send(piece, CORE_SWAP) for piece in far]
     shards = [far[0], twins[2], far[1], twins[1], far[2], twins[0]]

time: 93.9 us -> 92.4 us (0.984)
  waiting for transfers between devices: 32.6 us -> 30.8 us
    ppermute x16, waiting for transfers between devices: 14.6 us -> 12.8 us  [send(): return lax.ppermute(value, 'tensor', pairs)]
  transfers between devices with their start and end apart: 18 -> 18, of which waited for: 13 -> 11; matrix products, arithmetic and copies ran while one was open for 2% -> 2% of each run, Pallas kernels for 24% -> 24%
where the time goes in v6:
time: 92.4 us; the launch traced here: 92 us
  waiting for transfers between devices  30.8 us (33%)
  Pallas kernels  29.5 us (32%)
  starting transfers between devices  27.6 us (30%)
  local copies, waits for them, and re-layouts  1.95 us (2%)
  other arithmetic  1.46 us (2%)
    pallas_call x3, Pallas kernels, middle_stage(): pl.pallas_call(body, in_specs=in_specs, out_specs=VMEM, out_shape=jax.Sha...  18.7 us
    ppermute x16, starting transfers between devices, send(): return lax.ppermute(value, 'tensor', pairs)  14.1 us
    ppermute x16, waiting for transfers between devices, send(): return lax.ppermute(value, 'tensor', pairs)  12.8 us
    all_to_all x1, starting transfers between devices, shards(): lax.all_to_all(jnp.broadcast_to(query_rows.astype(BF16), (dp_size, half_r...  9.73 us
    all_to_all x1, waiting for transfers between devices, shards(): lax.all_to_all(jnp.broadcast_to(query_rows.astype(BF16), (dp_size, half_r...  9.47 us
    all_to_all x1, waiting for transfers between devices, shards(): grad_parts = lax.all_to_all(grads, 'tensor', 0, 0, tiled=True)  8.49 us
    pallas_call x1, Pallas kernels, last_stage(): pl.pallas_call(body, in_specs=[SMEM] * 4 + [ANY] * len(pieces) + [VMEM, A...  5.72 us
    all_to_all x1, starting transfers between devices, shards(): grad_parts = lax.all_to_all(grads, 'tensor', 0, 0, tiled=True)  3.74 us
  transfers between devices with their start and end apart: 18, of which 11 were waited for; matrix products, arithmetic and copies ran while one was open for 2% of the time, Pallas kernels for 24%

profile of v6, /device:TPU:1, one launch (start us, length us, event | category | flops | bytes accessed | tf_op | source)
XLA Modules:
  0.0 92.0 jit_solution(7676044646595717940)
XLA Ops:
  0.7 1.4 %first.1.refs_0_ = bf16[320,768]{1,0:T(8,128)(2,1)S(1)} custom-call(s32[1]{0:T(128)} %bitcast.9.place_ref, bf16[768,256]{1,0:T(8,128)(2,1)} %bitcast.41, bf16[768,256]{1,0:T(8,128)(2,1)} %bitcast.42, bf16[64,4096]{1,0:T(8,128)(2,1)} %bitcast.40), custom_call_target="tpu_custom_call" | custom-call | tf_op jit(solution)/shard_map/first/pallas_call | solution.py:75
  2.1 3.3 %collective-permute-start.1 = (bf16[320,768]{1,0:T(8,128)(2,1)S(1)}, bf16[320,768]{1,0:T(8,128)(2,1)S(1)}, u32[]{:S(2)}, u32[]{:S(2)}) collective-permute-start(bf16[320,768]{1,0:T(8,128)(2,1)S(1)} %first.1.refs_0_), channel_id=1, source_target_pairs={{0,1},{1,0},{2,3},{3,2},{4,5},{5,4},{6,7},{7,6},{8,9},{9,8},{10,11... | collective-permute-start | bytes 1474568 | tf_op jit(solution)/shard_map/ppermute | solution.py:45
  5.4 2.7 %collective-permute-start.4 = (bf16[320,768]{1,0:T(8,128)(2,1)S(1)}, bf16[320,768]{1,0:T(8,128)(2,1)}, u32[]{:S(2)}, u32[]{:S(2)}) collective-permute-start(bf16[320,768]{1,0:T(8,128)(2,1)S(1)} %first.1.refs_0_), channel_id=1, source_target_pairs={{0,12},{1,13},{2,14},{3,15},{4,0},{5,1},{6,2},{7,3},{8,4},{9,5},{1... | collective-permute-start | bytes 1474568 | tf_op jit(solution)/shard_map/ppermute | solution.py:45
  8.1 3.6 %prepare.1 = (bf16[1024,768]{1,0:T(8,128)(2,1)S(1)}, f32[64,768]{1,0:T(8,128)}) custom-call(bf16[768,1024]{1,0:T(8,128)(2,1)} %bitcast.38, bf16[768,1024]{1,0:T(8,128)(2,1)} %bitcast.39, bf16[64,1024]{1,0:T(8,128)(2,1)} %bitcast.45), custom_call_target="tpu_custom_call" | custom-call | tf_op jit(solution)/shard_map/prepare/pallas_call | solution.py:105
  11.8 4.1 %middle_stage.3.refs_10_ = f32[192,768]{1,0:T(8,128)S(1)} custom-call(s32[1]{0:T(128)} %bitcast.core_ref, s32[8]{0:T(128)S(1)} %stack.35.chips_ref, bf16[320,768]{1,0:T(8,128)(2,1)S(1)} %first.1.refs_0_, bf16[320,768]{1,0:T(8,128)(2,1)S(1)} %collective-permute-done.1.refs_1_, bf16[1024,4096]{1,0:T(8,128)(2,1)} %refs_3_.1, bf16[64,4096]{1,0:T(8,128)(2,1)} %bitcast.34, ...), custom_call_target="tpu_custom_call" | custom-call | flops 1006632960 | bytes 1835008 | tf_op jit(solution)/shard_map/middle_stage/pallas_call | solution.py:271
  15.9 3.4 %collective-permute-done.refs_0_ = bf16[320,768]{1,0:T(8,128)(2,1)S(1)} collective-permute-done((bf16[320,768]{1,0:T(8,128)(2,1)S(1)}, bf16[320,768]{1,0:T(8,128)(2,1)S(1)}, u32[]{:S(2)}, u32[]{:S(2)}) %collective-permute-start) | collective-permute-done | bytes 491552 | tf_op jit(solution)/shard_map/ppermute | solution.py:45
  19.4 0.9 %collective-permute-done.5.refs_4_ = bf16[320,768]{1,0:T(8,128)(2,1)} collective-permute-done((bf16[320,768]{1,0:T(8,128)(2,1)S(1)}, bf16[320,768]{1,0:T(8,128)(2,1)}, u32[]{:S(2)}, u32[]{:S(2)}) %collective-permute-start.5) | collective-permute-done | bytes 491552 | tf_op jit(solution)/shard_map/ppermute | solution.py:45
  20.3 1.5 %collective-permute-start.6 = (bf16[320,768]{1,0:T(8,128)(2,1)}, bf16[320,768]{1,0:T(8,128)(2,1)S(1)}, u32[]{:S(2)}, u32[]{:S(2)}) collective-permute-start(bf16[320,768]{1,0:T(8,128)(2,1)} %collective-permute-done.4.refs_2_), channel_id=1, source_target_pairs={{0,1},{1,0},{2,3},{3,2},{4,5},{5,4},{6,7},{7,6},{8,9},{9,8},{10,11... | collective-permute-start | bytes 1474568 | tf_op jit(solution)/shard_map/ppermute | solution.py:45
  22.3 1.2 %collective-permute-start.11 = (bf16[320,768]{1,0:T(8,128)(2,1)}, bf16[320,768]{1,0:T(8,128)(2,1)S(1)}, u32[]{:S(2)}, u32[]{:S(2)}) collective-permute-start(bf16[320,768]{1,0:T(8,128)(2,1)} %collective-permute-done.5.refs_4_), channel_id=1, source_target_pairs={{0,12},{1,13},{2,14},{3,15},{4,0},{5,1},{6,2},{7,3},{8,4},{9,5},{1... | collective-permute-start | bytes 1474568 | tf_op jit(solution)/shard_map/ppermute | solution.py:45
  23.8 1.1 %collective-permute-done.7.refs_5_ = bf16[320,768]{1,0:T(8,128)(2,1)S(1)} collective-permute-done((bf16[320,768]{1,0:T(8,128)(2,1)}, bf16[320,768]{1,0:T(8,128)(2,1)S(1)}, u32[]{:S(2)}, u32[]{:S(2)}) %collective-permute-start.7) | collective-permute-done | bytes 491552 | tf_op jit(solution)/shard_map/ppermute | solution.py:45
  24.9 7.2 %middle_stage.4.refs_10_ = f32[192,768]{1,0:T(8,128)S(1)} custom-call(s32[1]{0:T(128)} %bitcast.core_ref, s32[8]{0:T(128)S(1)} %stack.35.chips_ref, bf16[320,768]{1,0:T(8,128)(2,1)S(1)} %collective-permute-done.refs_0_, bf16[320,768]{1,0:T(8,128)(2,1)S(1)} %collective-permute-done.3.refs_1_, bf16[320,768]{1,0:T(8,128)(2,1)} %collective-permute-done.4.refs_2_, ...), custom_call_target="tpu_custom_call" | custom-call | flops 2617245696 | bytes 5505024 | tf_op jit(solution)/shard_map/middle_stage/pallas_call | solution.py:271
  32.2 3.2 %collective-permute-done.11.refs_2_ = bf16[320,768]{1,0:T(8,128)(2,1)S(1)} collective-permute-done((bf16[320,768]{1,0:T(8,128)(2,1)}, bf16[320,768]{1,0:T(8,128)(2,1)S(1)}, u32[]{:S(2)}, u32[]{:S(2)}) %collective-permute-start.11) | collective-permute-done | bytes 491552 | tf_op jit(solution)/shard_map/ppermute | solution.py:45
  35.4 0.8 collective-permute-start.12
  36.2 1.0 %collective-permute-done.9.refs_4_ = bf16[320,768]{1,0:T(8,128)(2,1)S(1)} collective-permute-done((bf16[320,768]{1,0:T(8,128)(2,1)S(1)}, bf16[320,768]{1,0:T(8,128)(2,1)S(1)}, u32[]{:S(2)}, u32[]{:S(2)}) %collective-permute-start.9) | collective-permute-done | bytes 491552 | tf_op jit(solution)/shard_map/ppermute | solution.py:45
  37.4 1.0 %collective-permute-start.13 = (bf16[320,768]{1,0:T(8,128)(2,1)S(1)}, bf16[320,768]{1,0:T(8,128)(2,1)S(1)}, u32[]{:S(2)}, u32[]{:S(2)}) collective-permute-start(bf16[320,768]{1,0:T(8,128)(2,1)S(1)} %collective-permute-done.2.refs_0_), channel_id=1, source_target_pairs={{0,1},{1,0},{2,3},{3,2},{4,5},{5,4},{6,7},{7,6},{8,9},{9,8},{10,11... | collective-permute-start | bytes 1474568 | tf_op jit(solution)/shard_map/ppermute | solution.py:45
  39.1 0.8 collective-permute-done.13.refs_5_
  39.9 7.4 %middle_stage.5.refs_2_ = f32[192,768]{1,0:T(8,128)S(1)} custom-call(s32[1]{0:T(128)} %bitcast.core_ref, s32[8]{0:T(128)S(1)} %stack.35.chips_ref, bf16[320,768]{1,0:T(8,128)(2,1)S(1)} %collective-permute-done.2.refs_0_, bf16[320,768]{1,0:T(8,128)(2,1)S(1)} %collective-permute-done.10.refs_1_, bf16[320,768]{1,0:T(8,128)(2,1)S(1)} %collective-permute-done.11.refs_2_, ...), custom_call_target="tpu_custom_call" | custom-call | flops 2617245696 | bytes 5505024 | tf_op jit(solution)/shard_map/middle_stage/pallas_call | solution.py:271
  47.9 1.4 %collective-permute-done.14.refs_1_ = bf16[320,768]{1,0:T(8,128)(2,1)S(1)} collective-permute-done((bf16[320,768]{1,0:T(8,128)(2,1)S(1)}, bf16[320,768]{1,0:T(8,128)(2,1)S(1)}, u32[]{:S(2)}, u32[]{:S(2)}) %collective-permute-start.14) | collective-permute-done | bytes 491552 | tf_op jit(solution)/shard_map/ppermute | solution.py:45
  49.3 5.7 %last_stage.1 = bf16[16,96,128]{2,1,0:T(8,128)(2,1)} custom-call(s32[1]{0:T(128)} %bitcast.core_ref, s32[8]{0:T(128)S(1)} %stack.35.chips_ref, s32[3,2]{1,0:T(4,128)S(1)} %copy.29.lengths_ref, f32[3]{0:T(128)S(1)} %add_divide_fusion.pair_ref, bf16[320,768]{1,0:T(8,128)(2,1)S(1)} %collective-permute-done.8.refs_0_, ...), custom_call_target="tpu_custom_call" | custom-call | flops 1006632960 | bytes 1835008 | tf_op jit(solution)/shard_map/last_stage/pallas_call | solution.py:342
  55.0 3.7 %all-to-all-start = ((bf16[16,96,128]{2,1,0:T(8,128)(2,1)}), bf16[16,96,128]{2,1,0:T(8,128)(2,1)S(1)}, u32[]{:S(2)}, u32[]{:S(2)}) async-start(bf16[16,96,128]{2,1,0:T(8,128)(2,1)} %last_stage.1), calls=%async_computation | async-start | bytes 786432 | tf_op jit(solution)/shard_map/all_to_all | solution.py:429
  58.9 8.5 %all-to-all-done = bf16[16,96,128]{2,1,0:T(8,128)(2,1)S(1)} async-done(((bf16[16,96,128]{2,1,0:T(8,128)(2,1)}), bf16[16,96,128]{2,1,0:T(8,128)(2,1)S(1)}, u32[]{:S(2)}, u32[]{:S(2)}) %all-to-all-start) | async-done | bytes 393248 | tf_op jit(solution)/shard_map/all_to_all | solution.py:429
  68.1 9.7 %all-to-all-start.1 = ((bf16[16,32,128]{2,1,0:T(8,128)(2,1)}), bf16[16,32,128]{2,1,0:T(8,128)(2,1)S(1)}, u32[]{:S(2)}, u32[]{:S(2)}) async-start(bf16[16,32,128]{2,1,0:T(8,128)(2,1)} %broadcast_in_dim.10), calls=%async_computation.1 | async-start | bytes 262144 | tf_op jit(solution)/shard_map/all_to_all | solution.py:433
  78.3 9.5 %all-to-all-done.1 = bf16[16,32,128]{2,1,0:T(8,128)(2,1)S(1)} async-done(((bf16[16,32,128]{2,1,0:T(8,128)(2,1)}), bf16[16,32,128]{2,1,0:T(8,128)(2,1)S(1)}, u32[]{:S(2)}, u32[]{:S(2)}) %all-to-all-start.1) | async-done | bytes 131104 | tf_op jit(solution)/shard_map/all_to_all | solution.py:433
  88.2 2.2 %collective-permute-start.15 = (f32[17,2]{0,1:T(2,128)S(1)}, f32[17,2]{0,1:T(2,128)S(1)}, u32[]{:S(2)}, u32[]{:S(2)}) collective-permute-start(f32[17,2]{0,1:T(2,128)S(1)} %pad_maximum_fusion), channel_id=1, source_target_pairs={{0,1},{1,0},{2,3},{3,2},{4,5},{5,4},{6,7},{7,6},{8,9},{9,8},{10,11... | collective-permute-start | bytes 416 | tf_op jit(solution)/shard_map/ppermute | solution.py:45
  (50 shorter events, 5.8 us)
Async XLA Ops:
  0.6 58.1 %copy-start = (f32[2,64,64]{2,1,0:T(8,128)S(1)}, f32[2,64,64]{2,1,0:T(8,128)}, u32[]{:S(2)}) copy-start(f32[2,64,64]{2,1,0:T(8,128)} %param.23) | copy-start | bytes 98308
  2.1 9.7 %collective-permute-start.1 = (bf16[320,768]{1,0:T(8,128)(2,1)S(1)}, bf16[320,768]{1,0:T(8,128)(2,1)S(1)}, u32[]{:S(2)}, u32[]{:S(2)}) collective-permute-start(bf16[320,768]{1,0:T(8,128)(2,1)S(1)} %first.1.refs_0_), channel_id=1, source_target_pairs={{0,1},{1,0},{2,3},{3,2},{4,5},{5,4},{6,7},{7,6},{8,9},{9,8},{10,11... | collective-permute-start | bytes 1474568 | tf_op jit(solution)/shard_map/ppermute | solution.py:45
  5.4 14.0 %collective-permute-start = (bf16[320,768]{1,0:T(8,128)(2,1)S(1)}, bf16[320,768]{1,0:T(8,128)(2,1)S(1)}, u32[]{:S(2)}, u32[]{:S(2)}) collective-permute-start(bf16[320,768]{1,0:T(8,128)(2,1)S(1)} %first.1.refs_0_), channel_id=1, source_target_pairs={{0,4},{1,5},{2,6},{3,7},{4,8},{5,9},{6,10},{7,11},{8,12},{9,13},{1... | collective-permute-start | bytes 1474568 | tf_op jit(solution)/shard_map/ppermute | solution.py:45
  5.4 14.0 %collective-permute-start.4 = (bf16[320,768]{1,0:T(8,128)(2,1)S(1)}, bf16[320,768]{1,0:T(8,128)(2,1)}, u32[]{:S(2)}, u32[]{:S(2)}) collective-permute-start(bf16[320,768]{1,0:T(8,128)(2,1)S(1)} %first.1.refs_0_), channel_id=1, source_target_pairs={{0,12},{1,13},{2,14},{3,15},{4,0},{5,1},{6,2},{7,3},{8,4},{9,5},{1... | collective-permute-start | bytes 1474568 | tf_op jit(solution)/shard_map/ppermute | solution.py:45
  8.1 12.2 %collective-permute-start.5 = (bf16[320,768]{1,0:T(8,128)(2,1)S(1)}, bf16[320,768]{1,0:T(8,128)(2,1)}, u32[]{:S(2)}, u32[]{:S(2)}) collective-permute-start(bf16[320,768]{1,0:T(8,128)(2,1)S(1)} %first.1.refs_0_), channel_id=1, source_target_pairs={{0,2},{1,3},{2,0},{3,1},{4,6},{5,7},{6,4},{7,5},{8,10},{9,11},{10,... | collective-permute-start | bytes 1474568 | tf_op jit(solution)/shard_map/ppermute | solution.py:45
  8.1 3.7 %copy-start.1 = (bf16[1024,64]{0,1:T(8,128)(2,1)S(1)}, bf16[1024,64]{0,1:T(8,128)(2,1)}, u32[]{:S(2)}) copy-start(bf16[1024,64]{0,1:T(8,128)(2,1)} %param.18) | copy-start | bytes 393220
  20.3 3.5 %collective-permute-start.6 = (bf16[320,768]{1,0:T(8,128)(2,1)}, bf16[320,768]{1,0:T(8,128)(2,1)S(1)}, u32[]{:S(2)}, u32[]{:S(2)}) collective-permute-start(bf16[320,768]{1,0:T(8,128)(2,1)} %collective-permute-done.4.refs_2_), channel_id=1, source_target_pairs={{0,1},{1,0},{2,3},{3,2},{4,5},{5,4},{6,7},{7,6},{8,9},{9,8},{10,11... | collective-permute-start | bytes 1474568 | tf_op jit(solution)/shard_map/ppermute | solution.py:45
  21.8 3.1 %collective-permute-start.7 = (bf16[320,768]{1,0:T(8,128)(2,1)}, bf16[320,768]{1,0:T(8,128)(2,1)S(1)}, u32[]{:S(2)}, u32[]{:S(2)}) collective-permute-start(bf16[320,768]{1,0:T(8,128)(2,1)} %collective-permute-done.5.refs_4_), channel_id=1, source_target_pairs={{0,1},{1,0},{2,3},{3,2},{4,5},{5,4},{6,7},{7,6},{8,9},{9,8},{10,11... | collective-permute-start | bytes 1474568 | tf_op jit(solution)/shard_map/ppermute | solution.py:45
  21.8 3.1 %collective-permute-start.3 = (bf16[320,768]{1,0:T(8,128)(2,1)S(1)}, bf16[320,768]{1,0:T(8,128)(2,1)S(1)}, u32[]{:S(2)}, u32[]{:S(2)}) collective-permute-start(bf16[320,768]{1,0:T(8,128)(2,1)S(1)} %collective-permute-done.refs_0_), channel_id=1, source_target_pairs={{0,1},{1,0},{2,3},{3,2},{4,5},{5,4},{6,7},{7,6},{8,9},{9,8},{10,11... | collective-permute-start | bytes 1474568 | tf_op jit(solution)/shard_map/ppermute | solution.py:45
  22.3 13.1 %collective-permute-start.11 = (bf16[320,768]{1,0:T(8,128)(2,1)}, bf16[320,768]{1,0:T(8,128)(2,1)S(1)}, u32[]{:S(2)}, u32[]{:S(2)}) collective-permute-start(bf16[320,768]{1,0:T(8,128)(2,1)} %collective-permute-done.5.refs_4_), channel_id=1, source_target_pairs={{0,12},{1,13},{2,14},{3,15},{4,0},{5,1},{6,2},{7,3},{8,4},{9,5},{1... | collective-permute-start | bytes 1474568 | tf_op jit(solution)/shard_map/ppermute | solution.py:45
  23.5 13.7 %collective-permute-start.9 = (bf16[320,768]{1,0:T(8,128)(2,1)S(1)}, bf16[320,768]{1,0:T(8,128)(2,1)S(1)}, u32[]{:S(2)}, u32[]{:S(2)}) collective-permute-start(bf16[320,768]{1,0:T(8,128)(2,1)S(1)} %collective-permute-done.refs_0_), channel_id=1, source_target_pairs={{0,2},{1,5},{2,0},{3,7},{4,6},{5,9},{6,4},{7,11},{8,10},{9,13},{10... | collective-permute-start | bytes 1474568 | tf_op jit(solution)/shard_map/ppermute | solution.py:45
  23.8 13.6 %collective-permute-start.2 = (bf16[320,768]{1,0:T(8,128)(2,1)S(1)}, bf16[320,768]{1,0:T(8,128)(2,1)S(1)}, u32[]{:S(2)}, u32[]{:S(2)}) collective-permute-start(bf16[320,768]{1,0:T(8,128)(2,1)S(1)} %collective-permute-done.refs_0_), channel_id=1, source_target_pairs={{0,4},{1,3},{2,6},{3,1},{4,8},{5,7},{6,10},{7,5},{8,12},{9,11},{10... | collective-permute-start | bytes 1474568 | tf_op jit(solution)/shard_map/ppermute | solution.py:45
  32.2 15.6 %copy-start.2 = (s32[3,2]{0,1:T(2,128)S(1)}, s32[3,2]{0,1:T(2,128)}, u32[]{:S(2)}) copy-start(s32[3,2]{0,1:T(2,128)} %param.21) | copy-start | bytes 76
  32.2 15.7 %copy-start.3 = (f32[3]{0:T(128)S(1)}, f32[3]{0:T(128)}, u32[]{:S(2)}) copy-start(f32[3]{0:T(128)} %param.22) | copy-start | bytes 40
  35.4 3.0 %collective-permute-start.12 = (bf16[320,768]{1,0:T(8,128)(2,1)S(1)}, bf16[320,768]{1,0:T(8,128)(2,1)S(1)}, u32[]{:S(2)}, u32[]{:S(2)}) collective-permute-start(bf16[320,768]{1,0:T(8,128)(2,1)S(1)} %collective-permute-done.11.refs_2_), channel_id=1, source_target_pairs={{0,1},{1,0},{2,3},{3,2},{4,5},{5,4},{6,7},{7,6},{8,9},{9,8},{10,11... | collective-permute-start | bytes 1474568 | tf_op jit(solution)/shard_map/ppermute | solution.py:45
  37.2 1.9 %collective-permute-start.10 = (bf16[320,768]{1,0:T(8,128)(2,1)S(1)}, bf16[320,768]{1,0:T(8,128)(2,1)S(1)}, u32[]{:S(2)}, u32[]{:S(2)}) collective-permute-start(bf16[320,768]{1,0:T(8,128)(2,1)S(1)} %collective-permute-done.9.refs_4_), channel_id=1, source_target_pairs={{0,1},{1,0},{2,3},{3,2},{4,5},{5,4},{6,7},{7,6},{8,9},{9,8},{10,11... | collective-permute-start | bytes 1474568 | tf_op jit(solution)/shard_map/ppermute | solution.py:45
  37.4 2.4 %collective-permute-start.13 = (bf16[320,768]{1,0:T(8,128)(2,1)S(1)}, bf16[320,768]{1,0:T(8,128)(2,1)S(1)}, u32[]{:S(2)}, u32[]{:S(2)}) collective-permute-start(bf16[320,768]{1,0:T(8,128)(2,1)S(1)} %collective-permute-done.2.refs_0_), channel_id=1, source_target_pairs={{0,1},{1,0},{2,3},{3,2},{4,5},{5,4},{6,7},{7,6},{8,9},{9,8},{10,11... | collective-permute-start | bytes 1474568 | tf_op jit(solution)/shard_map/ppermute | solution.py:45
  38.4 8.9 %collective-permute-start.8 = (bf16[320,768]{1,0:T(8,128)(2,1)S(1)}, bf16[320,768]{1,0:T(8,128)(2,1)S(1)}, u32[]{:S(2)}, u32[]{:S(2)}) collective-permute-start(bf16[320,768]{1,0:T(8,128)(2,1)S(1)} %collective-permute-done.2.refs_0_), channel_id=1, source_target_pairs={{0,2},{1,5},{2,0},{3,7},{4,6},{5,9},{6,4},{7,11},{8,10},{9,13},{10... | collective-permute-start | bytes 1474568 | tf_op jit(solution)/shard_map/ppermute | solution.py:45
  47.3 2.0 %collective-permute-start.14 = (bf16[320,768]{1,0:T(8,128)(2,1)S(1)}, bf16[320,768]{1,0:T(8,128)(2,1)S(1)}, u32[]{:S(2)}, u32[]{:S(2)}) collective-permute-start(bf16[320,768]{1,0:T(8,128)(2,1)S(1)} %collective-permute-done.8.refs_0_), channel_id=1, source_target_pairs={{0,1},{1,0},{2,3},{3,2},{4,5},{5,4},{6,7},{7,6},{8,9},{9,8},{10,11... | collective-permute-start | bytes 1474568 | tf_op jit(solution)/shard_map/ppermute | solution.py:45
  55.0 12.4 %all-to-all-start = ((bf16[16,96,128]{2,1,0:T(8,128)(2,1)}), bf16[16,96,128]{2,1,0:T(8,128)(2,1)S(1)}, u32[]{:S(2)}, u32[]{:S(2)}) async-start(bf16[16,96,128]{2,1,0:T(8,128)(2,1)} %last_stage.1), calls=%async_computation | async-start | bytes 786432 | tf_op jit(solution)/shard_map/all_to_all | solution.py:429
  68.1 19.7 %all-to-all-start.1 = ((bf16[16,32,128]{2,1,0:T(8,128)(2,1)}), bf16[16,32,128]{2,1,0:T(8,128)(2,1)S(1)}, u32[]{:S(2)}, u32[]{:S(2)}) async-start(bf16[16,32,128]{2,1,0:T(8,128)(2,1)} %broadcast_in_dim.10), calls=%async_computation.1 | async-start | bytes 262144 | tf_op jit(solution)/shard_map/all_to_all | solution.py:433
  88.2 3.0 %collective-permute-start.15 = (f32[17,2]{0,1:T(2,128)S(1)}, f32[17,2]{0,1:T(2,128)S(1)}, u32[]{:S(2)}, u32[]{:S(2)}) collective-permute-start(f32[17,2]{0,1:T(2,128)S(1)} %pad_maximum_fusion), channel_id=1, source_target_pairs={{0,1},{1,0},{2,3},{3,2},{4,5},{5,4},{6,7},{7,6},{8,9},{9,8},{10,11... | collective-permute-start | bytes 416 | tf_op jit(solution)/shard_map/ppermute | solution.py:45

commit v7 on v6

--- a/solution.py
+++ b/solution.py
@@ -411,9 +411,8 @@
 
     near = (send(own, X_UP), send(own, X_DOWN), send(own, Y_SWAP))
     sums = middle_stage(core[None], chips, 0, with_twins([own]), w_down, gates, *bases)
-    left_own, first_sums = lax.optimization_barrier((near[0], sums))
-    right_own, across, sums = lax.optimization_barrier((*near[1:], first_sums))
-    near = (left_own, right_own, across)
+    near = [lax.optimization_barrier((piece, sums))[0] for piece in near]
+    left_own, right_own, across = near
     straight, right_across, bent = send(left_own, X_OR_Y), send(across, X_DOWN), send(left_own, Y_OR_X)
     sums = middle_stage(core[None], chips, 1, with_twins(near), w_down, gates, *bases, before=sums)
     far = [lax.optimization_barrier((piece, sums))[0] for piece in (straight, right_across, bent)]

time: 92.4 us -> 92.5 us (level)
  waiting for transfers between devices: 30.8 us -> 29.2 us
  starting transfers between devices: 27.6 us -> 29.2 us
    ppermute x16, waiting for transfers between devices: 12.8 us -> 11.3 us  [send(): return lax.ppermute(value, 'tensor', pairs)]
  transfers between devices with their start and end apart: 18 -> 18, of which waited for: 11 -> 10; matrix products, arithmetic and copies ran while one was open for 2% -> 2% of each run, Pallas kernels for 24% -> 24%
where the time goes in v7:
time: 92.5 us; the launch traced here: 92.1 us
  Pallas kernels  29.5 us (32%)
  starting transfers between devices  29.2 us (32%)
  waiting for transfers between devices  29.2 us (32%)
  local copies, waits for them, and re-layouts  1.95 us (2%)
  other arithmetic  1.46 us (2%)
    pallas_call x3, Pallas kernels, middle_stage(): pl.pallas_call(body, in_specs=in_specs, out_specs=VMEM, out_shape=jax.Sha...  18.7 us
    ppermute x16, starting transfers between devices, send(): return lax.ppermute(value, 'tensor', pairs)  14.8 us
    ppermute x16, waiting for transfers between devices, send(): return lax.ppermute(value, 'tensor', pairs)  11.3 us
    all_to_all x1, starting transfers between devices, shards(): lax.all_to_all(jnp.broadcast_to(query_rows.astype(BF16), (dp_size, half_r...  10.6 us
    all_to_all x1, waiting for transfers between devices, shards(): lax.all_to_all(jnp.broadcast_to(query_rows.astype(BF16), (dp_size, half_r...  9.47 us
    all_to_all x1, waiting for transfers between devices, shards(): grad_parts = lax.all_to_all(grads, 'tensor', 0, 0, tiled=True)  8.49 us
    pallas_call x1, Pallas kernels, last_stage(): pl.pallas_call(body, in_specs=[SMEM] * 4 + [ANY] * len(pieces) + [VMEM, A...  5.72 us
    all_to_all x1, starting transfers between devices, shards(): grad_parts = lax.all_to_all(grads, 'tensor', 0, 0, tiled=True)  3.72 us
  transfers between devices with their start and end apart: 18, of which 10 were waited for; matrix products, arithmetic and copies ran while one was open for 2% of the time, Pallas kernels for 24%

profile of v7, /device:TPU:1, one launch (start us, length us, event | category | flops | bytes accessed | tf_op | source)
XLA Modules:
  0.0 92.1 jit_solution(15161301737104974317)
XLA Ops:
  0.7 1.4 %first.1.refs_0_ = bf16[320,768]{1,0:T(8,128)(2,1)S(1)} custom-call(s32[1]{0:T(128)} %bitcast.9.place_ref, bf16[768,256]{1,0:T(8,128)(2,1)} %bitcast.41, bf16[768,256]{1,0:T(8,128)(2,1)} %bitcast.42, bf16[64,4096]{1,0:T(8,128)(2,1)} %bitcast.40), custom_call_target="tpu_custom_call" | custom-call | tf_op jit(solution)/shard_map/first/pallas_call | solution.py:75
  2.1 3.3 %collective-permute-start.1 = (bf16[320,768]{1,0:T(8,128)(2,1)S(1)}, bf16[320,768]{1,0:T(8,128)(2,1)S(1)}, u32[]{:S(2)}, u32[]{:S(2)}) collective-permute-start(bf16[320,768]{1,0:T(8,128)(2,1)S(1)} %first.1.refs_0_), channel_id=1, source_target_pairs={{0,1},{1,0},{2,3},{3,2},{4,5},{5,4},{6,7},{7,6},{8,9},{9,8},{10,11... | collective-permute-start | bytes 1474568 | tf_op jit(solution)/shard_map/ppermute | solution.py:45
  5.4 0.8 collective-permute-start.4
  6.1 1.3 %collective-permute-start.6 = (bf16[320,768]{1,0:T(8,128)(2,1)S(1)}, bf16[320,768]{1,0:T(8,128)(2,1)}, u32[]{:S(2)}, u32[]{:S(2)}) collective-permute-start(bf16[320,768]{1,0:T(8,128)(2,1)S(1)} %first.1.refs_0_), channel_id=1, source_target_pairs={{0,2},{1,3},{2,0},{3,1},{4,6},{5,7},{6,4},{7,5},{8,10},{9,11},{10,... | collective-permute-start | bytes 1474568 | tf_op jit(solution)/shard_map/ppermute | solution.py:45
  7.4 3.6 %prepare.1 = (bf16[1024,768]{1,0:T(8,128)(2,1)S(1)}, f32[64,768]{1,0:T(8,128)}) custom-call(bf16[768,1024]{1,0:T(8,128)(2,1)} %bitcast.38, bf16[768,1024]{1,0:T(8,128)(2,1)} %bitcast.39, bf16[64,1024]{1,0:T(8,128)(2,1)} %bitcast.45), custom_call_target="tpu_custom_call" | custom-call | tf_op jit(solution)/shard_map/prepare/pallas_call | solution.py:105
  11.2 4.1 %middle_stage.3.refs_10_ = f32[192,768]{1,0:T(8,128)S(1)} custom-call(s32[1]{0:T(128)} %bitcast.core_ref, s32[8]{0:T(128)S(1)} %stack.35.chips_ref, bf16[320,768]{1,0:T(8,128)(2,1)S(1)} %first.1.refs_0_, bf16[320,768]{1,0:T(8,128)(2,1)S(1)} %collective-permute-done.1.refs_1_, bf16[1024,4096]{1,0:T(8,128)(2,1)} %refs_3_.1, bf16[64,4096]{1,0:T(8,128)(2,1)} %bitcast.34, ...), custom_call_target="tpu_custom_call" | custom-call | flops 1006632960 | bytes 1835008 | tf_op jit(solution)/shard_map/middle_stage/pallas_call | solution.py:271
  15.3 3.0 %collective-permute-done.4.refs_2_ = bf16[320,768]{1,0:T(8,128)(2,1)} collective-permute-done((bf16[320,768]{1,0:T(8,128)(2,1)S(1)}, bf16[320,768]{1,0:T(8,128)(2,1)}, u32[]{:S(2)}, u32[]{:S(2)}) %collective-permute-start.4) | collective-permute-done | bytes 491552 | tf_op jit(solution)/shard_map/ppermute | solution.py:45
  18.3 0.9 collective-permute-start.5
  19.1 0.7 collective-permute-start.7
  19.9 0.9 collective-permute-done.refs_0_
  20.8 1.5 %collective-permute-start.3 = (bf16[320,768]{1,0:T(8,128)(2,1)S(1)}, bf16[320,768]{1,0:T(8,128)(2,1)S(1)}, u32[]{:S(2)}, u32[]{:S(2)}) collective-permute-start(bf16[320,768]{1,0:T(8,128)(2,1)S(1)} %collective-permute-done.refs_0_), channel_id=1, source_target_pairs={{0,1},{1,0},{2,3},{3,2},{4,5},{5,4},{6,7},{7,6},{8,9},{9,8},{10,11... | collective-permute-start | bytes 1474568 | tf_op jit(solution)/shard_map/ppermute | solution.py:45
  22.3 1.5 %collective-permute-start.9 = (bf16[320,768]{1,0:T(8,128)(2,1)S(1)}, bf16[320,768]{1,0:T(8,128)(2,1)S(1)}, u32[]{:S(2)}, u32[]{:S(2)}) collective-permute-start(bf16[320,768]{1,0:T(8,128)(2,1)S(1)} %collective-permute-done.refs_0_), channel_id=1, source_target_pairs={{0,2},{1,5},{2,0},{3,7},{4,6},{5,9},{6,4},{7,11},{8,10},{9,13},{10... | collective-permute-start | bytes 1474568 | tf_op jit(solution)/shard_map/ppermute | solution.py:45
  23.9 7.2 %middle_stage.4.refs_10_ = f32[192,768]{1,0:T(8,128)S(1)} custom-call(s32[1]{0:T(128)} %bitcast.core_ref, s32[8]{0:T(128)S(1)} %stack.35.chips_ref, bf16[320,768]{1,0:T(8,128)(2,1)S(1)} %collective-permute-done.refs_0_, bf16[320,768]{1,0:T(8,128)(2,1)S(1)} %collective-permute-done.3.refs_1_, bf16[320,768]{1,0:T(8,128)(2,1)} %collective-permute-done.4.refs_2_, ...), custom_call_target="tpu_custom_call" | custom-call | flops 2617245696 | bytes 5505024 | tf_op jit(solution)/shard_map/middle_stage/pallas_call | solution.py:271
  31.2 4.2 %collective-permute-done.11.refs_2_ = bf16[320,768]{1,0:T(8,128)(2,1)S(1)} collective-permute-done((bf16[320,768]{1,0:T(8,128)(2,1)}, bf16[320,768]{1,0:T(8,128)(2,1)S(1)}, u32[]{:S(2)}, u32[]{:S(2)}) %collective-permute-start.11) | collective-permute-done | bytes 491552 | tf_op jit(solution)/shard_map/ppermute | solution.py:45
  35.4 0.8 collective-permute-start.12
  36.2 1.0 %collective-permute-start.13 = (bf16[320,768]{1,0:T(8,128)(2,1)S(1)}, bf16[320,768]{1,0:T(8,128)(2,1)S(1)}, u32[]{:S(2)}, u32[]{:S(2)}) collective-permute-start(bf16[320,768]{1,0:T(8,128)(2,1)S(1)} %collective-permute-done.2.refs_0_), channel_id=1, source_target_pairs={{0,1},{1,0},{2,3},{3,2},{4,5},{5,4},{6,7},{7,6},{8,9},{9,8},{10,11... | collective-permute-start | bytes 1474568 | tf_op jit(solution)/shard_map/ppermute | solution.py:45
  39.0 7.4 %middle_stage.5.refs_2_ = f32[192,768]{1,0:T(8,128)S(1)} custom-call(s32[1]{0:T(128)} %bitcast.core_ref, s32[8]{0:T(128)S(1)} %stack.35.chips_ref, bf16[320,768]{1,0:T(8,128)(2,1)S(1)} %collective-permute-done.2.refs_0_, bf16[320,768]{1,0:T(8,128)(2,1)S(1)} %collective-permute-done.10.refs_1_, bf16[320,768]{1,0:T(8,128)(2,1)S(1)} %collective-permute-done.11.refs_2_, ...), custom_call_target="tpu_custom_call" | custom-call | flops 2617245696 | bytes 5505024 | tf_op jit(solution)/shard_map/middle_stage/pallas_call | solution.py:271
  47.0 1.4 %collective-permute-done.14.refs_1_ = bf16[320,768]{1,0:T(8,128)(2,1)S(1)} collective-permute-done((bf16[320,768]{1,0:T(8,128)(2,1)S(1)}, bf16[320,768]{1,0:T(8,128)(2,1)S(1)}, u32[]{:S(2)}, u32[]{:S(2)}) %collective-permute-start.14) | collective-permute-done | bytes 491552 | tf_op jit(solution)/shard_map/ppermute | solution.py:45
  48.4 5.7 %last_stage.1 = bf16[16,96,128]{2,1,0:T(8,128)(2,1)} custom-call(s32[1]{0:T(128)} %bitcast.core_ref, s32[8]{0:T(128)S(1)} %stack.35.chips_ref, s32[3,2]{1,0:T(4,128)S(1)} %copy.29.lengths_ref, f32[3]{0:T(128)S(1)} %add_divide_fusion.pair_ref, bf16[320,768]{1,0:T(8,128)(2,1)S(1)} %collective-permute-done.8.refs_0_, ...), custom_call_target="tpu_custom_call" | custom-call | flops 1006632960 | bytes 1835008 | tf_op jit(solution)/shard_map/last_stage/pallas_call | solution.py:342
  54.1 3.7 %all-to-all-start = ((bf16[16,96,128]{2,1,0:T(8,128)(2,1)}), bf16[16,96,128]{2,1,0:T(8,128)(2,1)S(1)}, u32[]{:S(2)}, u32[]{:S(2)}) async-start(bf16[16,96,128]{2,1,0:T(8,128)(2,1)} %last_stage.1), calls=%async_computation | async-start | bytes 786432 | tf_op jit(solution)/shard_map/all_to_all | solution.py:428
  58.0 8.5 %all-to-all-done = bf16[16,96,128]{2,1,0:T(8,128)(2,1)S(1)} async-done(((bf16[16,96,128]{2,1,0:T(8,128)(2,1)}), bf16[16,96,128]{2,1,0:T(8,128)(2,1)S(1)}, u32[]{:S(2)}, u32[]{:S(2)}) %all-to-all-start) | async-done | bytes 393248 | tf_op jit(solution)/shard_map/all_to_all | solution.py:428
  67.2 10.6 %all-to-all-start.1 = ((bf16[16,32,128]{2,1,0:T(8,128)(2,1)}), bf16[16,32,128]{2,1,0:T(8,128)(2,1)S(1)}, u32[]{:S(2)}, u32[]{:S(2)}) async-start(bf16[16,32,128]{2,1,0:T(8,128)(2,1)} %broadcast_in_dim.10), calls=%async_computation.1 | async-start | bytes 262144 | tf_op jit(solution)/shard_map/all_to_all | solution.py:432
  78.4 9.5 %all-to-all-done.1 = bf16[16,32,128]{2,1,0:T(8,128)(2,1)S(1)} async-done(((bf16[16,32,128]{2,1,0:T(8,128)(2,1)}), bf16[16,32,128]{2,1,0:T(8,128)(2,1)S(1)}, u32[]{:S(2)}, u32[]{:S(2)}) %all-to-all-start.1) | async-done | bytes 131104 | tf_op jit(solution)/shard_map/all_to_all | solution.py:432
  88.2 2.2 %collective-permute-start.15 = (f32[17,2]{0,1:T(2,128)S(1)}, f32[17,2]{0,1:T(2,128)S(1)}, u32[]{:S(2)}, u32[]{:S(2)}) collective-permute-start(f32[17,2]{0,1:T(2,128)S(1)} %pad_maximum_fusion), channel_id=1, source_target_pairs={{0,1},{1,0},{2,3},{3,2},{4,5},{5,4},{6,7},{7,6},{8,9},{9,8},{10,11... | collective-permute-start | bytes 416 | tf_op jit(solution)/shard_map/ppermute | solution.py:45
  (50 shorter events, 6.2 us)
Async XLA Ops:
  0.6 57.2 %copy-start = (f32[2,64,64]{2,1,0:T(8,128)S(1)}, f32[2,64,64]{2,1,0:T(8,128)}, u32[]{:S(2)}) copy-start(f32[2,64,64]{2,1,0:T(8,128)} %param.23) | copy-start | bytes 98308
  2.1 9.1 %collective-permute-start.1 = (bf16[320,768]{1,0:T(8,128)(2,1)S(1)}, bf16[320,768]{1,0:T(8,128)(2,1)S(1)}, u32[]{:S(2)}, u32[]{:S(2)}) collective-permute-start(bf16[320,768]{1,0:T(8,128)(2,1)S(1)} %first.1.refs_0_), channel_id=1, source_target_pairs={{0,1},{1,0},{2,3},{3,2},{4,5},{5,4},{6,7},{7,6},{8,9},{9,8},{10,11... | collective-permute-start | bytes 1474568 | tf_op jit(solution)/shard_map/ppermute | solution.py:45
  5.4 12.9 %collective-permute-start.4 = (bf16[320,768]{1,0:T(8,128)(2,1)S(1)}, bf16[320,768]{1,0:T(8,128)(2,1)}, u32[]{:S(2)}, u32[]{:S(2)}) collective-permute-start(bf16[320,768]{1,0:T(8,128)(2,1)S(1)} %first.1.refs_0_), channel_id=1, source_target_pairs={{0,12},{1,13},{2,14},{3,15},{4,0},{5,1},{6,2},{7,3},{8,4},{9,5},{1... | collective-permute-start | bytes 1474568 | tf_op jit(solution)/shard_map/ppermute | solution.py:45
  6.1 13.0 %collective-permute-start.6 = (bf16[320,768]{1,0:T(8,128)(2,1)S(1)}, bf16[320,768]{1,0:T(8,128)(2,1)}, u32[]{:S(2)}, u32[]{:S(2)}) collective-permute-start(bf16[320,768]{1,0:T(8,128)(2,1)S(1)} %first.1.refs_0_), channel_id=1, source_target_pairs={{0,2},{1,3},{2,0},{3,1},{4,6},{5,7},{6,4},{7,5},{8,10},{9,11},{10,... | collective-permute-start | bytes 1474568 | tf_op jit(solution)/shard_map/ppermute | solution.py:45
  7.4 13.3 %collective-permute-start = (bf16[320,768]{1,0:T(8,128)(2,1)S(1)}, bf16[320,768]{1,0:T(8,128)(2,1)S(1)}, u32[]{:S(2)}, u32[]{:S(2)}) collective-permute-start(bf16[320,768]{1,0:T(8,128)(2,1)S(1)} %first.1.refs_0_), channel_id=1, source_target_pairs={{0,4},{1,5},{2,6},{3,7},{4,8},{5,9},{6,10},{7,11},{8,12},{9,13},{1... | collective-permute-start | bytes 1474568 | tf_op jit(solution)/shard_map/ppermute | solution.py:45
  7.4 3.7 %copy-start.1 = (bf16[1024,64]{0,1:T(8,128)(2,1)S(1)}, bf16[1024,64]{0,1:T(8,128)(2,1)}, u32[]{:S(2)}) copy-start(bf16[1024,64]{0,1:T(8,128)(2,1)} %param.18) | copy-start | bytes 393220
  18.3 5.5 %collective-permute-start.5 = (bf16[320,768]{1,0:T(8,128)(2,1)}, bf16[320,768]{1,0:T(8,128)(2,1)S(1)}, u32[]{:S(2)}, u32[]{:S(2)}) collective-permute-start(bf16[320,768]{1,0:T(8,128)(2,1)} %collective-permute-done.4.refs_2_), channel_id=1, source_target_pairs={{0,1},{1,0},{2,3},{3,2},{4,5},{5,4},{6,7},{7,6},{8,9},{9,8},{10,11... | collective-permute-start | bytes 1474568 | tf_op jit(solution)/shard_map/ppermute | solution.py:45
  19.1 4.8 %collective-permute-start.7 = (bf16[320,768]{1,0:T(8,128)(2,1)}, bf16[320,768]{1,0:T(8,128)(2,1)S(1)}, u32[]{:S(2)}, u32[]{:S(2)}) collective-permute-start(bf16[320,768]{1,0:T(8,128)(2,1)} %collective-permute-done.6.refs_4_), channel_id=1, source_target_pairs={{0,1},{1,0},{2,3},{3,2},{4,5},{5,4},{6,7},{7,6},{8,9},{9,8},{10,11... | collective-permute-start | bytes 1474568 | tf_op jit(solution)/shard_map/ppermute | solution.py:45
  20.8 3.2 %collective-permute-start.3 = (bf16[320,768]{1,0:T(8,128)(2,1)S(1)}, bf16[320,768]{1,0:T(8,128)(2,1)S(1)}, u32[]{:S(2)}, u32[]{:S(2)}) collective-permute-start(bf16[320,768]{1,0:T(8,128)(2,1)S(1)} %collective-permute-done.refs_0_), channel_id=1, source_target_pairs={{0,1},{1,0},{2,3},{3,2},{4,5},{5,4},{6,7},{7,6},{8,9},{9,8},{10,11... | collective-permute-start | bytes 1474568 | tf_op jit(solution)/shard_map/ppermute | solution.py:45
  22.3 13.1 %collective-permute-start.11 = (bf16[320,768]{1,0:T(8,128)(2,1)}, bf16[320,768]{1,0:T(8,128)(2,1)S(1)}, u32[]{:S(2)}, u32[]{:S(2)}) collective-permute-start(bf16[320,768]{1,0:T(8,128)(2,1)} %collective-permute-done.6.refs_4_), channel_id=1, source_target_pairs={{0,12},{1,13},{2,14},{3,15},{4,0},{5,1},{6,2},{7,3},{8,4},{9,5},{1... | collective-permute-start | bytes 1474568 | tf_op jit(solution)/shard_map/ppermute | solution.py:45
  22.3 13.8 %collective-permute-start.9 = (bf16[320,768]{1,0:T(8,128)(2,1)S(1)}, bf16[320,768]{1,0:T(8,128)(2,1)S(1)}, u32[]{:S(2)}, u32[]{:S(2)}) collective-permute-start(bf16[320,768]{1,0:T(8,128)(2,1)S(1)} %collective-permute-done.refs_0_), channel_id=1, source_target_pairs={{0,2},{1,5},{2,0},{3,7},{4,6},{5,9},{6,4},{7,11},{8,10},{9,13},{10... | collective-permute-start | bytes 1474568 | tf_op jit(solution)/shard_map/ppermute | solution.py:45
  23.8 12.4 %collective-permute-start.2 = (bf16[320,768]{1,0:T(8,128)(2,1)S(1)}, bf16[320,768]{1,0:T(8,128)(2,1)S(1)}, u32[]{:S(2)}, u32[]{:S(2)}) collective-permute-start(bf16[320,768]{1,0:T(8,128)(2,1)S(1)} %collective-permute-done.refs_0_), channel_id=1, source_target_pairs={{0,4},{1,3},{2,6},{3,1},{4,8},{5,7},{6,10},{7,5},{8,12},{9,11},{10... | collective-permute-start | bytes 1474568 | tf_op jit(solution)/shard_map/ppermute | solution.py:45
  31.2 15.7 %copy-start.2 = (s32[3,2]{0,1:T(2,128)S(1)}, s32[3,2]{0,1:T(2,128)}, u32[]{:S(2)}) copy-start(s32[3,2]{0,1:T(2,128)} %param.21) | copy-start | bytes 76
  31.2 15.8 %copy-start.3 = (f32[3]{0:T(128)S(1)}, f32[3]{0:T(128)}, u32[]{:S(2)}) copy-start(f32[3]{0:T(128)} %param.22) | copy-start | bytes 40
  35.4 2.3 %collective-permute-start.12 = (bf16[320,768]{1,0:T(8,128)(2,1)S(1)}, bf16[320,768]{1,0:T(8,128)(2,1)S(1)}, u32[]{:S(2)}, u32[]{:S(2)}) collective-permute-start(bf16[320,768]{1,0:T(8,128)(2,1)S(1)} %collective-permute-done.11.refs_2_), channel_id=1, source_target_pairs={{0,1},{1,0},{2,3},{3,2},{4,5},{5,4},{6,7},{7,6},{8,9},{9,8},{10,11... | collective-permute-start | bytes 1474568 | tf_op jit(solution)/shard_map/ppermute | solution.py:45
  36.1 2.2 %collective-permute-start.10 = (bf16[320,768]{1,0:T(8,128)(2,1)S(1)}, bf16[320,768]{1,0:T(8,128)(2,1)S(1)}, u32[]{:S(2)}, u32[]{:S(2)}) collective-permute-start(bf16[320,768]{1,0:T(8,128)(2,1)S(1)} %collective-permute-done.9.refs_4_), channel_id=1, source_target_pairs={{0,1},{1,0},{2,3},{3,2},{4,5},{5,4},{6,7},{7,6},{8,9},{9,8},{10,11... | collective-permute-start | bytes 1474568 | tf_op jit(solution)/shard_map/ppermute | solution.py:45
  36.2 2.9 %collective-permute-start.13 = (bf16[320,768]{1,0:T(8,128)(2,1)S(1)}, bf16[320,768]{1,0:T(8,128)(2,1)S(1)}, u32[]{:S(2)}, u32[]{:S(2)}) collective-permute-start(bf16[320,768]{1,0:T(8,128)(2,1)S(1)} %collective-permute-done.2.refs_0_), channel_id=1, source_target_pairs={{0,1},{1,0},{2,3},{3,2},{4,5},{5,4},{6,7},{7,6},{8,9},{9,8},{10,11... | collective-permute-start | bytes 1474568 | tf_op jit(solution)/shard_map/ppermute | solution.py:45
  37.1 9.3 %collective-permute-start.8 = (bf16[320,768]{1,0:T(8,128)(2,1)S(1)}, bf16[320,768]{1,0:T(8,128)(2,1)S(1)}, u32[]{:S(2)}, u32[]{:S(2)}) collective-permute-start(bf16[320,768]{1,0:T(8,128)(2,1)S(1)} %collective-permute-done.2.refs_0_), channel_id=1, source_target_pairs={{0,2},{1,5},{2,0},{3,7},{4,6},{5,9},{6,4},{7,11},{8,10},{9,13},{10... | collective-permute-start | bytes 1474568 | tf_op jit(solution)/shard_map/ppermute | solution.py:45
  46.5 2.0 %collective-permute-start.14 = (bf16[320,768]{1,0:T(8,128)(2,1)S(1)}, bf16[320,768]{1,0:T(8,128)(2,1)S(1)}, u32[]{:S(2)}, u32[]{:S(2)}) collective-permute-start(bf16[320,768]{1,0:T(8,128)(2,1)S(1)} %collective-permute-done.8.refs_0_), channel_id=1, source_target_pairs={{0,1},{1,0},{2,3},{3,2},{4,5},{5,4},{6,7},{7,6},{8,9},{9,8},{10,11... | collective-permute-start | bytes 1474568 | tf_op jit(solution)/shard_map/ppermute | solution.py:45
  54.1 12.4 %all-to-all-start = ((bf16[16,96,128]{2,1,0:T(8,128)(2,1)}), bf16[16,96,128]{2,1,0:T(8,128)(2,1)S(1)}, u32[]{:S(2)}, u32[]{:S(2)}) async-start(bf16[16,96,128]{2,1,0:T(8,128)(2,1)} %last_stage.1), calls=%async_computation | async-start | bytes 786432 | tf_op jit(solution)/shard_map/all_to_all | solution.py:428
  67.2 20.6 %all-to-all-start.1 = ((bf16[16,32,128]{2,1,0:T(8,128)(2,1)}), bf16[16,32,128]{2,1,0:T(8,128)(2,1)S(1)}, u32[]{:S(2)}, u32[]{:S(2)}) async-start(bf16[16,32,128]{2,1,0:T(8,128)(2,1)} %broadcast_in_dim.10), calls=%async_computation.1 | async-start | bytes 262144 | tf_op jit(solution)/shard_map/all_to_all | solution.py:432
  88.2 3.0 %collective-permute-start.15 = (f32[17,2]{0,1:T(2,128)S(1)}, f32[17,2]{0,1:T(2,128)S(1)}, u32[]{:S(2)}, u32[]{:S(2)}) collective-permute-start(f32[17,2]{0,1:T(2,128)S(1)} %pad_maximum_fusion), channel_id=1, source_target_pairs={{0,1},{1,0},{2,3},{3,2},{4,5},{5,4},{6,7},{7,6},{8,9},{9,8},{10,11... | collective-permute-start | bytes 416 | tf_op jit(solution)/shard_map/ppermute | solution.py:45
